TPU v7x, 256 devices: a whole 4x4x8 slice. The times are simulated.
256 devices in a mesh: enc: 8 (over z), rep: 4 (over x), seq: 8 (over y, core).
Axes of the slice: x: 4, y: 4, z: 8, core: 2. Of those that a mesh axis runs over, the one named last changes fastest.
Arguments:
- queries: bfloat16 [65536, 3072], P(('rep', 'seq'), 'enc'), may hold values from -6 to 6
- text: bfloat16 [16, 512, 5120], P('rep', ('enc', 'seq')), may hold values from -6 to 6
- kv_weight: bfloat16 [5120, 2, 3072], P(None, None, 'enc'), may hold values from -0.078125 to 0.078125
- query_gain: float32 [3072], P('enc'), may hold values from 1 to 2.6
- key_gain: float32 [3072], P('enc'), may hold values from 1 to 2.6
- prompt_len: int32 [16], replicated, may hold values from 1 to 512, 4096 in all
- served: int32 [16], replicated, may hold values from 0 to 15, each once
- frame_slot: int32 [4, 128], P('rep', 'seq'), may hold values from 0 to 3, never falling along the last dimension, each value on 1 to 64 neighbouring positions
Outputs:
- attended: bfloat16 [65536, 3072], P(('rep', 'seq'), 'enc')
Inputs may be any that keep to these rules, and one draw needn't show every extreme that they name: `prompt_len`: the largest length is exactly 512. `served`: each tenant appears exactly once. `frame_slot`: along each replica's row the value never falls; every one of the 4 positions holds 1 to 64 frame blocks.
All inputs are finite; a program needn't handle non-finite values.
Results may differ from a plain program's by a relative error of at most 0.0099.
Values may be sent and summed in bfloat16 or wider, within the bound.
No kernel may reach another device: no remote copies, remote signals or barrier semaphores. Data moves between devices by JAX's collectives and lax.ppermute only.
A program may use at most 128 MiB of HBM per device.

v0:
```python
import math

import jax
import jax.numpy as jnp
from jax import lax
from jax.sharding import PartitionSpec as P

HD = 128
FRAME = 128


def local(queries, text, kv_weight, query_gain, key_gain, prompt_len, served, frame_slot):
    tenants_here, rows_block, text_width = text.shape
    columns = kv_weight.shape[2]
    enc_size = lax.axis_size("enc")
    rep_size = lax.axis_size("rep")
    seq_size = lax.axis_size("seq")
    full_width = columns * enc_size
    flat_weight = kv_weight.reshape(text_width, 2 * columns)
    rep_now = lax.axis_index("rep")
    my_tenants = lax.dynamic_slice_in_dim(served, rep_now * tenants_here, tenants_here)
    home_rep = my_tenants // tenants_here
    home_slot = my_tenants % tenants_here
    block_rows = lax.all_gather(text, "enc", axis=1, tiled=True)
    mixed = jnp.einsum("trd,dc->trc", block_rows, flat_weight, preferred_element_type=jnp.float32)
    projected = mixed.reshape(block_rows.shape[0], block_rows.shape[1], 2, columns)
    local_rows = projected.shape[1]
    raw_keys = projected[:, :, 0]
    key_square = jnp.sum(raw_keys * raw_keys, axis=-1)
    query_float = queries.astype(jnp.float32)
    query_square = jnp.sum(query_float * query_float, axis=-1)
    query_total, key_total = lax.psum((query_square, key_square), "enc")
    key_scale = lax.rsqrt(key_total / full_width + 1e-06)
    keys_part = (raw_keys * key_scale[:, :, None] * key_gain).astype(jnp.bfloat16)
    values_part = projected[:, :, 1].astype(jnp.bfloat16)
    local_pairs = jnp.stack([keys_part, values_part], axis=2)
    query_scale = lax.rsqrt(query_total / full_width + 1e-06)
    everything = lax.all_gather(local_pairs, ("rep", "seq"), axis=0, tiled=True)
    everything = everything.reshape(rep_size, seq_size, tenants_here, local_rows, 2, columns)
    picked = everything[home_rep, :, home_slot]
    picked = picked.reshape(tenants_here, seq_size * local_rows, 2, columns)
    seq_ids = jnp.arange(seq_size, dtype=jnp.int32)[:, None, None]
    enc_ids = jnp.arange(enc_size, dtype=jnp.int32)[None, :, None]
    within = jnp.arange(rows_block, dtype=jnp.int32)[None, None, :]
    positions = ((enc_ids * seq_size + seq_ids) * rows_block + within).reshape(-1)
    key_count = picked.shape[1]
    lengths = prompt_len[my_tenants]
    frames_dev = queries.shape[0] // FRAME
    per_step = math.gcd(frames_dev, max(1, 512 // FRAME))
    heads_here = columns // HD
    frame_slots = frame_slot.reshape(-1)
    query_blocks = queries.reshape(frames_dev // per_step, per_step * FRAME, columns)
    scale_blocks = query_scale.reshape(frames_dev // per_step, per_step * FRAME)
    slot_blocks = frame_slots.reshape(frames_dev // per_step, per_step)

    def attend(block_items):
        query_rows, row_scale, slot_ids = block_items
        scaled = (
            query_rows.astype(jnp.float32) * row_scale[:, None] * query_gain * HD ** (-0.5)
        ).astype(jnp.bfloat16)
        scaled = scaled.reshape(per_step, FRAME, heads_here, HD)
        chosen = picked[slot_ids]
        keys_block = chosen[:, :, 0].reshape(per_step, key_count, heads_here, HD)
        values_block = chosen[:, :, 1].reshape(per_step, key_count, heads_here, HD)
        scores = jnp.einsum(
            "gqhd,gkhd->ghqk", scaled, keys_block, preferred_element_type=jnp.float32
        )
        live = positions[None, :] < lengths[slot_ids][:, None]
        raised = jnp.where(live[:, None, None, :], jnp.exp(scores), jnp.zeros_like(scores))
        probs = (raised / jnp.sum(raised, axis=-1, keepdims=True)).astype(jnp.bfloat16)
        mixed = jnp.einsum(
            "ghqk,gkhd->gqhd", probs, values_block, preferred_element_type=jnp.float32
        )
        return mixed.astype(jnp.bfloat16).reshape(per_step * FRAME, columns)

    result = lax.map(attend, (query_blocks, scale_blocks, slot_blocks))
    return result.reshape(queries.shape[0], columns)


def solution(mesh):
    placed = (
        P(("rep", "seq"), "enc"),
        P("rep", ("enc", "seq"), None),
        P(None, None, "enc"),
        P("enc"),
        P("enc"),
        P(),
        P(),
        P("rep", "seq"),
    )
    return jax.shard_map(
        local, mesh=mesh, in_specs=placed, out_specs=P(("rep", "seq"), "enc"), check_vma=False
    )
```

profile of v0, /device:TPU:1, one launch (start us, length us, event | category | flops | bytes accessed | tf_op | source)
XLA Modules:
  0.0 258.4 jit_solution(9246806252824550482)
XLA Ops:
  6.5 0.7 all-gather.3.cloned.1.call-update
  7.3 7.7 %copy.44 = bf16[640,8,2,384]{3,1,2,0:T(8,128)(2,1)} copy(bf16[640,8,2,384]{3,2,1,0:T(2,128)(2,1)} %bitcast.58) | data formatting | bytes 15728640
  15.0 10.8 %copy.33 = bf16[768,5120]{1,0:T(8,128)(2,1)} copy(bf16[768,5120]{0,1:T(8,128)(2,1)} %bitcast.56) | data formatting | bytes 15728640 | tf_op jit(solution)/shard_map/trd,dc->trc/dot_general | solution.py:25
  26.3 26.4 %all-gather.3.cloned.1.call-done = bf16[4,64,5120]{2,1,0:T(8,128)(2,1)} async-done(((bf16[4,8,5120]{2,1,0:T(8,128)(2,1)}), bf16[4,64,5120]{2,1,0:T(8,128)(2,1)}) %all-gather.3.cloned.1.call-update) | async-done | bytes 2621456 | tf_op jit(solution)/shard_map/all_gather | solution.py:24
  52.7 6.1 %fusion.12 = f32[4,64,2,384]{3,1,2,0:T(8,128)S(1)} fusion(bf16[2,384,5120,1]{2,1,0,3:T(8,128)(2,1)} %bitcast.59, bf16[4,64,5120]{2,1,0:T(8,128)(2,1)} %all-gather.3.cloned.1.call-done), kind=kOutput, calls=%fused_computation.27 | convolution fusion | flops 2013265920 | bytes 11272192 | tf_op jit(solution)/shard_map/trd,dc->trc/dot_general | solution.py:25
  58.9 21.3 %all-reduce = (f32[4,64]{1,0:T(4,128)S(1)}, f32[2048]{0:T(1024)S(1)}) all-reduce(f32[4,64]{1,0:T(4,128)S(1)} %multiply_reduce_fusion.1, f32[2048]{0:T(1024)S(1)} %multiply_reduce_fusion), channel_id=1, replica_groups=mesh['enc'=8,'rep'=4,'seq'=8] {'enc'}, use_global_device_ids=true, to_apply=%region_3.4 | all-reduce | flops 2304 | bytes 18432 | tf_op jit(solution)/shard_map/psum | solution.py:32
  80.4 0.8 pad_maximum_fusion
  82.4 0.7 reshape_reshape.3
  85.1 73.8 %all-gather.5.cloned.1.call-done = bf16[128,64,2,384]{3,1,2,0:T(8,128)(2,1)} async-done(((bf16[4,64,2,384]{3,1,2,0:T(8,128)(2,1)}), bf16[128,64,2,384]{3,1,2,0:T(8,128)(2,1)}) %all-gather.5.cloned.1.call-update) | async-done | bytes 12582928 | tf_op jit(solution)/shard_map/all_gather | solution.py:38
  158.8 5.8 %gather_fusion.2 = bf16[4,8,64,2,384]{4,2,3,1,0:T(8,128)(2,1)S(1)} fusion(bf16[4,8,4,64,2,384]{5,3,4,2,1,0:T(8,128)(2,1)} %bitcast.60, s32[4]{0:T(128)S(1)} %get-tuple-element.117), kind=kCustom, calls=%fused_computation.2 | custom fusion | bytes 6291488 | tf_op jit(solution)/shard_map/gather | solution.py:40
  164.7 2.0 copy.34
  166.7 84.9 %while.11 = (s32[]{:T(128)}, bf16[4,512,384]{2,1,0:T(8,128)(2,1)}, s32[4,4]{1,0:T(4,128)}, bf16[4,512,2,384]{3,1,2,0:T(8,128)(2,1)}, s32[4]{0:T(128)S(1)}, /*ind...) while((s32[]{:T(128)}, bf16[4,512,384]{2,1,0:T(8,128)(2,1)}, ...), condition=%wide.region_6.7_spmd.clone, body=%wide.region_4.6_spmd.clone.sunk | while | flops 407570432 | bytes 41720332 | solution.py:76
  166.7 1.0 constant_dynamic-slice_fusion.5
  168.2 0.7 constant_dynamic-slice_fusion.6
  168.9 1.2 multiply_convert_fusion.3
  170.0 0.7 fusion.31
  171.4 0.8 iota_add_fusion.2
  172.2 0.7 broadcast_compare_fusion.2
  172.9 3.1 %gather_fusion = bf16[4,512,2,384]{3,1,2,0:T(8,128)(2,1)S(1)} fusion(bf16[4,512,2,384]{3,1,2,0:T(8,128)(2,1)} %get-tuple-element.204, s32[1024]{0:T(1024)S(1)} %pad_clamp_fusion.3), kind=kCustom, calls=%fused_computation.clone.clone.1 | custom fusion | bytes 6291472 | tf_op jit(solution)/shard_map/while/body/eval_jaxpr/gather | solution.py:62
  176.0 2.0 fusion.32
  178.0 1.7 copy.56
  179.7 3.2 %fusion.33 = (f32[4,3,128]{2,1,0:T(4,128)S(1)}, f32[4,3,128,512]{3,2,1,0:T(8,128)}) fusion(pred[4,512]{1,0:T(4,128)(4,1)} %broadcast_compare_fusion.2, bf16[4,512,3,128]{1,3,2,0:T(8,128)(2,1)S(1)} %bitcast.53, bf16[4,128,3,128]{1,0,3,2:T(4,128)(2,1)S(1)} %multiply_convert_fusion.3), kind=kOutput, calls=%fused_computation.7.clone.1 | convolution fusion | flops 202897920 | bytes 5120000 | tf_op jit(solution)/shard_map/while/body/eval_jaxpr/gqhd,gkhd->ghqk/dot_general | solution.py:65
  182.9 0.8 copy.55
  183.7 2.8 %fusion.34 = bf16[4,128,3,128]{1,3,2,0:T(8,128)(2,1)S(1)} fusion(bf16[4,512,3,128]{1,3,2,0:T(8,128)(2,1)S(1)} %bitcast.55, f32[4,3,128,512]{3,2,1,0:T(8,128)} %get-tuple-element.179, f32[4,3,128]{2,1,0:T(4,128)S(1)} %get-tuple-element.180, pred[4,512]{1,0:T(4,128)(4,1)} %broadcast_compare_fusion.2), kind=kOutput, calls=%fused_computation.11.clone.1 | convolution fusion | flops 203882496 | bytes 5120000 | tf_op jit(solution)/shard_map/while/body/eval_jaxpr/ghqk,gkhd->gqhd/dot_general | solution.py:71
  187.1 0.8 constant_dynamic-update-slice_fusion.2
  187.9 1.0 constant_dynamic-slice_fusion.5
  189.4 0.7 constant_dynamic-slice_fusion.6
  190.1 1.2 multiply_convert_fusion.3
  191.3 0.7 fusion.31
  192.6 0.8 iota_add_fusion.2
  193.4 0.7 broadcast_compare_fusion.2
  194.1 3.1 %gather_fusion = bf16[4,512,2,384]{3,1,2,0:T(8,128)(2,1)S(1)} fusion(bf16[4,512,2,384]{3,1,2,0:T(8,128)(2,1)} %get-tuple-element.204, s32[1024]{0:T(1024)S(1)} %pad_clamp_fusion.3), kind=kCustom, calls=%fused_computation.clone.clone.1 | custom fusion | bytes 6291472 | tf_op jit(solution)/shard_map/while/body/eval_jaxpr/gather | solution.py:62
  197.2 2.0 fusion.32
  199.2 1.7 copy.56
  201.0 3.2 %fusion.33 = (f32[4,3,128]{2,1,0:T(4,128)S(1)}, f32[4,3,128,512]{3,2,1,0:T(8,128)}) fusion(pred[4,512]{1,0:T(4,128)(4,1)} %broadcast_compare_fusion.2, bf16[4,512,3,128]{1,3,2,0:T(8,128)(2,1)S(1)} %bitcast.53, bf16[4,128,3,128]{1,0,3,2:T(4,128)(2,1)S(1)} %multiply_convert_fusion.3), kind=kOutput, calls=%fused_computation.7.clone.1 | convolution fusion | flops 202897920 | bytes 5120000 | tf_op jit(solution)/shard_map/while/body/eval_jaxpr/gqhd,gkhd->ghqk/dot_general | solution.py:65
  204.1 0.8 copy.55
  204.9 2.8 %fusion.34 = bf16[4,128,3,128]{1,3,2,0:T(8,128)(2,1)S(1)} fusion(bf16[4,512,3,128]{1,3,2,0:T(8,128)(2,1)S(1)} %bitcast.55, f32[4,3,128,512]{3,2,1,0:T(8,128)} %get-tuple-element.179, f32[4,3,128]{2,1,0:T(4,128)S(1)} %get-tuple-element.180, pred[4,512]{1,0:T(4,128)(4,1)} %broadcast_compare_fusion.2), kind=kOutput, calls=%fused_computation.11.clone.1 | convolution fusion | flops 203882496 | bytes 5120000 | tf_op jit(solution)/shard_map/while/body/eval_jaxpr/ghqk,gkhd->gqhd/dot_general | solution.py:71
  208.3 0.8 constant_dynamic-update-slice_fusion.2
  209.1 1.0 constant_dynamic-slice_fusion.5
  210.6 0.7 constant_dynamic-slice_fusion.6
  211.3 1.2 multiply_convert_fusion.3
  212.5 0.7 fusion.31
  213.8 0.8 iota_add_fusion.2
  214.7 0.7 broadcast_compare_fusion.2
  215.3 3.1 %gather_fusion = bf16[4,512,2,384]{3,1,2,0:T(8,128)(2,1)S(1)} fusion(bf16[4,512,2,384]{3,1,2,0:T(8,128)(2,1)} %get-tuple-element.204, s32[1024]{0:T(1024)S(1)} %pad_clamp_fusion.3), kind=kCustom, calls=%fused_computation.clone.clone.1 | custom fusion | bytes 6291472 | tf_op jit(solution)/shard_map/while/body/eval_jaxpr/gather | solution.py:62
  218.5 2.0 fusion.32
  220.4 1.7 copy.56
  222.2 3.2 %fusion.33 = (f32[4,3,128]{2,1,0:T(4,128)S(1)}, f32[4,3,128,512]{3,2,1,0:T(8,128)}) fusion(pred[4,512]{1,0:T(4,128)(4,1)} %broadcast_compare_fusion.2, bf16[4,512,3,128]{1,3,2,0:T(8,128)(2,1)S(1)} %bitcast.53, bf16[4,128,3,128]{1,0,3,2:T(4,128)(2,1)S(1)} %multiply_convert_fusion.3), kind=kOutput, calls=%fused_computation.7.clone.1 | convolution fusion | flops 202897920 | bytes 5120000 | tf_op jit(solution)/shard_map/while/body/eval_jaxpr/gqhd,gkhd->ghqk/dot_general | solution.py:65
  225.3 0.8 copy.55
  226.1 2.8 %fusion.34 = bf16[4,128,3,128]{1,3,2,0:T(8,128)(2,1)S(1)} fusion(bf16[4,512,3,128]{1,3,2,0:T(8,128)(2,1)S(1)} %bitcast.55, f32[4,3,128,512]{3,2,1,0:T(8,128)} %get-tuple-element.179, f32[4,3,128]{2,1,0:T(4,128)S(1)} %get-tuple-element.180, pred[4,512]{1,0:T(4,128)(4,1)} %broadcast_compare_fusion.2), kind=kOutput, calls=%fused_computation.11.clone.1 | convolution fusion | flops 203882496 | bytes 5120000 | tf_op jit(solution)/shard_map/while/body/eval_jaxpr/ghqk,gkhd->gqhd/dot_general | solution.py:71
  229.5 0.8 constant_dynamic-update-slice_fusion.2
  230.3 1.0 constant_dynamic-slice_fusion.5
  231.8 0.7 constant_dynamic-slice_fusion.6
  232.5 1.2 multiply_convert_fusion.3
  233.7 0.7 fusion.31
  235.0 0.8 iota_add_fusion.2
  235.9 0.7 broadcast_compare_fusion.2
  236.5 3.1 %gather_fusion = bf16[4,512,2,384]{3,1,2,0:T(8,128)(2,1)S(1)} fusion(bf16[4,512,2,384]{3,1,2,0:T(8,128)(2,1)} %get-tuple-element.204, s32[1024]{0:T(1024)S(1)} %pad_clamp_fusion.3), kind=kCustom, calls=%fused_computation.clone.clone.1 | custom fusion | bytes 6291472 | tf_op jit(solution)/shard_map/while/body/eval_jaxpr/gather | solution.py:62
  239.7 2.0 fusion.32
  241.7 1.7 copy.56
  243.4 3.2 %fusion.33 = (f32[4,3,128]{2,1,0:T(4,128)S(1)}, f32[4,3,128,512]{3,2,1,0:T(8,128)}) fusion(pred[4,512]{1,0:T(4,128)(4,1)} %broadcast_compare_fusion.2, bf16[4,512,3,128]{1,3,2,0:T(8,128)(2,1)S(1)} %bitcast.53, bf16[4,128,3,128]{1,0,3,2:T(4,128)(2,1)S(1)} %multiply_convert_fusion.3), kind=kOutput, calls=%fused_computation.7.clone.1 | convolution fusion | flops 202897920 | bytes 5120000 | tf_op jit(solution)/shard_map/while/body/eval_jaxpr/gqhd,gkhd->ghqk/dot_general | solution.py:65
  246.5 0.8 copy.55
  247.3 2.8 %fusion.34 = bf16[4,128,3,128]{1,3,2,0:T(8,128)(2,1)S(1)} fusion(bf16[4,512,3,128]{1,3,2,0:T(8,128)(2,1)S(1)} %bitcast.55, f32[4,3,128,512]{3,2,1,0:T(8,128)} %get-tuple-element.179, f32[4,3,128]{2,1,0:T(4,128)S(1)} %get-tuple-element.180, pred[4,512]{1,0:T(4,128)(4,1)} %broadcast_compare_fusion.2), kind=kOutput, calls=%fused_computation.11.clone.1 | convolution fusion | flops 203882496 | bytes 5120000 | tf_op jit(solution)/shard_map/while/body/eval_jaxpr/ghqk,gkhd->gqhd/dot_general | solution.py:71
  250.8 0.8 constant_dynamic-update-slice_fusion.2
  (64 shorter events, 11.1 us)
Async XLA Ops:
  6.5 76.6 %copy-start = (s32[16]{0:T(128)S(1)}, s32[16]{0:T(128)}, u32[]{:S(2)}) copy-start(s32[16]{0:T(128)} %param.15) | copy-start | bytes 196
  6.5 46.1 %all-gather.3.cloned.1.call-start = ((), (), s32[]{:S(2)}) async-start(), calls=%async_computation | async-start | bytes 2949120 | tf_op jit(solution)/shard_map/all_gather | solution.py:24
  7.3 151.6 %all-gather.5.cloned.1.call-start = ((), (), s32[]{:S(2)}) async-start(), calls=%async_computation.1 | async-start | bytes 12976128 | tf_op jit(solution)/shard_map/all_gather | solution.py:38
  15.0 10.8 %copy-start.2 = (bf16[2048,384]{1,0:T(8,128)(2,1)S(1)}, bf16[2048,384]{1,0:T(8,128)(2,1)}, u32[]{:S(2)}) copy-start(bf16[2048,384]{1,0:T(8,128)(2,1)} %param.10) | copy-start | bytes 4718596
  52.7 27.6 %copy-start.3 = (f32[384]{0:T(512)S(1)}, f32[384]{0:T(512)}, u32[]{:S(2)}) copy-start(f32[384]{0:T(512)} %param.14) | copy-start | bytes 4612
  52.7 29.1 %copy-start.5 = (s32[1,16]{1,0:T(1,128)S(1)}, s32[1,16]{1,0:T(1,128)}, u32[]{:S(2)}) copy-start(s32[1,16]{1,0:T(1,128)} %param.17) | copy-start | bytes 196
  52.7 30.4 %copy-start.4 = (s32[16]{0:T(128)S(1)}, s32[16]{0:T(128)}, u32[]{:S(2)}) copy-start(s32[16]{0:T(128)} %param.16) | copy-start | bytes 196
  179.7 3.2 %copy-start.1 = (bf16[4,512,1,384]{3,1,2,0:T(8,128)(2,1)S(1)}, bf16[4,512,1,384]{3,1,2,0:T(8,128)(2,1)}, u32[]{:S(2)}) copy-start(bf16[4,512,1,384]{3,1,2,0:T(8,128)(2,1)} %get-tuple-element.177) | copy-start | bytes 4718596 | tf_op jit(solution)/shard_map/while
  200.9 3.2 %copy-start.1 = (bf16[4,512,1,384]{3,1,2,0:T(8,128)(2,1)S(1)}, bf16[4,512,1,384]{3,1,2,0:T(8,128)(2,1)}, u32[]{:S(2)}) copy-start(bf16[4,512,1,384]{3,1,2,0:T(8,128)(2,1)} %get-tuple-element.177) | copy-start | bytes 4718596 | tf_op jit(solution)/shard_map/while
  222.2 3.2 %copy-start.1 = (bf16[4,512,1,384]{3,1,2,0:T(8,128)(2,1)S(1)}, bf16[4,512,1,384]{3,1,2,0:T(8,128)(2,1)}, u32[]{:S(2)}) copy-start(bf16[4,512,1,384]{3,1,2,0:T(8,128)(2,1)} %get-tuple-element.177) | copy-start | bytes 4718596 | tf_op jit(solution)/shard_map/while
  243.4 3.2 %copy-start.1 = (bf16[4,512,1,384]{3,1,2,0:T(8,128)(2,1)S(1)}, bf16[4,512,1,384]{3,1,2,0:T(8,128)(2,1)}, u32[]{:S(2)}) copy-start(bf16[4,512,1,384]{3,1,2,0:T(8,128)(2,1)} %get-tuple-element.177) | copy-start | bytes 4718596 | tf_op jit(solution)/shard_map/while
Sparse Core Ops, SparseCore 0:
  9.2 43.4 all-gather.2
  81.3 77.4 all-gather.4
where the time goes:
time: 260 us; the launch traced here: 258 us
  waiting for transfers between devices  101 us (39%)
  local copies, waits for them, and re-layouts  76.6 us (29%)
  matrix products  29.8 us (11%)
  blocking collectives  21.3 us (8%)
  other arithmetic  15.8 us (6%)
  between operations  13.5 us (5%)
    all_gather x1, waiting for transfers between devices, local(): everything = lax.all_gather(local_pairs, ('rep', 'seq'), axis=0, tiled=True)  73.8 us
    all_gather x1, waiting for transfers between devices, local(): block_rows = lax.all_gather(text, 'enc', axis=1, tiled=True)  26.4 us
    psum x1, blocking collectives, local(): query_total, key_total = lax.psum((query_square, key_square), 'enc')  21.3 us
    slice x8, local copies, waits for them, and re-layouts, attend(): keys_block = chosen[:, :, 0].reshape(per_step, key_count, heads_here, HD)  14.8 us
    dot_general x4, matrix products, attend(): jnp.einsum('gqhd,gkhd->ghqk', scaled, keys_block, preferred_element_type=...  12.6 us
    gather x4, local copies, waits for them, and re-layouts, attend(): chosen = picked[slot_ids]  12.5 us
    dot_general x4, matrix products, attend(): jnp.einsum('ghqk,gkhd->gqhd', probs, values_block, preferred_element_type...  11.1 us
    dot_general x1, local copies, waits for them, and re-layouts, local(): jnp.einsum('trd,dc->trc', block_rows, flat_weight, preferred_element_type...  10.8 us
  transfers between devices with their start and end apart: 2, of which 2 were waited for; matrix products, arithmetic and copies ran while one was open for 9% of the time, Pallas kernels for 0%

commit v1 on v0

v1 whole, which is shorter than its diff:
```python
import functools

import jax
import jax.numpy as jnp
from jax import lax
from jax.experimental import pallas as pl
from jax.experimental.pallas import tpu as pltpu
from jax.sharding import PartitionSpec as P

HD = 128
FRAME = 128
V_DOWN = 2.0 ** -12
HIGH = 48 * 1024 * 1024


def ring(n, k):
    return [(i, (i + k) % n) for i in range(n)]


def pick_kernel(code, text, ahead, behind, far_a, far_b, out_a, out_b, sem):
    half = out_a.shape[0]
    copies = []
    for j in range(2 * half):
        target = (out_a if j < half else out_b).at[j % half]
        shift, slot = code[j] // 4, code[j] % 4

        def send(source, index, target=target, j=j):
            pltpu.make_async_copy(source.at[index], target, sem.at[j]).start()

        pl.when(shift == 0)(functools.partial(send, text, slot))
        pl.when(shift == 1)(functools.partial(send, behind, slot))
        pl.when((shift == 2) & (slot < 2))(functools.partial(send, far_a, slot % 2))
        pl.when((shift == 2) & (slot >= 2))(functools.partial(send, far_b, slot % 2))
        pl.when(shift == 3)(functools.partial(send, ahead, slot))
        copies.append(pltpu.make_async_copy(text.at[0], target, sem.at[j]))
    for copy in copies:
        copy.wait()


def pick(code, text, ahead, behind, far_a, far_b):
    n, rows, width = text.shape
    half = jax.ShapeDtypeStruct((n // 2, rows, width), text.dtype)
    return pl.pallas_call(
        pick_kernel,
        out_shape=(half, half),
        in_specs=[pl.BlockSpec(memory_space=pltpu.SMEM)] + [pl.BlockSpec(memory_space=pl.ANY)] * 5,
        out_specs=[pl.BlockSpec(memory_space=pl.ANY)] * 2,
        scratch_shapes=[pltpu.SemaphoreType.DMA((n,))],
        name="pick",
    )(code, text, ahead, behind, far_a, far_b)


def project_kernel(info, *refs):
    blocks_a, blocks_b, weight = refs[:8], refs[8:16], refs[16]
    keys_out, values_out, total = refs[17:]
    step = pl.program_id(0)
    pieces = []
    for ref in blocks_a + blocks_b:
        for t in range(2):
            pieces.append(ref[t])
    rows = jnp.concatenate(pieces, axis=0)
    part = jnp.dot(rows, weight[...], preferred_element_type=jnp.float32)

    @pl.when(step == 0)
    def _():
        total[...] = part

    @pl.when(step > 0)
    def _():
        total[...] += part

    @pl.when(step == pl.num_programs(0) - 1)
    def _():
        columns = keys_out.shape[-1]
        enc, seq = info[0], info[1]
        place = lax.broadcasted_iota(jnp.int32, (8, columns), 0)
        row = 0
        for offsets, base in (((0, -1, -2, -3, -4, 1, 2, 3), 0), ((0, -1, -2, -3, 1, 2, 3, 4), 2)):
            for offset in offsets:
                plane = lax.rem(enc + offset + 8, 8)
                for t in range(2):
                    both = total[row * 8:row * 8 + 8, :]
                    row += 1
                    live = plane * 64 + seq * 8 + place < info[2 + base + t]
                    keys_out[base + t, plane] = both[:, :columns]
                    values_out[base + t, plane] = jnp.where(
                        live, both[:, columns:] * V_DOWN, 0.0
                    ).astype(values_out.dtype)


def project(info, blocks_a, blocks_b, weight):
    width, both = weight.shape
    chunk = 512
    columns = both // 2
    block = pl.BlockSpec((2, 8, chunk), lambda k: (0, 0, k))
    whole = pl.BlockSpec((4, 8, 8, columns), lambda k: (0, 0, 0, 0))
    return pl.pallas_call(
        project_kernel,
        out_shape=(
            jax.ShapeDtypeStruct((4, 8, 8, columns), jnp.float32),
            jax.ShapeDtypeStruct((4, 8, 8, columns), jnp.bfloat16),
        ),
        grid=(width // chunk,),
        in_specs=[pl.BlockSpec(memory_space=pltpu.SMEM)]
        + [block] * 16
        + [pl.BlockSpec((chunk, both), lambda k: (k, 0))],
        out_specs=[whole, whole],
        scratch_shapes=[pltpu.VMEM((256, both), jnp.float32)],
        compiler_params=pltpu.CompilerParams(vmem_limit_bytes=HIGH),
        cost_estimate=pl.CostEstimate(
            flops=2 * 256 * width * both, bytes_accessed=2 * (256 * width + width * both), transcendentals=0
        ),
        name="project",
    )(info, *blocks_a, *blocks_b, weight)


def attend_kernel(info, bounds, queries, *refs):
    key_parts, value_parts = refs[:10], refs[10:20]
    out = refs[20]
    q_buf, o_buf, k_buf, v_buf, sem = refs[21:]
    seq, heads = info[1], queries.shape[1] // HD
    total_rows = queries.shape[0]

    def spots(core):
        y, c = seq // 2, (seq % 2 + core) % 2
        return [(2 * lax.rem(y + d + 4, 4) + c, lo, n) for d, lo, n in ((0, 0, 4), (-1, 0, 4), (1, 0, 4), (2, 0, 2), (2, 2, 2))]

    where = spots(0) + spots(1)
    copies = [pltpu.make_async_copy(queries, q_buf.at[pl.ds(0, total_rows)], sem.at[0])]
    for n, (spot, lo, count) in enumerate(where):
        target = pl.ds(pl.multiple_of(spot * 64, 64), 64)
        copies.append(
            pltpu.make_async_copy(key_parts[n], k_buf.at[pl.ds(lo, count), target], sem.at[1 + 4 * n])
        )
        for h in range(heads):
            copies.append(
                pltpu.make_async_copy(
                    value_parts[n].at[:, :, pl.ds(h * HD, HD)],
                    v_buf.at[h, pl.ds(lo, count), target, pl.ds(0, HD)],
                    sem.at[2 + 4 * n + h],
                )
            )
    for copy in copies:
        copy.start()
    q_buf[total_rows:] = jnp.zeros((q_buf.shape[0] - total_rows, q_buf.shape[1]), q_buf.dtype)
    spot = lax.broadcasted_iota(jnp.int32, (512, HD), 0)
    position = (spot // 8) % 8 * 64 + spot // 64 * 8 + spot % 8
    for t in range(4):
        live = jnp.where(position < info[2 + t], 1.0, 0.0).astype(v_buf.dtype)
        for h in range(heads):
            v_buf[h, t, :, HD:] = live
    for copy in copies:
        copy.wait()

    for t in range(4):
        first, last = bounds[t], bounds[t + 1]

        def one(i, carry, t=t, first=first):
            rows = pl.ds(pl.multiple_of((first + 2 * i) * FRAME, FRAME), 2 * FRAME)
            for h in range(heads):
                lanes = slice(h * HD, (h + 1) * HD)
                scores = lax.dot_general(
                    q_buf[rows, lanes], k_buf[t, :, lanes], (((1,), (1,)), ((), ())),
                    preferred_element_type=jnp.float32,
                )
                raised = jnp.exp(scores).astype(jnp.bfloat16)
                mixed = jnp.dot(raised, v_buf[h, t], preferred_element_type=jnp.float32)
                o_buf[rows, lanes] = (
                    mixed[:, :HD] * (1.0 / mixed[:, HD:]) * (1.0 / V_DOWN)
                ).astype(o_buf.dtype)
            return carry

        lax.fori_loop(0, (last - first + 1) // 2, one, 0)
    copy = pltpu.make_async_copy(o_buf.at[pl.ds(0, total_rows)], out, sem.at[0])
    copy.start()
    copy.wait()


def attend(info, bounds, queries, key_parts, value_parts):
    rows, columns = queries.shape
    heads = columns // HD
    smem = pl.BlockSpec(memory_space=pltpu.SMEM)
    hbm = pl.BlockSpec(memory_space=pl.ANY)
    return pl.pallas_call(
        attend_kernel,
        out_shape=jax.ShapeDtypeStruct((rows, columns), queries.dtype),
        in_specs=[smem, smem] + [hbm] * 21,
        out_specs=hbm,
        scratch_shapes=[
            pltpu.VMEM((rows + FRAME, columns), queries.dtype),
            pltpu.VMEM((rows + FRAME, columns), queries.dtype),
            pltpu.VMEM((4, 512, columns), queries.dtype),
            pltpu.VMEM((heads, 4, 512, 2 * HD), queries.dtype),
            pltpu.SemaphoreType.DMA((64,)),
        ],
        compiler_params=pltpu.CompilerParams(vmem_limit_bytes=HIGH),
        cost_estimate=pl.CostEstimate(flops=4 * rows * columns * 512, bytes_accessed=4 * rows * columns, transcendentals=0),
        name="attend",
    )(info, bounds, queries, *key_parts, *value_parts)


def spread(piece):
    up = [(s, (s + 2) % 8) for s in range(8)]
    down = [(s, (s - 2) % 8) for s in range(8)]
    core = [(s, s ^ 1) for s in range(8)]
    ahead = lax.ppermute(piece, "seq", up)
    behind = lax.ppermute(piece, "seq", down)
    far_a = lax.ppermute(ahead[:2], "seq", up)
    far_b = lax.ppermute(behind[2:], "seq", down)
    mine = [piece, ahead, behind, far_a, far_b]
    return mine + [lax.ppermute(part, "seq", core) for part in mine]


def enc_total(square):
    for d in (1, 2, 4):
        square = square + lax.ppermute(square, "enc", [(i, i ^ d) for i in range(8)])
    return square


def local(queries, text, kv_weight, query_gain, key_gain, prompt_len, served, frame_slot):
    columns = queries.shape[1]
    full_width = columns * 8
    enc, rep, seq = (lax.axis_index(a) for a in ("enc", "rep", "seq"))

    ahead = lax.ppermute(text, "rep", ring(4, 1))
    behind = lax.ppermute(text, "rep", ring(4, -1))
    far_a = lax.ppermute(ahead[:2], "rep", ring(4, 1))
    far_b = lax.ppermute(behind[2:], "rep", ring(4, -1))
    mine = lax.dynamic_slice_in_dim(served, rep * 4, 4)
    code = (mine // 4 - rep + 4) % 4 * 4 + mine % 4
    info = jnp.concatenate([jnp.stack([enc, seq]).astype(jnp.int32), prompt_len[mine]])
    bounds = jnp.sum(frame_slot.reshape(1, -1) < jnp.arange(5, dtype=jnp.int32)[:, None], axis=1, dtype=jnp.int32)

    query_float = queries.astype(jnp.float32)
    query_total = enc_total(jnp.sum(query_float * query_float, axis=-1))
    query_scale = lax.rsqrt(query_total / full_width + 1e-06)
    scaled = (query_float * query_scale[:, None] * query_gain * HD ** (-0.5)).astype(jnp.bfloat16)

    weight = kv_weight.reshape(kv_weight.shape[0], 2 * columns)

    part_a, part_b = pick(code, text, ahead, behind, far_a, far_b)
    up, down = ring(8, 1), ring(8, -1)
    a_up, a_down, b_up, b_down = [part_a], [part_a], [part_b], [part_b]
    for i in range(4):
        a_up.append(lax.ppermute(a_up[-1], "enc", up))
        if i < 3:
            a_down.append(lax.ppermute(a_down[-1], "enc", down))
            b_up.append(lax.ppermute(b_up[-1], "enc", up))
        b_down.append(lax.ppermute(b_down[-1], "enc", down))

    raw_keys, values = project(info, a_up + a_down[1:], b_up + b_down[1:], weight)
    raw_keys = raw_keys.reshape(4, 64, columns)
    value_parts = spread(values.reshape(4, 64, columns))
    key_total = enc_total(jnp.sum(raw_keys * raw_keys, axis=-1))
    key_scale = lax.rsqrt(key_total / full_width + 1e-06)
    place = jnp.arange(64, dtype=jnp.int32)
    position = place // 8 * 64 + seq * 8 + place % 8
    live = position[None, :] < info[2:, None]
    keys = jnp.where(
        live[:, :, None], raw_keys * key_scale[:, :, None] * key_gain, 0.0
    ).astype(jnp.bfloat16)
    key_parts = spread(keys)
    return attend(info, bounds, scaled, key_parts, value_parts)


def solution(mesh):
    placed = (
        P(("rep", "seq"), "enc"),
        P("rep", ("enc", "seq"), None),
        P(None, None, "enc"),
        P("enc"),
        P("enc"),
        P(),
        P(),
        P("rep", "seq"),
    )
    return jax.shard_map(
        local, mesh=mesh, in_specs=placed, out_specs=P(("rep", "seq"), "enc"), check_vma=False
    )
```

time: 260 us -> 137 us (0.53)
  waiting for transfers between devices: 101 us -> 23.6 us
  starting transfers between devices: 0.04 us -> 68.9 us
  local copies, waits for them, and re-layouts: 76.6 us -> 9.18 us
  Pallas kernels: 0 us -> 30.5 us
  matrix products: 29.8 us -> 0 us
  blocking collectives: 21.3 us -> 0 us
  between operations: 13.5 us -> 0.43 us
  other arithmetic: 15.8 us -> 4.15 us
    all_gather x2 -> x0, waiting for transfers between devices: 100 us -> none  [the longest x1 73.8 us: local(): everything = lax.all_gather(local_pairs, ('rep', 'seq'), axis=0, tiled=True)]
    ppermute x0 -> x42, starting transfers between devices: none -> 68.9 us  [the longest x10 17.1 us: spread(): return mine + [lax.ppermute(part, 'seq', core) for part in mine]]
    pallas_call x0 -> x3, Pallas kernels: none -> 30.5 us  [the longest x1 11.7 us: pick(): pl.pallas_call(pick_kernel, out_shape=(half, half), in_specs=[pl.BlockSpe...]
    dot_general x9 -> x0, matrix products: 29.8 us -> none  [the longest x4 12.6 us: attend(): jnp.einsum('gqhd,gkhd->ghqk', scaled, keys_block, preferred_element_type=...]
    ppermute x0 -> x42, waiting for transfers between devices: none -> 23.6 us  [the longest x6 10 us: enc_total(): lax.ppermute(square, 'enc', [(i, i ^ d) for i in range(8)])]
    gather x11 -> x1, local copies, waits for them, and re-layouts: 23.6 us -> 0.64 us  [local(): prompt_len[mine]]
    psum x1 -> x0, blocking collectives: 21.3 us -> none  [local(): query_total, key_total = lax.psum((query_square, key_square), 'enc')]
    slice x13 -> x6, local copies, waits for them, and re-layouts: 17.8 us -> 0.07 us  [the longest x2 0.02 us: spread(): far_a = lax.ppermute(ahead[:2], 'seq', up)]
  transfers between devices with their start and end apart: 2 -> 42, of which waited for: 2 -> 16; matrix products, arithmetic and copies ran while one was open for 9% -> 9% of each run, Pallas kernels for 0% -> 0%
where the time goes in v1:
time: 137 us
  starting transfers between devices  68.9 us (50%)
  Pallas kernels  30.5 us (22%)
  waiting for transfers between devices  23.6 us (17%)
  local copies, waits for them, and re-layouts  9.18 us (7%)
  other arithmetic  4.15 us (3%)
    ppermute x10, starting transfers between devices, spread(): return mine + [lax.ppermute(part, 'seq', core) for part in mine]  17.1 us
    ppermute x4, starting transfers between devices, local(): b_down.append(lax.ppermute(b_down[-1], 'enc', down))  13 us
    ppermute x6, starting transfers between devices, enc_total(): lax.ppermute(square, 'enc', [(i, i ^ d) for i in range(8)])  11.9 us
    pallas_call x1, Pallas kernels, pick(): pl.pallas_call(pick_kernel, out_shape=(half, half), in_specs=[pl.BlockSpe...  11.7 us
    ppermute x6, waiting for transfers between devices, enc_total(): lax.ppermute(square, 'enc', [(i, i ^ d) for i in range(8)])  10 us
    pallas_call x1, Pallas kernels, attend(): pl.pallas_call(attend_kernel, out_shape=jax.ShapeDtypeStruct((rows, colum...  9.39 us
    pallas_call x1, Pallas kernels, project(): pl.pallas_call(project_kernel, out_shape=(jax.ShapeDtypeStruct((4, 8, 8,...  9.34 us
    unnamed x23, local copies, waits for them, and re-layouts  8.4 us
  transfers between devices with their start and end apart: 42, of which 16 were waited for; matrix products, arithmetic and copies ran while one was open for 9% of the time, Pallas kernels for 0%

profile of v1, /device:TPU:1, one launch (start us, length us, event | category | flops | bytes accessed | tf_op | source)
XLA Modules:
  0.0 136.7 jit_solution(11130079085441691182)
XLA Ops:
  0.0 2.0 %collective-permute-start.3 = (bf16[4,8,5120]{2,1,0:T(8,128)(2,1)}, bf16[4,8,5120]{2,1,0:T(8,128)(2,1)S(1)}, u32[]{:S(2)}, u32[]{:S(2)}) collective-permute-start(bf16[4,8,5120]{2,1,0:T(8,128)(2,1)} %text.1), channel_id=1, source_target_pairs={{0,8},{8,16},{16,24},{24,0},{1,9},{9,17},{17,25},{25,1},{2,10},{10... | collective-permute-start | bytes 983048 | tf_op jit(solution)/shard_map/ppermute | solution.py:225
  2.0 1.4 collective-permute-start.4
  3.4 5.3 %collective-permute-done.3.ahead = bf16[4,8,5120]{2,1,0:T(8,128)(2,1)S(1)} collective-permute-done((bf16[4,8,5120]{2,1,0:T(8,128)(2,1)}, bf16[4,8,5120]{2,1,0:T(8,128)(2,1)S(1)}, u32[]{:S(2)}, u32[]{:S(2)}) %collective-permute-start.3) | collective-permute-done | bytes 327712 | tf_op jit(solution)/shard_map/ppermute | solution.py:225
  8.7 2.0 %collective-permute-start.5 = (bf16[2,8,5120]{2,1,0:T(8,128)(2,1)S(1)}, bf16[2,8,5120]{2,1,0:T(8,128)(2,1)S(1)}, u32[]{:S(2)}, u32[]{:S(2)}) collective-permute-start(bf16[2,8,5120]{2,1,0:T(8,128)(2,1)S(1)} %slice.26), channel_id=1, source_target_pairs={{0,8},{8,16},{16,24},{24,0},{1,9},{9,17},{17,25},{25,1},{2,10},{10... | collective-permute-start | bytes 491528 | tf_op jit(solution)/shard_map/ppermute | solution.py:227
  10.7 1.7 %collective-permute-start.6 = (bf16[2,8,5120]{2,1,0:T(8,128)(2,1)S(1)}, bf16[2,8,5120]{2,1,0:T(8,128)(2,1)S(1)}, u32[]{:S(2)}, u32[]{:S(2)}) collective-permute-start(bf16[2,8,5120]{2,1,0:T(8,128)(2,1)S(1)} %slice.27), channel_id=1, source_target_pairs={{0,24},{8,0},{16,8},{24,16},{1,25},{9,1},{17,9},{25,17},{2,26},{10... | collective-permute-start | bytes 491528 | tf_op jit(solution)/shard_map/ppermute | solution.py:228
  12.3 1.3 fusion.8
  13.6 1.3 collective-permute-done.5.far_a
  15.0 0.6 copy-done.6
  15.6 11.7 %pick.1 = (bf16[2,8,5120]{2,1,0:T(8,128)(2,1)}, bf16[2,8,5120]{2,1,0:T(8,128)(2,1)}) custom-call(s32[4]{0:T(128)} %get-tuple-element.13.code, bf16[4,8,5120]{2,1,0:T(8,128)(2,1)} %text.1, bf16[4,8,5120]{2,1,0:T(8,128)(2,1)} %copy-done.4, bf16[4,8,5120]{2,1,0:T(8,128)(2,1)} %copy-done.5, bf16[2,8,5120]{2,1,0:T(8,128)(2,1)} %copy-done.6, ...), custom_call_target="tpu_custom_call" | custom-call | tf_op jit(solution)/shard_map/pick/pallas_call | solution.py:43
  27.4 3.1 %collective-permute-start.7 = (bf16[2,8,5120]{2,1,0:T(8,128)(2,1)}, bf16[2,8,5120]{2,1,0:T(8,128)(2,1)S(1)}, u32[]{:S(2)}, u32[]{:S(2)}) collective-permute-start(bf16[2,8,5120]{2,1,0:T(8,128)(2,1)} %get-tuple-element.9.refs_0_), channel_id=1, source_target_pairs={{0,32},{32,64},{64,96},{96,128},{128,160},{160,192},{192,224},{224... | collective-permute-start | bytes 491528 | tf_op jit(solution)/shard_map/ppermute | solution.py:245
  30.5 4.0 %collective-permute-start.17 = (bf16[2,8,5120]{2,1,0:T(8,128)(2,1)}, bf16[2,8,5120]{2,1,0:T(8,128)(2,1)S(1)}, u32[]{:S(2)}, u32[]{:S(2)}) collective-permute-start(bf16[2,8,5120]{2,1,0:T(8,128)(2,1)} %get-tuple-element.10.refs_8_), channel_id=1, source_target_pairs={{0,224},{32,0},{64,32},{96,64},{128,96},{160,128},{192,160},{224,1... | collective-permute-start | bytes 491528 | tf_op jit(solution)/shard_map/ppermute | solution.py:249
  34.5 1.4 %collective-permute-start.11 = (bf16[2,8,5120]{2,1,0:T(8,128)(2,1)}, bf16[2,8,5120]{2,1,0:T(8,128)(2,1)S(1)}, u32[]{:S(2)}, u32[]{:S(2)}) collective-permute-start(bf16[2,8,5120]{2,1,0:T(8,128)(2,1)} %get-tuple-element.9.refs_0_), channel_id=1, source_target_pairs={{0,224},{32,0},{64,32},{96,64},{128,96},{160,128},{192,160},{224,1... | collective-permute-start | bytes 491528 | tf_op jit(solution)/shard_map/ppermute | solution.py:247
  35.9 0.1 collective-permute-start.14
  36.0 1.4 collective-permute-done.7.refs_1_
  37.3 2.8 %collective-permute-start.18 = (bf16[2,8,5120]{2,1,0:T(8,128)(2,1)S(1)}, bf16[2,8,5120]{2,1,0:T(8,128)(2,1)S(1)}, u32[]{:S(2)}, u32[]{:S(2)}) collective-permute-start(bf16[2,8,5120]{2,1,0:T(8,128)(2,1)S(1)} %collective-permute-done.17.refs_12_), channel_id=1, source_target_pairs={{0,224},{32,0},{64,32},{96,64},{128,96},{160,128},{192,160},{224,1... | collective-permute-start | bytes 491528 | tf_op jit(solution)/shard_map/ppermute | solution.py:249
  40.1 0.2 collective-permute-done.11.refs_5_
  40.4 2.1 %collective-permute-start.12 = (bf16[2,8,5120]{2,1,0:T(8,128)(2,1)S(1)}, bf16[2,8,5120]{2,1,0:T(8,128)(2,1)S(1)}, u32[]{:S(2)}, u32[]{:S(2)}) collective-permute-start(bf16[2,8,5120]{2,1,0:T(8,128)(2,1)S(1)} %collective-permute-done.11.refs_5_), channel_id=1, source_target_pairs={{0,224},{32,0},{64,32},{96,64},{128,96},{160,128},{192,160},{224,1... | collective-permute-start | bytes 491528 | tf_op jit(solution)/shard_map/ppermute | solution.py:247
  42.4 1.3 collective-permute-done.8.refs_2_
  43.7 0.3 collective-permute-done.18.refs_13_
  44.0 3.2 %collective-permute-start.19 = (bf16[2,8,5120]{2,1,0:T(8,128)(2,1)S(1)}, bf16[2,8,5120]{2,1,0:T(8,128)(2,1)S(1)}, u32[]{:S(2)}, u32[]{:S(2)}) collective-permute-start(bf16[2,8,5120]{2,1,0:T(8,128)(2,1)S(1)} %collective-permute-done.18.refs_13_), channel_id=1, source_target_pairs={{0,224},{32,0},{64,32},{96,64},{128,96},{160,128},{192,160},{224,1... | collective-permute-start | bytes 491528 | tf_op jit(solution)/shard_map/ppermute | solution.py:249
  47.2 2.3 %collective-permute-start.13 = (bf16[2,8,5120]{2,1,0:T(8,128)(2,1)S(1)}, bf16[2,8,5120]{2,1,0:T(8,128)(2,1)S(1)}, u32[]{:S(2)}, u32[]{:S(2)}) collective-permute-start(bf16[2,8,5120]{2,1,0:T(8,128)(2,1)S(1)} %collective-permute-done.12.refs_6_), channel_id=1, source_target_pairs={{0,224},{32,0},{64,32},{96,64},{128,96},{160,128},{192,160},{224,1... | collective-permute-start | bytes 491528 | tf_op jit(solution)/shard_map/ppermute | solution.py:247
  49.5 1.3 collective-permute-done.9.refs_3_
  50.8 3.0 %collective-permute-start.20 = (bf16[2,8,5120]{2,1,0:T(8,128)(2,1)S(1)}, bf16[2,8,5120]{2,1,0:T(8,128)(2,1)S(1)}, u32[]{:S(2)}, u32[]{:S(2)}) collective-permute-start(bf16[2,8,5120]{2,1,0:T(8,128)(2,1)S(1)} %collective-permute-done.19.refs_14_), channel_id=1, source_target_pairs={{0,224},{32,0},{64,32},{96,64},{128,96},{160,128},{192,160},{224,1... | collective-permute-start | bytes 491528 | tf_op jit(solution)/shard_map/ppermute | solution.py:249
  53.8 7.7 %copy.9 = bf16[640,8,2,384]{3,1,2,0:T(8,128)(2,1)} copy(bf16[640,8,2,384]{3,2,1,0:T(2,128)(2,1)} %bitcast.19) | data formatting | bytes 15728640
  61.5 0.6 gather_fusion
  62.2 0.1 pad_add_fusion.info
  62.3 9.3 %project.1 = (f32[4,8,8,384]{3,2,1,0:T(8,128)S(1)}, bf16[4,8,8,384]{3,2,1,0:T(8,128)(2,1)S(1)}) custom-call(s32[6]{0:T(128)S(1)} %pad_add_fusion.info, bf16[2,8,5120]{2,1,0:T(8,128)(2,1)S(1)} %copy-done.1, bf16[2,8,5120]{2,1,0:T(8,128)(2,1)S(1)} %collective-permute-done.7.refs_1_, bf16[2,8,5120]{2,1,0:T(8,128)(2,1)S(1)} %collective-permute-done.8.refs_2_, ...), custom_call_target="tpu_custom_call" | custom-call | flops 2013265920 | bytes 10485760 | tf_op jit(solution)/shard_map/project/pallas_call | solution.py:97
  71.7 0.1 multiply_reduce_fusion
  71.8 0.1 reduce_sum.32
  71.9 2.4 %collective-permute-done.21 = f32[4,64]{1,0:T(4,128)S(1)} collective-permute-done((f32[4,64]{1,0:T(4,128)S(1)}, f32[4,64]{1,0:T(4,128)S(1)}, u32[]{:S(2)}, u32[]{:S(2)}) %collective-permute-start.21) | collective-permute-done | bytes 1056 | tf_op jit(solution)/shard_map/ppermute | solution.py:216
  74.4 2.0 %collective-permute-start.22 = (f32[4,64]{1,0:T(4,128)S(1)}, f32[4,64]{1,0:T(4,128)S(1)}, u32[]{:S(2)}, u32[]{:S(2)}) collective-permute-start(f32[4,64]{1,0:T(4,128)S(1)} %add.100), channel_id=1, source_target_pairs={{0,64},{32,96},{64,0},{96,32},{128,192},{160,224},{192,128},{224,1... | collective-permute-start | bytes 3080 | tf_op jit(solution)/shard_map/ppermute | solution.py:216
  76.4 1.3 collective-permute-done.22
  77.7 5.6 %collective-permute-start.23 = (f32[4,64]{1,0:T(4,128)S(1)}, f32[4,64]{1,0:T(4,128)S(1)}, u32[]{:S(2)}, u32[]{:S(2)}) collective-permute-start(f32[4,64]{1,0:T(4,128)S(1)} %add.101), channel_id=1, source_target_pairs={{0,128},{32,160},{64,192},{96,224},{128,0},{160,32},{192,64},{224,... | collective-permute-start | bytes 3080 | tf_op jit(solution)/shard_map/ppermute | solution.py:216
  83.4 1.3 collective-permute-start.33
  84.7 1.4 %collective-permute-start.34 = (bf16[4,64,384]{2,1,0:T(8,128)(2,1)S(1)}, bf16[4,64,384]{2,1,0:T(8,128)(2,1)S(1)}, u32[]{:S(2)}, u32[]{:S(2)}) collective-permute-start(bf16[4,64,384]{2,1,0:T(8,128)(2,1)S(1)} %bitcast.15), channel_id=1, source_target_pairs={{0,6},{1,7},{2,0},{3,1},{4,2},{5,3},{6,4},{7,5},{8,14},{9,15},{10,... | collective-permute-start | bytes 589832 | tf_op jit(solution)/shard_map/ppermute | solution.py:207
  86.1 0.1 fusion.6.refs_0_
  86.3 0.1 collective-permute-start.24
  86.4 2.7 %collective-permute-start.25 = (bf16[4,64,384]{2,1,0:T(8,128)(2,1)S(1)}, bf16[4,64,384]{2,1,0:T(8,128)(2,1)S(1)}, u32[]{:S(2)}, u32[]{:S(2)}) collective-permute-start(bf16[4,64,384]{2,1,0:T(8,128)(2,1)S(1)} %fusion.6.refs_0_), channel_id=1, source_target_pairs={{0,6},{1,7},{2,0},{3,1},{4,2},{5,3},{6,4},{7,5},{8,14},{9,15},{10,... | collective-permute-start | bytes 589832 | tf_op jit(solution)/shard_map/ppermute | solution.py:207
  89.0 1.8 %fusion = f32[2048]{0:T(1024)S(1)} fusion(bf16[2048,384]{1,0:T(8,128)(2,1)} %param.8), kind=kLoop, calls=%fused_computation.3 | loop fusion | flops 2357248 | bytes 1581056 | tf_op jit(solution)/shard_map/reduce_sum | solution.py:235
  90.8 0.1 collective-permute-start
  90.9 2.8 %collective-permute-done = f32[2048]{0:T(1024)S(1)} collective-permute-done((f32[2048]{0:T(1024)S(1)}, f32[2048]{0:T(1024)S(1)}, u32[]{:S(2)}, u32[]{:S(2)}) %collective-permute-start) | collective-permute-done | bytes 8224 | tf_op jit(solution)/shard_map/ppermute | solution.py:216
  93.7 0.1 collective-permute-start.1
  93.8 3.6 %collective-permute-done.1 = f32[2048]{0:T(1024)S(1)} collective-permute-done((f32[2048]{0:T(1024)S(1)}, f32[2048]{0:T(1024)S(1)}, u32[]{:S(2)}, u32[]{:S(2)}) %collective-permute-start.1) | collective-permute-done | bytes 8224 | tf_op jit(solution)/shard_map/ppermute | solution.py:216
  97.4 12.3 %collective-permute-start.37 = (bf16[4,64,384]{2,1,0:T(8,128)(2,1)S(1)}, bf16[4,64,384]{2,1,0:T(8,128)(2,1)S(1)}, u32[]{:S(2)}, u32[]{:S(2)}) collective-permute-start(bf16[4,64,384]{2,1,0:T(8,128)(2,1)S(1)} %bitcast.16), channel_id=1, source_target_pairs={{0,1},{1,0},{2,3},{3,2},{4,5},{5,4},{6,7},{7,6},{8,9},{9,8},{10,11... | collective-permute-start | bytes 589832 | tf_op jit(solution)/shard_map/ppermute | solution.py:211
  109.8 4.0 %collective-permute-start.2 = (f32[2048]{0:T(1024)S(1)}, f32[2048]{0:T(1024)S(1)}, u32[]{:S(2)}, u32[]{:S(2)}) collective-permute-start(f32[2048]{0:T(1024)S(1)} %add.88), channel_id=1, source_target_pairs={{0,128},{32,160},{64,192},{96,224},{128,0},{160,32},{192,64},{224,... | collective-permute-start | bytes 24584 | tf_op jit(solution)/shard_map/ppermute | solution.py:216
  113.8 0.4 collective-permute-start.35
  114.2 2.6 %collective-permute-start.36 = (bf16[2,64,384]{2,1,0:T(8,128)(2,1)S(1)}, bf16[2,64,384]{2,1,0:T(8,128)(2,1)S(1)}, u32[]{:S(2)}, u32[]{:S(2)}) collective-permute-start(bf16[2,64,384]{2,1,0:T(8,128)(2,1)S(1)} %slice.31), channel_id=1, source_target_pairs={{0,6},{1,7},{2,0},{3,1},{4,2},{5,3},{6,4},{7,5},{8,14},{9,15},{10,... | collective-permute-start | bytes 294920 | tf_op jit(solution)/shard_map/ppermute | solution.py:209
  116.8 0.1 convert_reduce_fusion.bounds
  116.9 1.4 %collective-permute-start.38 = (bf16[4,64,384]{2,1,0:T(8,128)(2,1)S(1)}, bf16[4,64,384]{2,1,0:T(8,128)(2,1)S(1)}, u32[]{:S(2)}, u32[]{:S(2)}) collective-permute-start(bf16[4,64,384]{2,1,0:T(8,128)(2,1)S(1)} %collective-permute-done.33.refs_11_), channel_id=1, source_target_pairs={{0,1},{1,0},{2,3},{3,2},{4,5},{5,4},{6,7},{7,6},{8,9},{9,8},{10,11... | collective-permute-start | bytes 589832 | tf_op jit(solution)/shard_map/ppermute | solution.py:211
  118.4 0.1 collective-permute-start.39
  118.5 0.3 collective-permute-done.35.refs_13_
  118.8 2.4 %collective-permute-start.27 = (bf16[2,64,384]{2,1,0:T(8,128)(2,1)S(1)}, bf16[2,64,384]{2,1,0:T(8,128)(2,1)S(1)}, u32[]{:S(2)}, u32[]{:S(2)}) collective-permute-start(bf16[2,64,384]{2,1,0:T(8,128)(2,1)S(1)} %slice.29), channel_id=1, source_target_pairs={{0,6},{1,7},{2,0},{3,1},{4,2},{5,3},{6,4},{7,5},{8,14},{9,15},{10,... | collective-permute-start | bytes 294920 | tf_op jit(solution)/shard_map/ppermute | solution.py:209
  121.2 1.0 collective-permute-start.40
  122.1 1.5 %collective-permute-done.26.refs_3_ = bf16[2,64,384]{2,1,0:T(8,128)(2,1)S(1)} collective-permute-done((bf16[2,64,384]{2,1,0:T(8,128)(2,1)S(1)}, bf16[2,64,384]{2,1,0:T(8,128)(2,1)S(1)}, u32[]{:S(2)}, u32[]{:S(2)}) %collective-permute-start.26) | collective-permute-done | bytes 98336 | tf_op jit(solution)/shard_map/ppermute | solution.py:208
  123.7 1.2 collective-permute-start.29
  124.9 0.4 collective-permute-start.30
  125.3 0.1 collective-permute-start.41
  125.4 0.4 collective-permute-start.31
  125.8 0.1 collective-permute-start.32
  125.9 0.5 fusion.3.queries
  126.5 0.1 collective-permute-done.41.refs_19_
  126.6 0.2 collective-permute-done.31.refs_8_
  126.8 0.4 collective-permute-done.32.refs_9_
  127.1 9.4 %attend.1 = bf16[2048,384]{1,0:T(8,128)(2,1)} custom-call(s32[6]{0:T(128)S(1)} %pad_add_fusion.info, s32[5]{0:T(128)S(1)} %convert_reduce_fusion.bounds, bf16[2048,384]{1,0:T(8,128)(2,1)S(1)} %fusion.3.queries, bf16[4,64,384]{2,1,0:T(8,128)(2,1)S(1)} %fusion.6.refs_0_, bf16[4,64,384]{2,1,0:T(8,128)(2,1)S(1)} %collective-permute-done.24.refs_1_, ...), custom_call_target="tpu_custom_call" | custom-call | flops 1610612736 | bytes 3145728 | tf_op jit(solution)/shard_map/attend/pallas_call | solution.py:184
  (70 shorter events, 0.4 us)
Async XLA Ops:
  0.0 61.5 %copy-start = (s32[16]{0:T(128)S(1)}, s32[16]{0:T(128)}, u32[]{:S(2)}) copy-start(s32[16]{0:T(128)} %param.13) | copy-start | bytes 196
  0.0 8.7 %collective-permute-start.3 = (bf16[4,8,5120]{2,1,0:T(8,128)(2,1)}, bf16[4,8,5120]{2,1,0:T(8,128)(2,1)S(1)}, u32[]{:S(2)}, u32[]{:S(2)}) collective-permute-start(bf16[4,8,5120]{2,1,0:T(8,128)(2,1)} %text.1), channel_id=1, source_target_pairs={{0,8},{8,16},{16,24},{24,0},{1,9},{9,17},{17,25},{25,1},{2,10},{10... | collective-permute-start | bytes 983048 | tf_op jit(solution)/shard_map/ppermute | solution.py:225
  2.0 8.6 %collective-permute-start.4 = (bf16[4,8,5120]{2,1,0:T(8,128)(2,1)}, bf16[4,8,5120]{2,1,0:T(8,128)(2,1)S(1)}, u32[]{:S(2)}, u32[]{:S(2)}) collective-permute-start(bf16[4,8,5120]{2,1,0:T(8,128)(2,1)} %text.1), channel_id=1, source_target_pairs={{0,24},{8,0},{16,8},{24,16},{1,25},{9,1},{17,9},{25,17},{2,26},{10... | collective-permute-start | bytes 983048 | tf_op jit(solution)/shard_map/ppermute | solution.py:226
  8.7 6.3 %copy-start.4 = (bf16[4,8,5120]{2,1,0:T(8,128)(2,1)}, bf16[4,8,5120]{2,1,0:T(8,128)(2,1)S(1)}, u32[]{:S(2)}) copy-start(bf16[4,8,5120]{2,1,0:T(8,128)(2,1)S(1)} %collective-permute-done.3.ahead) | copy-start | bytes 983044
  8.7 6.2 %collective-permute-start.5 = (bf16[2,8,5120]{2,1,0:T(8,128)(2,1)S(1)}, bf16[2,8,5120]{2,1,0:T(8,128)(2,1)S(1)}, u32[]{:S(2)}, u32[]{:S(2)}) collective-permute-start(bf16[2,8,5120]{2,1,0:T(8,128)(2,1)S(1)} %slice.26), channel_id=1, source_target_pairs={{0,8},{8,16},{16,24},{24,0},{1,9},{9,17},{17,25},{25,1},{2,10},{10... | collective-permute-start | bytes 491528 | tf_op jit(solution)/shard_map/ppermute | solution.py:227
  10.6 4.3 %copy-start.5 = (bf16[4,8,5120]{2,1,0:T(8,128)(2,1)}, bf16[4,8,5120]{2,1,0:T(8,128)(2,1)S(1)}, u32[]{:S(2)}) copy-start(bf16[4,8,5120]{2,1,0:T(8,128)(2,1)S(1)} %collective-permute-done.4.behind) | copy-start | bytes 983044
  10.7 4.3 %collective-permute-start.6 = (bf16[2,8,5120]{2,1,0:T(8,128)(2,1)S(1)}, bf16[2,8,5120]{2,1,0:T(8,128)(2,1)S(1)}, u32[]{:S(2)}, u32[]{:S(2)}) collective-permute-start(bf16[2,8,5120]{2,1,0:T(8,128)(2,1)S(1)} %slice.27), channel_id=1, source_target_pairs={{0,24},{8,0},{16,8},{24,16},{1,25},{9,1},{17,9},{25,17},{2,26},{10... | collective-permute-start | bytes 491528 | tf_op jit(solution)/shard_map/ppermute | solution.py:228
  14.9 0.7 copy-start.6
  14.9 0.7 copy-start.7
  27.4 10.0 %collective-permute-start.7 = (bf16[2,8,5120]{2,1,0:T(8,128)(2,1)}, bf16[2,8,5120]{2,1,0:T(8,128)(2,1)S(1)}, u32[]{:S(2)}, u32[]{:S(2)}) collective-permute-start(bf16[2,8,5120]{2,1,0:T(8,128)(2,1)} %get-tuple-element.9.refs_0_), channel_id=1, source_target_pairs={{0,32},{32,64},{64,96},{96,128},{128,160},{160,192},{192,224},{224... | collective-permute-start | bytes 491528 | tf_op jit(solution)/shard_map/ppermute | solution.py:245
  30.5 6.9 %collective-permute-start.17 = (bf16[2,8,5120]{2,1,0:T(8,128)(2,1)}, bf16[2,8,5120]{2,1,0:T(8,128)(2,1)S(1)}, u32[]{:S(2)}, u32[]{:S(2)}) collective-permute-start(bf16[2,8,5120]{2,1,0:T(8,128)(2,1)} %get-tuple-element.10.refs_8_), channel_id=1, source_target_pairs={{0,224},{32,0},{64,32},{96,64},{128,96},{160,128},{192,160},{224,1... | collective-permute-start | bytes 491528 | tf_op jit(solution)/shard_map/ppermute | solution.py:249
  34.5 5.8 %collective-permute-start.11 = (bf16[2,8,5120]{2,1,0:T(8,128)(2,1)}, bf16[2,8,5120]{2,1,0:T(8,128)(2,1)S(1)}, u32[]{:S(2)}, u32[]{:S(2)}) collective-permute-start(bf16[2,8,5120]{2,1,0:T(8,128)(2,1)} %get-tuple-element.9.refs_0_), channel_id=1, source_target_pairs={{0,224},{32,0},{64,32},{96,64},{128,96},{160,128},{192,160},{224,1... | collective-permute-start | bytes 491528 | tf_op jit(solution)/shard_map/ppermute | solution.py:247
  35.9 6.6 %collective-permute-start.14 = (bf16[2,8,5120]{2,1,0:T(8,128)(2,1)}, bf16[2,8,5120]{2,1,0:T(8,128)(2,1)S(1)}, u32[]{:S(2)}, u32[]{:S(2)}) collective-permute-start(bf16[2,8,5120]{2,1,0:T(8,128)(2,1)} %get-tuple-element.10.refs_8_), channel_id=1, source_target_pairs={{0,32},{32,64},{64,96},{96,128},{128,160},{160,192},{192,224},{224... | collective-permute-start | bytes 491528 | tf_op jit(solution)/shard_map/ppermute | solution.py:248
  37.3 6.4 %collective-permute-start.8 = (bf16[2,8,5120]{2,1,0:T(8,128)(2,1)S(1)}, bf16[2,8,5120]{2,1,0:T(8,128)(2,1)S(1)}, u32[]{:S(2)}, u32[]{:S(2)}) collective-permute-start(bf16[2,8,5120]{2,1,0:T(8,128)(2,1)S(1)} %collective-permute-done.7.refs_1_), channel_id=1, source_target_pairs={{0,32},{32,64},{64,96},{96,128},{128,160},{160,192},{192,224},{224... | collective-permute-start | bytes 491528 | tf_op jit(solution)/shard_map/ppermute | solution.py:245
  37.3 6.7 %collective-permute-start.18 = (bf16[2,8,5120]{2,1,0:T(8,128)(2,1)S(1)}, bf16[2,8,5120]{2,1,0:T(8,128)(2,1)S(1)}, u32[]{:S(2)}, u32[]{:S(2)}) collective-permute-start(bf16[2,8,5120]{2,1,0:T(8,128)(2,1)S(1)} %collective-permute-done.17.refs_12_), channel_id=1, source_target_pairs={{0,224},{32,0},{64,32},{96,64},{128,96},{160,128},{192,160},{224,1... | collective-permute-start | bytes 491528 | tf_op jit(solution)/shard_map/ppermute | solution.py:249
  40.4 6.9 %collective-permute-start.12 = (bf16[2,8,5120]{2,1,0:T(8,128)(2,1)S(1)}, bf16[2,8,5120]{2,1,0:T(8,128)(2,1)S(1)}, u32[]{:S(2)}, u32[]{:S(2)}) collective-permute-start(bf16[2,8,5120]{2,1,0:T(8,128)(2,1)S(1)} %collective-permute-done.11.refs_5_), channel_id=1, source_target_pairs={{0,224},{32,0},{64,32},{96,64},{128,96},{160,128},{192,160},{224,1... | collective-permute-start | bytes 491528 | tf_op jit(solution)/shard_map/ppermute | solution.py:247
  42.4 7.1 %collective-permute-start.15 = (bf16[2,8,5120]{2,1,0:T(8,128)(2,1)S(1)}, bf16[2,8,5120]{2,1,0:T(8,128)(2,1)S(1)}, u32[]{:S(2)}, u32[]{:S(2)}) collective-permute-start(bf16[2,8,5120]{2,1,0:T(8,128)(2,1)S(1)} %collective-permute-done.14.refs_9_), channel_id=1, source_target_pairs={{0,32},{32,64},{64,96},{96,128},{128,160},{160,192},{192,224},{224... | collective-permute-start | bytes 491528 | tf_op jit(solution)/shard_map/ppermute | solution.py:248
  43.7 7.1 %collective-permute-start.9 = (bf16[2,8,5120]{2,1,0:T(8,128)(2,1)S(1)}, bf16[2,8,5120]{2,1,0:T(8,128)(2,1)S(1)}, u32[]{:S(2)}, u32[]{:S(2)}) collective-permute-start(bf16[2,8,5120]{2,1,0:T(8,128)(2,1)S(1)} %collective-permute-done.8.refs_2_), channel_id=1, source_target_pairs={{0,32},{32,64},{64,96},{96,128},{128,160},{160,192},{192,224},{224... | collective-permute-start | bytes 491528 | tf_op jit(solution)/shard_map/ppermute | solution.py:245
  44.0 6.8 %collective-permute-start.19 = (bf16[2,8,5120]{2,1,0:T(8,128)(2,1)S(1)}, bf16[2,8,5120]{2,1,0:T(8,128)(2,1)S(1)}, u32[]{:S(2)}, u32[]{:S(2)}) collective-permute-start(bf16[2,8,5120]{2,1,0:T(8,128)(2,1)S(1)} %collective-permute-done.18.refs_13_), channel_id=1, source_target_pairs={{0,224},{32,0},{64,32},{96,64},{128,96},{160,128},{192,160},{224,1... | collective-permute-start | bytes 491528 | tf_op jit(solution)/shard_map/ppermute | solution.py:249
  47.2 15.0 %collective-permute-start.13 = (bf16[2,8,5120]{2,1,0:T(8,128)(2,1)S(1)}, bf16[2,8,5120]{2,1,0:T(8,128)(2,1)S(1)}, u32[]{:S(2)}, u32[]{:S(2)}) collective-permute-start(bf16[2,8,5120]{2,1,0:T(8,128)(2,1)S(1)} %collective-permute-done.12.refs_6_), channel_id=1, source_target_pairs={{0,224},{32,0},{64,32},{96,64},{128,96},{160,128},{192,160},{224,1... | collective-permute-start | bytes 491528 | tf_op jit(solution)/shard_map/ppermute | solution.py:247
  49.5 12.8 %collective-permute-start.16 = (bf16[2,8,5120]{2,1,0:T(8,128)(2,1)S(1)}, bf16[2,8,5120]{2,1,0:T(8,128)(2,1)S(1)}, u32[]{:S(2)}, u32[]{:S(2)}) collective-permute-start(bf16[2,8,5120]{2,1,0:T(8,128)(2,1)S(1)} %collective-permute-done.15.refs_10_), channel_id=1, source_target_pairs={{0,32},{32,64},{64,96},{96,128},{128,160},{160,192},{192,224},{224... | collective-permute-start | bytes 491528 | tf_op jit(solution)/shard_map/ppermute | solution.py:248
  50.8 11.5 %collective-permute-start.10 = (bf16[2,8,5120]{2,1,0:T(8,128)(2,1)S(1)}, bf16[2,8,5120]{2,1,0:T(8,128)(2,1)S(1)}, u32[]{:S(2)}, u32[]{:S(2)}) collective-permute-start(bf16[2,8,5120]{2,1,0:T(8,128)(2,1)S(1)} %collective-permute-done.9.refs_3_), channel_id=1, source_target_pairs={{0,32},{32,64},{64,96},{96,128},{128,160},{160,192},{192,224},{224... | collective-permute-start | bytes 491528 | tf_op jit(solution)/shard_map/ppermute | solution.py:245
  50.8 11.5 %collective-permute-start.20 = (bf16[2,8,5120]{2,1,0:T(8,128)(2,1)S(1)}, bf16[2,8,5120]{2,1,0:T(8,128)(2,1)S(1)}, u32[]{:S(2)}, u32[]{:S(2)}) collective-permute-start(bf16[2,8,5120]{2,1,0:T(8,128)(2,1)S(1)} %collective-permute-done.19.refs_14_), channel_id=1, source_target_pairs={{0,224},{32,0},{64,32},{96,64},{128,96},{160,128},{192,160},{224,1... | collective-permute-start | bytes 491528 | tf_op jit(solution)/shard_map/ppermute | solution.py:249
  53.8 8.4 %copy-start.1 = (bf16[2,8,5120]{2,1,0:T(8,128)(2,1)S(1)}, bf16[2,8,5120]{2,1,0:T(8,128)(2,1)}, u32[]{:S(2)}) copy-start(bf16[2,8,5120]{2,1,0:T(8,128)(2,1)} %get-tuple-element.9.refs_0_) | copy-start | bytes 491524
  53.8 8.4 %copy-start.2 = (bf16[2,8,5120]{2,1,0:T(8,128)(2,1)S(1)}, bf16[2,8,5120]{2,1,0:T(8,128)(2,1)}, u32[]{:S(2)}) copy-start(bf16[2,8,5120]{2,1,0:T(8,128)(2,1)} %get-tuple-element.10.refs_8_) | copy-start | bytes 491524
  62.3 23.8 %copy-start.8 = (f32[384]{0:T(512)S(1)}, f32[384]{0:T(512)}, u32[]{:S(2)}) copy-start(f32[384]{0:T(512)} %param.12) | copy-start | bytes 4612
  62.3 54.5 %copy-start.10 = (s32[1,16]{1,0:T(1,128)S(1)}, s32[1,16]{1,0:T(1,128)}, u32[]{:S(2)}) copy-start(s32[1,16]{1,0:T(1,128)} %param.15) | copy-start | bytes 196
  71.7 54.3 %copy-start.3 = (bf16[2048,384]{1,0:T(8,128)(2,1)S(1)}, bf16[2048,384]{1,0:T(8,128)(2,1)}, u32[]{:S(2)}) copy-start(bf16[2048,384]{1,0:T(8,128)(2,1)} %param.8) | copy-start | bytes 4718596
  71.7 54.3 %copy-start.9 = (f32[384]{0:T(512)S(1)}, f32[384]{0:T(512)}, u32[]{:S(2)}) copy-start(f32[384]{0:T(512)} %param.11) | copy-start | bytes 4612
  71.9 2.5 %collective-permute-start.21 = (f32[4,64]{1,0:T(4,128)S(1)}, f32[4,64]{1,0:T(4,128)S(1)}, u32[]{:S(2)}, u32[]{:S(2)}) collective-permute-start(f32[4,64]{1,0:T(4,128)S(1)} %reduce_sum.32), channel_id=1, source_target_pairs={{0,32},{32,0},{64,96},{96,64},{128,160},{160,128},{192,224},{224,1... | collective-permute-start | bytes 3080 | tf_op jit(solution)/shard_map/ppermute | solution.py:216
  74.4 3.3 %collective-permute-start.22 = (f32[4,64]{1,0:T(4,128)S(1)}, f32[4,64]{1,0:T(4,128)S(1)}, u32[]{:S(2)}, u32[]{:S(2)}) collective-permute-start(f32[4,64]{1,0:T(4,128)S(1)} %add.100), channel_id=1, source_target_pairs={{0,64},{32,96},{64,0},{96,32},{128,192},{160,224},{192,128},{224,1... | collective-permute-start | bytes 3080 | tf_op jit(solution)/shard_map/ppermute | solution.py:216
  77.7 8.4 %collective-permute-start.23 = (f32[4,64]{1,0:T(4,128)S(1)}, f32[4,64]{1,0:T(4,128)S(1)}, u32[]{:S(2)}, u32[]{:S(2)}) collective-permute-start(f32[4,64]{1,0:T(4,128)S(1)} %add.101), channel_id=1, source_target_pairs={{0,128},{32,160},{64,192},{96,224},{128,0},{160,32},{192,64},{224,... | collective-permute-start | bytes 3080 | tf_op jit(solution)/shard_map/ppermute | solution.py:216
  83.4 26.4 %collective-permute-start.33 = (bf16[4,64,384]{2,1,0:T(8,128)(2,1)S(1)}, bf16[4,64,384]{2,1,0:T(8,128)(2,1)S(1)}, u32[]{:S(2)}, u32[]{:S(2)}) collective-permute-start(bf16[4,64,384]{2,1,0:T(8,128)(2,1)S(1)} %bitcast.14), channel_id=1, source_target_pairs={{0,2},{1,3},{2,4},{3,5},{4,6},{5,7},{6,0},{7,1},{8,10},{9,11},{10,... | collective-permute-start | bytes 589832 | tf_op jit(solution)/shard_map/ppermute | solution.py:206
  84.7 25.1 %collective-permute-start.34 = (bf16[4,64,384]{2,1,0:T(8,128)(2,1)S(1)}, bf16[4,64,384]{2,1,0:T(8,128)(2,1)S(1)}, u32[]{:S(2)}, u32[]{:S(2)}) collective-permute-start(bf16[4,64,384]{2,1,0:T(8,128)(2,1)S(1)} %bitcast.15), channel_id=1, source_target_pairs={{0,6},{1,7},{2,0},{3,1},{4,2},{5,3},{6,4},{7,5},{8,14},{9,15},{10,... | collective-permute-start | bytes 589832 | tf_op jit(solution)/shard_map/ppermute | solution.py:207
  86.3 27.5 %collective-permute-start.24 = (bf16[4,64,384]{2,1,0:T(8,128)(2,1)S(1)}, bf16[4,64,384]{2,1,0:T(8,128)(2,1)S(1)}, u32[]{:S(2)}, u32[]{:S(2)}) collective-permute-start(bf16[4,64,384]{2,1,0:T(8,128)(2,1)S(1)} %fusion.6.refs_0_), channel_id=1, source_target_pairs={{0,2},{1,3},{2,4},{3,5},{4,6},{5,7},{6,0},{7,1},{8,10},{9,11},{10,... | collective-permute-start | bytes 589832 | tf_op jit(solution)/shard_map/ppermute | solution.py:206
  86.4 27.8 %collective-permute-start.25 = (bf16[4,64,384]{2,1,0:T(8,128)(2,1)S(1)}, bf16[4,64,384]{2,1,0:T(8,128)(2,1)S(1)}, u32[]{:S(2)}, u32[]{:S(2)}) collective-permute-start(bf16[4,64,384]{2,1,0:T(8,128)(2,1)S(1)} %fusion.6.refs_0_), channel_id=1, source_target_pairs={{0,6},{1,7},{2,0},{3,1},{4,2},{5,3},{6,4},{7,5},{8,14},{9,15},{10,... | collective-permute-start | bytes 589832 | tf_op jit(solution)/shard_map/ppermute | solution.py:207
  90.8 2.9 %collective-permute-start = (f32[2048]{0:T(1024)S(1)}, f32[2048]{0:T(1024)S(1)}, u32[]{:S(2)}, u32[]{:S(2)}) collective-permute-start(f32[2048]{0:T(1024)S(1)} %fusion), channel_id=1, source_target_pairs={{0,32},{32,0},{64,96},{96,64},{128,160},{160,128},{192,224},{224,1... | collective-permute-start | bytes 24584 | tf_op jit(solution)/shard_map/ppermute | solution.py:216
  93.7 3.7 %collective-permute-start.1 = (f32[2048]{0:T(1024)S(1)}, f32[2048]{0:T(1024)S(1)}, u32[]{:S(2)}, u32[]{:S(2)}) collective-permute-start(f32[2048]{0:T(1024)S(1)} %add.87), channel_id=1, source_target_pairs={{0,64},{32,96},{64,0},{96,32},{128,192},{160,224},{192,128},{224,1... | collective-permute-start | bytes 24584 | tf_op jit(solution)/shard_map/ppermute | solution.py:216
  97.4 21.0 %collective-permute-start.37 = (bf16[4,64,384]{2,1,0:T(8,128)(2,1)S(1)}, bf16[4,64,384]{2,1,0:T(8,128)(2,1)S(1)}, u32[]{:S(2)}, u32[]{:S(2)}) collective-permute-start(bf16[4,64,384]{2,1,0:T(8,128)(2,1)S(1)} %bitcast.16), channel_id=1, source_target_pairs={{0,1},{1,0},{2,3},{3,2},{4,5},{5,4},{6,7},{7,6},{8,9},{9,8},{10,11... | collective-permute-start | bytes 589832 | tf_op jit(solution)/shard_map/ppermute | solution.py:211
  109.7 8.7 %collective-permute-start.28 = (bf16[4,64,384]{2,1,0:T(8,128)(2,1)S(1)}, bf16[4,64,384]{2,1,0:T(8,128)(2,1)S(1)}, u32[]{:S(2)}, u32[]{:S(2)}) collective-permute-start(bf16[4,64,384]{2,1,0:T(8,128)(2,1)S(1)} %fusion.6.refs_0_), channel_id=1, source_target_pairs={{0,1},{1,0},{2,3},{3,2},{4,5},{5,4},{6,7},{7,6},{8,9},{9,8},{10,11... | collective-permute-start | bytes 589832 | tf_op jit(solution)/shard_map/ppermute | solution.py:211
  109.8 7.1 %collective-permute-start.2 = (f32[2048]{0:T(1024)S(1)}, f32[2048]{0:T(1024)S(1)}, u32[]{:S(2)}, u32[]{:S(2)}) collective-permute-start(f32[2048]{0:T(1024)S(1)} %add.88), channel_id=1, source_target_pairs={{0,128},{32,160},{64,192},{96,224},{128,0},{160,32},{192,64},{224,... | collective-permute-start | bytes 24584 | tf_op jit(solution)/shard_map/ppermute | solution.py:216
  113.8 5.0 %collective-permute-start.35 = (bf16[2,64,384]{2,1,0:T(8,128)(2,1)S(1)}, bf16[2,64,384]{2,1,0:T(8,128)(2,1)S(1)}, u32[]{:S(2)}, u32[]{:S(2)}) collective-permute-start(bf16[2,64,384]{2,1,0:T(8,128)(2,1)S(1)} %slice.30), channel_id=1, source_target_pairs={{0,2},{1,3},{2,4},{3,5},{4,6},{5,7},{6,0},{7,1},{8,10},{9,11},{10,... | collective-permute-start | bytes 294920 | tf_op jit(solution)/shard_map/ppermute | solution.py:208
  114.2 7.0 %collective-permute-start.36 = (bf16[2,64,384]{2,1,0:T(8,128)(2,1)S(1)}, bf16[2,64,384]{2,1,0:T(8,128)(2,1)S(1)}, u32[]{:S(2)}, u32[]{:S(2)}) collective-permute-start(bf16[2,64,384]{2,1,0:T(8,128)(2,1)S(1)} %slice.31), channel_id=1, source_target_pairs={{0,6},{1,7},{2,0},{3,1},{4,2},{5,3},{6,4},{7,5},{8,14},{9,15},{10,... | collective-permute-start | bytes 294920 | tf_op jit(solution)/shard_map/ppermute | solution.py:209
  116.9 8.4 %collective-permute-start.38 = (bf16[4,64,384]{2,1,0:T(8,128)(2,1)S(1)}, bf16[4,64,384]{2,1,0:T(8,128)(2,1)S(1)}, u32[]{:S(2)}, u32[]{:S(2)}) collective-permute-start(bf16[4,64,384]{2,1,0:T(8,128)(2,1)S(1)} %collective-permute-done.33.refs_11_), channel_id=1, source_target_pairs={{0,1},{1,0},{2,3},{3,2},{4,5},{5,4},{6,7},{7,6},{8,9},{9,8},{10,11... | collective-permute-start | bytes 589832 | tf_op jit(solution)/shard_map/ppermute | solution.py:211
  118.4 7.1 %collective-permute-start.39 = (bf16[4,64,384]{2,1,0:T(8,128)(2,1)S(1)}, bf16[4,64,384]{2,1,0:T(8,128)(2,1)S(1)}, u32[]{:S(2)}, u32[]{:S(2)}) collective-permute-start(bf16[4,64,384]{2,1,0:T(8,128)(2,1)S(1)} %collective-permute-done.34.refs_12_), channel_id=1, source_target_pairs={{0,1},{1,0},{2,3},{3,2},{4,5},{5,4},{6,7},{7,6},{8,9},{9,8},{10,11... | collective-permute-start | bytes 589832 | tf_op jit(solution)/shard_map/ppermute | solution.py:211
  118.5 5.2 %collective-permute-start.26 = (bf16[2,64,384]{2,1,0:T(8,128)(2,1)S(1)}, bf16[2,64,384]{2,1,0:T(8,128)(2,1)S(1)}, u32[]{:S(2)}, u32[]{:S(2)}) collective-permute-start(bf16[2,64,384]{2,1,0:T(8,128)(2,1)S(1)} %slice.28), channel_id=1, source_target_pairs={{0,2},{1,3},{2,4},{3,5},{4,6},{5,7},{6,0},{7,1},{8,10},{9,11},{10,... | collective-permute-start | bytes 294920 | tf_op jit(solution)/shard_map/ppermute | solution.py:208
  118.8 6.1 %collective-permute-start.27 = (bf16[2,64,384]{2,1,0:T(8,128)(2,1)S(1)}, bf16[2,64,384]{2,1,0:T(8,128)(2,1)S(1)}, u32[]{:S(2)}, u32[]{:S(2)}) collective-permute-start(bf16[2,64,384]{2,1,0:T(8,128)(2,1)S(1)} %slice.29), channel_id=1, source_target_pairs={{0,6},{1,7},{2,0},{3,1},{4,2},{5,3},{6,4},{7,5},{8,14},{9,15},{10,... | collective-permute-start | bytes 294920 | tf_op jit(solution)/shard_map/ppermute | solution.py:209
  121.2 4.7 %collective-permute-start.40 = (bf16[2,64,384]{2,1,0:T(8,128)(2,1)S(1)}, bf16[2,64,384]{2,1,0:T(8,128)(2,1)S(1)}, u32[]{:S(2)}, u32[]{:S(2)}) collective-permute-start(bf16[2,64,384]{2,1,0:T(8,128)(2,1)S(1)} %collective-permute-done.35.refs_13_), channel_id=1, source_target_pairs={{0,1},{1,0},{2,3},{3,2},{4,5},{5,4},{6,7},{7,6},{8,9},{9,8},{10,11... | collective-permute-start | bytes 294920 | tf_op jit(solution)/shard_map/ppermute | solution.py:211
  123.7 3.0 %collective-permute-start.29 = (bf16[4,64,384]{2,1,0:T(8,128)(2,1)S(1)}, bf16[4,64,384]{2,1,0:T(8,128)(2,1)S(1)}, u32[]{:S(2)}, u32[]{:S(2)}) collective-permute-start(bf16[4,64,384]{2,1,0:T(8,128)(2,1)S(1)} %collective-permute-done.24.refs_1_), channel_id=1, source_target_pairs={{0,1},{1,0},{2,3},{3,2},{4,5},{5,4},{6,7},{7,6},{8,9},{9,8},{10,11... | collective-permute-start | bytes 589832 | tf_op jit(solution)/shard_map/ppermute | solution.py:211
  124.9 1.7 %collective-permute-start.30 = (bf16[4,64,384]{2,1,0:T(8,128)(2,1)S(1)}, bf16[4,64,384]{2,1,0:T(8,128)(2,1)S(1)}, u32[]{:S(2)}, u32[]{:S(2)}) collective-permute-start(bf16[4,64,384]{2,1,0:T(8,128)(2,1)S(1)} %collective-permute-done.25.refs_2_), channel_id=1, source_target_pairs={{0,1},{1,0},{2,3},{3,2},{4,5},{5,4},{6,7},{7,6},{8,9},{9,8},{10,11... | collective-permute-start | bytes 589832 | tf_op jit(solution)/shard_map/ppermute | solution.py:211
  125.3 1.3 collective-permute-start.41
  125.4 1.4 collective-permute-start.31
  125.8 1.3 collective-permute-start.32

commit v2 on v0

v2 whole, which is shorter than its diff:
```python
import functools
import math

import jax
import jax.numpy as jnp
from jax import lax
from jax.experimental import pallas as pl
from jax.experimental.pallas import tpu as pltpu
from jax.sharding import PartitionSpec as P

HD = 128
FRAME = 128
V_DOWN = 2.0 ** -12
MIB = 1024 * 1024
CHUNK = 512
GROUP = 4
PLANES = (0, -1, -2, -3, 4, 1, 2, 3)

SMEM = pl.BlockSpec(memory_space=pltpu.SMEM)
VMEM = pl.BlockSpec(memory_space=pltpu.VMEM)
HBM = pl.BlockSpec(memory_space=pl.ANY)


def ring(n, k):
    return [(i, (i + k) % n) for i in range(n)]


Y_UP = [(s, (s + 2) % 8) for s in range(8)]
Y_DOWN = [(s, (s - 2) % 8) for s in range(8)]
CORE = [(s, s ^ 1) for s in range(8)]


def pick_kernel(code, text, ahead, behind, far_a, far_b, *refs):
    out, sem = refs[-2:]
    rows, width = text.shape[1:]
    copies = []
    for j in range(out.shape[0]):
        target = out.at[j] if out.shape[2] == width else out.at[j, :, pl.ds(0, width)]
        shift, slot = code[j] // 4, code[j] % 4

        def send(source, index, target=target, j=j):
            pltpu.make_async_copy(source.at[index], target, sem.at[j]).start()

        pl.when(shift == 0)(functools.partial(send, text, slot))
        pl.when(shift == 1)(functools.partial(send, behind, slot))
        pl.when((shift == 2) & (slot < 2))(functools.partial(send, far_a, slot % 2))
        pl.when((shift == 2) & (slot >= 2))(functools.partial(send, far_b, slot % 2))
        pl.when(shift == 3)(functools.partial(send, ahead, slot))
        copies.append(pltpu.make_async_copy(text.at[0], target, sem.at[j]))
    if out.shape[2] > width:
        square = refs[0]
        for j in range(2):
            part = square[j * rows:(j + 1) * rows, :]
            upper = part.astype(out.dtype)
            out[j, :, width:] = upper
            out[2 + j, :, width:] = (part - upper.astype(jnp.float32)).astype(out.dtype)
    for copy in copies:
        copy.wait()


def pick(code, text, ahead, behind, far_a, far_b, square=None, *first):
    extra = 0 if square is None else HD
    first = first if square is None else (square,) + first
    n, rows, width = text.shape
    return pl.pallas_call(
        pick_kernel,
        out_shape=jax.ShapeDtypeStruct((n, rows, width + extra), text.dtype),
        in_specs=[SMEM] + [HBM] * 5 + [VMEM] * (extra // HD) + [HBM] * (len(first) - extra // HD),
        out_specs=VMEM,
        scratch_shapes=[pltpu.SemaphoreType.DMA((text.shape[0],))],
        compiler_params=pltpu.CompilerParams(vmem_limit_bytes=4 * MIB),
        name="pick",
    )(code, text, ahead, behind, far_a, far_b, *first)


def project_kernel(info, gain, *refs):
    n = len(PLANES)
    halves, weight = (refs[:n], refs[n:2 * n]), refs[2 * n]
    out, squares, query_total, row_buf, weight_buf, total, raw, row_sem, weight_sem = refs[-9:]
    width = weight.shape[0] // 2
    steps = [(half, k) for half in range(2) for k in range(0, width, CHUNK)]
    loads = [
        pltpu.make_async_copy(weight.at[pl.ds(half * width + k, CHUNK)], weight_buf.at[i], weight_sem.at[i])
        for i, (half, k) in enumerate(steps)
    ]
    fetches = [
        [
            pltpu.make_async_copy(
                block, row_buf.at[half, pl.ds(32 * i, 32), pl.ds(0, block.shape[1])], row_sem.at[half, i]
            )
            for i, block in enumerate(blocks)
        ]
        for half, blocks in enumerate(halves)
    ]
    for copy in fetches[0] + loads[:2] + fetches[1] + loads[2:]:
        copy.start()
    for i, (half, k) in enumerate(steps):
        if k == 0:
            for fetch in fetches[half]:
                fetch.wait()
        loads[i].wait()
        part = jnp.dot(row_buf[half, :, k:k + CHUNK], weight_buf[i], preferred_element_type=jnp.float32)
        if i == 0:
            total[...] = part
        else:
            total[...] += part
    riders = [row_buf[1, 32 * i:32 * i + 32, width:].astype(jnp.float32) for i in range(n)]
    query_total[...] = sum(rider[:16] + rider[16:] for rider in riders)
    columns = out.shape[-1] // 2
    enc, seq = info[0], info[1]
    place = lax.broadcasted_iota(jnp.int32, (8, columns), 0)
    for i, offset in enumerate(PLANES):
        plane = lax.rem(enc + offset + 8, 8)
        for t in range(4):
            both = total[32 * i + 8 * t:32 * i + 8 * t + 8, :]
            live = plane * 64 + seq * 8 + place < info[2 + t]
            raw[t, plane] = both[:, :columns]
            out[t, plane, :, :columns] = (both[:, :columns] * gain[...]).astype(out.dtype)
            out[t, plane, :, columns:] = jnp.where(
                live, both[:, columns:] * V_DOWN, 0.0
            ).astype(out.dtype)
    square = raw[...].reshape(256, columns)
    square = square * square
    upper = square.astype(jnp.bfloat16)
    lower = (square - upper.astype(jnp.float32)).astype(jnp.bfloat16)
    ones = jnp.ones((squares.shape[0], columns), jnp.bfloat16)
    across = (((1,), (1,)), ((), ()))
    squares[...] = lax.dot_general(
        ones, upper, across, preferred_element_type=jnp.float32
    ) + lax.dot_general(ones, lower, across, preferred_element_type=jnp.float32)


def project(info, gain, blocks, weight):
    width, both = weight.shape
    return pl.pallas_call(
        project_kernel,
        out_shape=(
            jax.ShapeDtypeStruct((4, 8, 8, both), jnp.bfloat16),
            jax.ShapeDtypeStruct((64, 256), jnp.float32),
            jax.ShapeDtypeStruct((16, HD), jnp.float32),
        ),
        in_specs=[SMEM, VMEM] + [HBM] * (len(blocks) + 1),
        out_specs=[VMEM] * 3,
        scratch_shapes=[
            pltpu.VMEM((2, 256, width // 2 + HD), jnp.bfloat16),
            pltpu.VMEM((width // CHUNK, CHUNK, both), jnp.bfloat16),
            pltpu.VMEM((256, both), jnp.float32),
            pltpu.VMEM((4, 8, 8, both // 2), jnp.float32),
            pltpu.SemaphoreType.DMA((2, len(PLANES))),
            pltpu.SemaphoreType.DMA((width // CHUNK,)),
        ],
        compiler_params=pltpu.CompilerParams(vmem_limit_bytes=56 * MIB),
        cost_estimate=pl.CostEstimate(
            flops=2 * 256 * width * both, bytes_accessed=2 * (256 * width + width * both), transcendentals=0
        ),
        name="project",
    )(info, gain, *blocks, weight)


def cut_kernel(ahead, behind, squares, out_a, out_b, total, sem):
    count = out_a.shape[0]
    copies = [
        pltpu.make_async_copy(ahead.at[pl.ds(0, count)], out_a, sem.at[0]),
        pltpu.make_async_copy(behind.at[pl.ds(count, count)], out_b, sem.at[1]),
    ]
    for copy in copies:
        copy.start()
    total[...] = jnp.sum(squares[...].reshape(8, 8, 256), axis=0)
    for copy in copies:
        copy.wait()


def cut(ahead, behind, squares):
    n, rows, columns = ahead.shape
    half = jax.ShapeDtypeStruct((n // 2, rows, columns), ahead.dtype)
    return pl.pallas_call(
        cut_kernel,
        out_shape=(half, half, jax.ShapeDtypeStruct((8, 256), jnp.float32)),
        in_specs=[HBM, HBM, VMEM],
        out_specs=[VMEM] * 3,
        scratch_shapes=[pltpu.SemaphoreType.DMA((2,))],
        compiler_params=pltpu.CompilerParams(vmem_limit_bytes=4 * MIB),
        name="cut",
    )(ahead, behind, squares)


def attend_kernel(width, info, bounds, queries, gain, query_total, key_total, *refs):
    parts, out = refs[:10], refs[10]
    raw_buf, q_buf, o_buf, k_buf, v_buf, scale_buf, sem, query_sem = refs[11:]
    seq, heads = info[1], queries.shape[1] // HD
    columns = heads * HD
    frames = queries.shape[0] // FRAME
    load = pltpu.make_async_copy(queries, raw_buf, query_sem)
    load.start()

    def piece_seq(piece):
        y, c = seq // 2, seq % 2
        kind = piece % 4
        shift = jnp.where(kind == 0, 0, jnp.where(kind == 1, 3, jnp.where(kind == 2, 1, 2)))
        return 2 * ((y + shift) % 4) + (c + piece // 4) % 2

    def position(shape, axis):
        key = lax.broadcasted_iota(jnp.int32, shape, axis)
        return key // 8 % 8 * 64 + piece_seq(key // 64) * 8 + key % 8

    down, across = position((512, HD), 0), position((1, 512), 1)
    totals = [key_total[pl.ds(piece_seq(p), 1), :] for p in range(8)]
    scales = [lax.rsqrt(total / width + 1e-06) * math.log2(math.e) for total in totals]
    for t in range(4):
        live = jnp.where(down < info[2 + t], 1.0, 0.0).astype(v_buf.dtype)
        row = jnp.concatenate([scale[:, t * 64:t * 64 + 64] for scale in scales], axis=1)
        scale_buf[t:t + 1, :] = jnp.where(across < info[2 + t], row, 0.0)
        for p in range(8):
            own = parts[p // 4 * 5 + p % 4]
            piece, slot = (own, t) if p % 4 < 3 else (parts[p // 4 * 5 + 3 + t // 2], t % 2)
            spot = slice(64 * p, 64 * p + 64)
            k_buf[t, spot, :] = piece[slot, :, :columns]
            for h in range(heads):
                v_buf[h, t, spot, :HD] = piece[slot, :, columns + h * HD:columns + (h + 1) * HD]
        for h in range(heads):
            v_buf[h, t, :, HD:] = live

    query_scale = jnp.transpose(lax.rsqrt(query_total[...] / width + 1e-06))
    load.wait()
    for f in range(frames):
        rows = slice(f * FRAME, (f + 1) * FRAME)
        q_buf[rows, :] = (
            raw_buf[rows, :].astype(jnp.float32) * query_scale[:, f:f + 1] * gain[...] * HD ** (-0.5)
        ).astype(q_buf.dtype)

    def frame_copy(f):
        rows = pl.ds(pl.multiple_of(f * FRAME, FRAME), FRAME)
        return pltpu.make_async_copy(o_buf.at[rows], out.at[rows], sem.at[f])

    for t in range(4):
        first, last = bounds[t], bounds[t + 1]

        def one(i, carry, t=t, first=first, last=last):
            frame = first + GROUP * i
            base = jnp.minimum(frame, frames - GROUP)
            rows = pl.ds(pl.multiple_of(base * FRAME, FRAME), GROUP * FRAME)
            places = [
                pl.ds(pl.multiple_of(jnp.where(base + g < frame, frames, base + g) * FRAME, FRAME), FRAME)
                for g in range(GROUP)
            ]
            for h in range(heads):
                lanes = slice(h * HD, (h + 1) * HD)
                scores = lax.dot_general(
                    q_buf[rows, lanes], k_buf[t, :, lanes], (((1,), (1,)), ((), ())),
                    preferred_element_type=jnp.float32,
                )
                raised = jnp.exp2(scores * scale_buf[t:t + 1, :]).astype(jnp.bfloat16)
                mixed = jnp.dot(raised, v_buf[h, t], preferred_element_type=jnp.float32)
                result = (mixed[:, :HD] * (1.0 / mixed[:, HD:]) * (1.0 / V_DOWN)).astype(o_buf.dtype)
                for g, place in enumerate(places):
                    o_buf[place, lanes] = result[g * FRAME:(g + 1) * FRAME]
            for g in range(GROUP):

                @pl.when(frame + g < last)
                def _(g=g):
                    frame_copy(frame + g).start()

            return carry

        lax.fori_loop(0, (last - first + GROUP - 1) // GROUP, one, 0)
    for f in range(frames):
        frame_copy(f).wait()


def attend(width, info, bounds, queries, gain, query_total, key_total, parts):
    rows, columns = queries.shape
    return pl.pallas_call(
        functools.partial(attend_kernel, width),
        out_shape=jax.ShapeDtypeStruct((rows, columns), queries.dtype),
        in_specs=[SMEM, SMEM, HBM] + [VMEM] * 13,
        out_specs=HBM,
        scratch_shapes=[
            pltpu.VMEM((rows, columns), queries.dtype),
            pltpu.VMEM((rows, columns), queries.dtype),
            pltpu.VMEM((rows + FRAME, columns), queries.dtype),
            pltpu.VMEM((4, 512, columns), queries.dtype),
            pltpu.VMEM((columns // HD, 4, 512, 2 * HD), queries.dtype),
            pltpu.VMEM((8, 512), jnp.float32),
            pltpu.SemaphoreType.DMA((rows // FRAME,)),
            pltpu.SemaphoreType.DMA,
        ],
        compiler_params=pltpu.CompilerParams(vmem_limit_bytes=20 * MIB),
        cost_estimate=pl.CostEstimate(flops=4 * rows * columns * 512, bytes_accessed=4 * rows * columns, transcendentals=0),
        name="attend",
    )(info, bounds, queries, gain, query_total, key_total, *parts)


def local(queries, text, kv_weight, query_gain, key_gain, prompt_len, served, frame_slot):
    columns = queries.shape[1]
    full_width = columns * 8
    enc, rep, seq = (lax.axis_index(a) for a in ("enc", "rep", "seq"))
    mine = lax.dynamic_slice_in_dim(served, rep * 4, 4)
    code = (mine // 4 - rep + 4) % 4 * 4 + mine % 4
    info = jnp.concatenate([jnp.stack([enc, seq]).astype(jnp.int32), prompt_len[mine]])
    bounds = jnp.sum(frame_slot.reshape(1, -1) < jnp.arange(5, dtype=jnp.int32)[:, None], axis=1, dtype=jnp.int32)
    query_float = queries.astype(jnp.float32)
    query_square = jnp.sum(query_float * query_float, axis=-1).reshape(-1, HD)
    half = text.shape[2] // 2
    weight = kv_weight.reshape(kv_weight.shape[0], 2 * columns)

    blocks = []
    for n in range(2):
        part = text[:, :, n * half:(n + 1) * half]
        ahead = lax.ppermute(part, "rep", ring(4, 1))
        behind = lax.ppermute(part, "rep", ring(4, -1))
        far_a = lax.ppermute(ahead[:2], "rep", ring(4, 1))
        far_b = lax.ppermute(behind[2:], "rep", ring(4, -1))
        first = (query_square,) if n == 1 else ()
        picked = pick(code, part, ahead, behind, far_a, far_b, *first)
        blocks.append(picked.reshape(32, picked.shape[2]))

    ups, downs = [[b] for b in blocks], [[b] for b in blocks]
    for i in range(4):
        for n in range(2):
            if n == 0 or i < 3:
                ups[n].append(lax.ppermute(ups[n][-1], "enc", ring(8, 1)))
            if n == 1 or i < 3:
                downs[n].append(lax.ppermute(downs[n][-1], "enc", ring(8, -1)))
    held = ups[0] + downs[0][1:] + ups[1] + [downs[1][4]] + downs[1][1:4]
    pair, squares, query_total = project(info, key_gain[None], held, weight)
    pair = pair.reshape(4, 64, 2 * columns)

    ahead = lax.ppermute(pair, "seq", Y_UP)
    behind = lax.ppermute(pair, "seq", Y_DOWN)
    squares = lax.all_to_all(squares, ("enc", "seq"), 0, 0, tiled=True)
    cut_a, cut_b, key_total = cut(ahead, behind, squares)
    far_a = lax.ppermute(cut_a, "seq", Y_UP)
    far_b = lax.ppermute(cut_b, "seq", Y_DOWN)
    parts = [pair, ahead, behind, far_a, far_b]
    parts = parts + [lax.ppermute(part, "seq", CORE) for part in parts]
    return attend(full_width, info, bounds, queries, query_gain[None], query_total, key_total, parts)


def solution(mesh):
    placed = (
        P(("rep", "seq"), "enc"),
        P("rep", ("enc", "seq"), None),
        P(None, None, "enc"),
        P("enc"),
        P("enc"),
        P(),
        P(),
        P("rep", "seq"),
    )
    return jax.shard_map(
        local, mesh=mesh, in_specs=placed, out_specs=P(("rep", "seq"), "enc"), check_vma=False
    )
```

time: 260 us -> 114 us (0.44)
  waiting for transfers between devices: 101 us -> 22.8 us
  local copies, waits for them, and re-layouts: 76.6 us -> 14.6 us
  starting transfers between devices: 0.04 us -> 54.7 us
  matrix products: 29.8 us -> 0 us
  blocking collectives: 21.3 us -> 0 us
  Pallas kernels: 0 us -> 17.4 us
  between operations: 13.5 us -> 0.6 us
  other arithmetic: 15.8 us -> 3.22 us
    all_gather x2 -> x0, waiting for transfers between devices: 100 us -> none  [the longest x1 73.8 us: local(): everything = lax.all_gather(local_pairs, ('rep', 'seq'), axis=0, tiled=True)]
    ppermute x0 -> x31, starting transfers between devices: none -> 40.2 us  [the longest x7 19.1 us: local(): downs[n].append(lax.ppermute(downs[n][-1], 'enc', ring(8, -1)))]
    dot_general x9 -> x0, matrix products: 29.8 us -> none  [the longest x4 12.6 us: attend(): jnp.einsum('gqhd,gkhd->ghqk', scaled, keys_block, preferred_element_type=...]
    gather x11 -> x1, local copies, waits for them, and re-layouts: 23.6 us -> 0.64 us  [local(): prompt_len[mine]]
    psum x1 -> x0, blocking collectives: 21.3 us -> none  [local(): query_total, key_total = lax.psum((query_square, key_square), 'enc')]
    pallas_call x0 -> x5, Pallas kernels: none -> 17.4 us  [the longest x1 7.54 us: attend(): pl.pallas_call(functools.partial(attend_kernel, width), out_shape=jax.Sha...]
    slice x13 -> x5, local copies, waits for them, and re-layouts: 17.8 us -> 1.06 us  [the longest x1 1.03 us: local(): part = text[:, :, n * half:(n + 1) * half]]
    all_to_all x0 -> x1, starting transfers between devices: none -> 14.5 us  [local(): squares = lax.all_to_all(squares, ('enc', 'seq'), 0, 0, tiled=True)]
  transfers between devices with their start and end apart: 2 -> 32, of which waited for: 2 -> 9; matrix products, arithmetic and copies ran while one was open for 9% -> 12% of each run, Pallas kernels for 0% -> 2%
where the time goes in v2:
time: 114 us; the launch traced here: 113 us
  starting transfers between devices  54.7 us (48%)
  waiting for transfers between devices  22.8 us (20%)
  Pallas kernels  17.4 us (15%)
  local copies, waits for them, and re-layouts  14.6 us (13%)
  other arithmetic  3.22 us (3%)
    ppermute x7, starting transfers between devices, local(): downs[n].append(lax.ppermute(downs[n][-1], 'enc', ring(8, -1)))  19.1 us
    all_to_all x1, starting transfers between devices, local(): squares = lax.all_to_all(squares, ('enc', 'seq'), 0, 0, tiled=True)  14.5 us
    unnamed x50, local copies, waits for them, and re-layouts  10.8 us
    all_to_all x1, waiting for transfers between devices, local(): squares = lax.all_to_all(squares, ('enc', 'seq'), 0, 0, tiled=True)  9.33 us
    pallas_call x1, Pallas kernels, attend(): pl.pallas_call(functools.partial(attend_kernel, width), out_shape=jax.Sha...  7.54 us
    pallas_call x1, Pallas kernels, project(): pl.pallas_call(project_kernel, out_shape=(jax.ShapeDtypeStruct((4, 8, 8,...  7.4 us
    ppermute x2, starting transfers between devices, local(): far_b = lax.ppermute(behind[2:], 'rep', ring(4, -1))  5.45 us
    ppermute x7, waiting for transfers between devices, local(): downs[n].append(lax.ppermute(downs[n][-1], 'enc', ring(8, -1)))  5.01 us
  transfers between devices with their start and end apart: 32, of which 9 were waited for; matrix products, arithmetic and copies ran while one was open for 12% of the time, Pallas kernels for 2%

profile of v2, /device:TPU:1, one launch (start us, length us, event | category | flops | bytes accessed | tf_op | source)
XLA Modules:
  0.0 113.2 jit_solution(2752312015580547706)
XLA Ops:
  0.0 1.0 fusion.3
  1.0 2.1 %collective-permute-start.11 = (bf16[4,8,2560]{2,1,0:T(8,128)(2,1)S(1)}, bf16[4,8,2560]{2,1,0:T(8,128)(2,1)S(1)}, u32[]{:S(2)}, u32[]{:S(2)}) collective-permute-start(bf16[4,8,2560]{2,1,0:T(8,128)(2,1)S(1)} %get-tuple-element.17.text), channel_id=1, source_target_pairs={{0,8},{8,16},{16,24},{24,0},{1,9},{9,17},{17,25},{25,1},{2,10},{10... | collective-permute-start | bytes 491528 | tf_op jit(solution)/shard_map/ppermute | solution.py:309
  3.2 1.4 %collective-permute-start.12 = (bf16[4,8,2560]{2,1,0:T(8,128)(2,1)S(1)}, bf16[4,8,2560]{2,1,0:T(8,128)(2,1)S(1)}, u32[]{:S(2)}, u32[]{:S(2)}) collective-permute-start(bf16[4,8,2560]{2,1,0:T(8,128)(2,1)S(1)} %get-tuple-element.17.text), channel_id=1, source_target_pairs={{0,24},{8,0},{16,8},{24,16},{1,25},{9,1},{17,9},{25,17},{2,26},{10... | collective-permute-start | bytes 491528 | tf_op jit(solution)/shard_map/ppermute | solution.py:310
  4.5 0.1 collective-permute-start
  4.6 2.6 %collective-permute-start.1 = (bf16[4,8,2560]{2,1,0:T(8,128)(2,1)S(1)}, bf16[4,8,2560]{2,1,0:T(8,128)(2,1)S(1)}, u32[]{:S(2)}, u32[]{:S(2)}) collective-permute-start(bf16[4,8,2560]{2,1,0:T(8,128)(2,1)S(1)} %get-tuple-element.18.text), channel_id=1, source_target_pairs={{0,24},{8,0},{16,8},{24,16},{1,25},{9,1},{17,9},{25,17},{2,26},{10... | collective-permute-start | bytes 491528 | tf_op jit(solution)/shard_map/ppermute | solution.py:310
  7.2 1.8 %multiply_reduce_fusion = f32[2048]{0:T(1024)S(1)} fusion(bf16[2048,384]{1,0:T(8,128)(2,1)} %queries.1), kind=kLoop, calls=%fused_computation.1 | loop fusion | flops 2357248 | bytes 1581056 | tf_op jit(solution)/shard_map/reduce_sum | solution.py:302
  9.0 0.1 collective-permute-start.13
  9.1 2.7 %collective-permute-start.14 = (bf16[2,8,2560]{2,1,0:T(8,128)(2,1)S(1)}, bf16[2,8,2560]{2,1,0:T(8,128)(2,1)S(1)}, u32[]{:S(2)}, u32[]{:S(2)}) collective-permute-start(bf16[2,8,2560]{2,1,0:T(8,128)(2,1)S(1)} %slice.29), channel_id=1, source_target_pairs={{0,24},{8,0},{16,8},{24,16},{1,25},{9,1},{17,9},{25,17},{2,26},{10... | collective-permute-start | bytes 245768 | tf_op jit(solution)/shard_map/ppermute | solution.py:312
  11.9 0.0 collective-permute-done.ahead
  11.9 0.1 collective-permute-start.2
  12.0 0.0 collective-permute-done.1.behind
  12.0 2.7 %collective-permute-start.3 = (bf16[2,8,2560]{2,1,0:T(8,128)(2,1)S(1)}, bf16[2,8,2560]{2,1,0:T(8,128)(2,1)S(1)}, u32[]{:S(2)}, u32[]{:S(2)}) collective-permute-start(bf16[2,8,2560]{2,1,0:T(8,128)(2,1)S(1)} %slice.27), channel_id=1, source_target_pairs={{0,24},{8,0},{16,8},{24,16},{1,25},{9,1},{17,9},{25,17},{2,26},{10... | collective-permute-start | bytes 245768 | tf_op jit(solution)/shard_map/ppermute | solution.py:312
  14.7 0.7 fusion
  15.5 0.0 collective-permute-done.13.far_a
  15.5 0.9 pick.3
  16.4 5.8 %collective-permute-start.18 = (bf16[32,2688]{1,0:T(8,128)(2,1)S(1)}, bf16[32,2688]{1,0:T(8,128)(2,1)S(1)}, u32[]{:S(2)}, u32[]{:S(2)}) collective-permute-start(bf16[32,2688]{1,0:T(8,128)(2,1)S(1)} %bitcast.13), channel_id=1, source_target_pairs={{0,224},{32,0},{64,32},{96,64},{128,96},{160,128},{192,160},{224,1... | collective-permute-start | bytes 516104 | tf_op jit(solution)/shard_map/ppermute | solution.py:323
  22.2 0.0 collective-permute-done.2.far_a
  22.2 0.0 collective-permute-done.3.far_b
  22.2 0.9 pick.2
  23.1 0.1 collective-permute-start.4
  23.2 0.1 collective-permute-start.15
  23.3 1.2 %collective-permute-done.18.refs_13_ = bf16[32,2688]{1,0:T(8,128)(2,1)S(1)} collective-permute-done((bf16[32,2688]{1,0:T(8,128)(2,1)S(1)}, bf16[32,2688]{1,0:T(8,128)(2,1)S(1)}, u32[]{:S(2)}, u32[]{:S(2)}) %collective-permute-start.18) | collective-permute-done | bytes 172064 | tf_op jit(solution)/shard_map/ppermute | solution.py:323
  24.5 3.1 %collective-permute-start.19 = (bf16[32,2688]{1,0:T(8,128)(2,1)S(1)}, bf16[32,2688]{1,0:T(8,128)(2,1)S(1)}, u32[]{:S(2)}, u32[]{:S(2)}) collective-permute-start(bf16[32,2688]{1,0:T(8,128)(2,1)S(1)} %collective-permute-done.18.refs_13_), channel_id=1, source_target_pairs={{0,224},{32,0},{64,32},{96,64},{128,96},{160,128},{192,160},{224,1... | collective-permute-start | bytes 516104 | tf_op jit(solution)/shard_map/ppermute | solution.py:323
  27.7 0.0 collective-permute-start.8
  27.7 0.9 collective-permute-done.4.refs_1_
  28.6 0.5 collective-permute-start.5
  29.1 1.3 %collective-permute-done.15.refs_9_ = bf16[32,2688]{1,0:T(8,128)(2,1)S(1)} collective-permute-done((bf16[32,2688]{1,0:T(8,128)(2,1)S(1)}, bf16[32,2688]{1,0:T(8,128)(2,1)S(1)}, u32[]{:S(2)}, u32[]{:S(2)}) %collective-permute-start.15) | collective-permute-done | bytes 172064 | tf_op jit(solution)/shard_map/ppermute | solution.py:321
  30.5 0.0 collective-permute-start.16
  30.5 2.7 %collective-permute-start.20 = (bf16[32,2688]{1,0:T(8,128)(2,1)S(1)}, bf16[32,2688]{1,0:T(8,128)(2,1)S(1)}, u32[]{:S(2)}, u32[]{:S(2)}) collective-permute-start(bf16[32,2688]{1,0:T(8,128)(2,1)S(1)} %collective-permute-done.19.refs_14_), channel_id=1, source_target_pairs={{0,224},{32,0},{64,32},{96,64},{128,96},{160,128},{192,160},{224,1... | collective-permute-start | bytes 516104 | tf_op jit(solution)/shard_map/ppermute | solution.py:323
  33.1 1.7 %collective-permute-start.9 = (bf16[32,2560]{1,0:T(8,128)(2,1)S(1)}, bf16[32,2560]{1,0:T(8,128)(2,1)S(1)}, u32[]{:S(2)}, u32[]{:S(2)}) collective-permute-start(bf16[32,2560]{1,0:T(8,128)(2,1)S(1)} %collective-permute-done.8.refs_5_), channel_id=1, source_target_pairs={{0,224},{32,0},{64,32},{96,64},{128,96},{160,128},{192,160},{224,1... | collective-permute-start | bytes 491528 | tf_op jit(solution)/shard_map/ppermute | solution.py:323
  34.9 1.2 %collective-permute-done.5.refs_2_ = bf16[32,2560]{1,0:T(8,128)(2,1)S(1)} collective-permute-done((bf16[32,2560]{1,0:T(8,128)(2,1)S(1)}, bf16[32,2560]{1,0:T(8,128)(2,1)S(1)}, u32[]{:S(2)}, u32[]{:S(2)}) %collective-permute-start.5) | collective-permute-done | bytes 163872 | tf_op jit(solution)/shard_map/ppermute | solution.py:321
  36.1 3.8 %collective-permute-done.9.refs_6_ = bf16[32,2560]{1,0:T(8,128)(2,1)S(1)} collective-permute-done((bf16[32,2560]{1,0:T(8,128)(2,1)S(1)}, bf16[32,2560]{1,0:T(8,128)(2,1)S(1)}, u32[]{:S(2)}, u32[]{:S(2)}) %collective-permute-start.9) | collective-permute-done | bytes 163872 | tf_op jit(solution)/shard_map/ppermute | solution.py:323
  39.9 3.1 %collective-permute-start.10 = (bf16[32,2560]{1,0:T(8,128)(2,1)S(1)}, bf16[32,2560]{1,0:T(8,128)(2,1)S(1)}, u32[]{:S(2)}, u32[]{:S(2)}) collective-permute-start(bf16[32,2560]{1,0:T(8,128)(2,1)S(1)} %collective-permute-done.9.refs_6_), channel_id=1, source_target_pairs={{0,224},{32,0},{64,32},{96,64},{128,96},{160,128},{192,160},{224,1... | collective-permute-start | bytes 491528 | tf_op jit(solution)/shard_map/ppermute | solution.py:323
  43.0 0.1 collective-permute-start.7
  43.2 2.6 %collective-permute-start.21 = (bf16[32,2688]{1,0:T(8,128)(2,1)S(1)}, bf16[32,2688]{1,0:T(8,128)(2,1)S(1)}, u32[]{:S(2)}, u32[]{:S(2)}) collective-permute-start(bf16[32,2688]{1,0:T(8,128)(2,1)S(1)} %collective-permute-done.20.refs_15_), channel_id=1, source_target_pairs={{0,224},{32,0},{64,32},{96,64},{128,96},{160,128},{192,160},{224,1... | collective-permute-start | bytes 516104 | tf_op jit(solution)/shard_map/ppermute | solution.py:323
  45.8 7.7 %copy.12 = bf16[640,8,2,384]{3,1,2,0:T(8,128)(2,1)} copy(bf16[640,8,2,384]{3,2,1,0:T(2,128)(2,1)} %bitcast.26) | data formatting | bytes 15728640
  53.6 0.6 broadcast_in_dim.12.gain
  54.2 0.6 gather_fusion
  54.8 0.6 pad_add_fusion.info
  55.4 0.6 copy-done.19
  56.0 0.1 copy-done.20
  56.1 0.0 copy-done.12
  56.2 0.6 copy-done.13
  56.8 7.4 %project.1 = (bf16[4,8,8,768]{3,2,1,0:T(8,128)(2,1)}, f32[64,256]{1,0:T(8,128)}, f32[16,128]{1,0:T(8,128)}) custom-call(s32[6]{0:T(128)} %pad_add_fusion.info, f32[1,384]{1,0:T(1,128)} %broadcast_in_dim.12.gain, bf16[32,2560]{1,0:T(8,128)(2,1)} %bitcast.18, bf16[32,2560]{1,0:T(8,128)(2,1)} %copy-done.14, bf16[32,2560]{1,0:T(8,128)(2,1)} %copy-done.16, ...), custom_call_target="tpu_custom_call" | custom-call | flops 2013265920 | bytes 10485760 | tf_op jit(solution)/shard_map/project/pallas_call | solution.py:135
  64.2 1.4 %collective-permute-start.22 = (bf16[4,64,768]{2,1,0:T(8,128)(2,1)}, bf16[4,64,768]{2,1,0:T(8,128)(2,1)S(1)}, u32[]{:S(2)}, u32[]{:S(2)}) collective-permute-start(bf16[4,64,768]{2,1,0:T(8,128)(2,1)} %bitcast.19), channel_id=1, source_target_pairs={{0,2},{1,3},{2,4},{3,5},{4,6},{5,7},{6,0},{7,1},{8,10},{9,11},{10,... | collective-permute-start | bytes 1179656 | tf_op jit(solution)/shard_map/ppermute | solution.py:328
  65.6 1.5 %collective-permute-start.23 = (bf16[4,64,768]{2,1,0:T(8,128)(2,1)}, bf16[4,64,768]{2,1,0:T(8,128)(2,1)S(1)}, u32[]{:S(2)}, u32[]{:S(2)}) collective-permute-start(bf16[4,64,768]{2,1,0:T(8,128)(2,1)} %bitcast.20), channel_id=1, source_target_pairs={{0,6},{1,7},{2,0},{3,1},{4,2},{5,3},{6,4},{7,5},{8,14},{9,15},{10,... | collective-permute-start | bytes 1179656 | tf_op jit(solution)/shard_map/ppermute | solution.py:329
  67.1 1.5 %copy.10 = f32[64,1,256]{2,1,0:T(1,128)} copy(f32[64,1,256]{2,0,1:T(8,128)} %bitcast.27) | data formatting | bytes 131072 | tf_op jit(solution)/shard_map/all_to_all | solution.py:330
  68.6 14.5 %all-to-all-start = ((f32[64,1,256]{2,1,0:T(1,128)}), f32[64,1,256]{2,1,0:T(1,128)S(1)}, u32[]{:S(2)}, u32[]{:S(2)}) async-start(f32[64,1,256]{2,1,0:T(1,128)} %copy.10), calls=%async_computation | async-start | bytes 131072 | tf_op jit(solution)/shard_map/all_to_all | solution.py:330
  83.1 0.8 collective-permute-start.26
  83.9 9.3 %all-to-all-done = f32[64,1,256]{2,1,0:T(1,128)S(1)} async-done(((f32[64,1,256]{2,1,0:T(1,128)}), f32[64,1,256]{2,1,0:T(1,128)S(1)}, u32[]{:S(2)}, u32[]{:S(2)}) %all-to-all-start) | async-done | bytes 65568 | tf_op jit(solution)/shard_map/all_to_all | solution.py:330
  93.2 0.5 cut.1
  93.8 0.3 collective-permute-start.24
  94.0 2.5 %collective-permute-start.25 = (bf16[2,64,768]{2,1,0:T(8,128)(2,1)S(1)}, bf16[2,64,768]{2,1,0:T(8,128)(2,1)S(1)}, u32[]{:S(2)}, u32[]{:S(2)}) collective-permute-start(bf16[2,64,768]{2,1,0:T(8,128)(2,1)S(1)} %get-tuple-element.16), channel_id=1, source_target_pairs={{0,6},{1,7},{2,0},{3,1},{4,2},{5,3},{6,4},{7,5},{8,14},{9,15},{10,... | collective-permute-start | bytes 589832 | tf_op jit(solution)/shard_map/ppermute | solution.py:333
  96.5 1.0 collective-permute-start.27
  97.5 3.7 %collective-permute-done.24.refs_3_ = bf16[2,64,768]{2,1,0:T(8,128)(2,1)S(1)} collective-permute-done((bf16[2,64,768]{2,1,0:T(8,128)(2,1)S(1)}, bf16[2,64,768]{2,1,0:T(8,128)(2,1)S(1)}, u32[]{:S(2)}, u32[]{:S(2)}) %collective-permute-start.24) | collective-permute-done | bytes 196640 | tf_op jit(solution)/shard_map/ppermute | solution.py:332
  101.1 1.2 %collective-permute-start.29 = (bf16[2,64,768]{2,1,0:T(8,128)(2,1)S(1)}, bf16[2,64,768]{2,1,0:T(8,128)(2,1)S(1)}, u32[]{:S(2)}, u32[]{:S(2)}) collective-permute-start(bf16[2,64,768]{2,1,0:T(8,128)(2,1)S(1)} %collective-permute-done.24.refs_3_), channel_id=1, source_target_pairs={{0,1},{1,0},{2,3},{3,2},{4,5},{5,4},{6,7},{7,6},{8,9},{9,8},{10,11... | collective-permute-start | bytes 589832 | tf_op jit(solution)/shard_map/ppermute | solution.py:335
  102.4 0.0 collective-permute-start.30
  102.4 0.1 convert_reduce_fusion.bounds
  102.5 0.9 collective-permute-done.29.refs_8_
  103.4 0.4 collective-permute-done.30.refs_9_
  103.8 0.0 copy-start.4
  103.8 1.0 copy-done.4
  104.8 0.7 copy-done.5
  105.5 7.5 %attend.1 = bf16[2048,384]{1,0:T(8,128)(2,1)} custom-call(s32[6]{0:T(128)S(1)} %copy-done.6, s32[5]{0:T(128)S(1)} %convert_reduce_fusion.bounds, bf16[2048,384]{1,0:T(8,128)(2,1)S(1)} %copy-done.1, f32[1,384]{1,0:T(1,128)S(1)} %broadcast_in_dim.11.gain, f32[16,128]{1,0:T(8,128)S(1)} %copy-done.5, f32[8,256]{1,0:T(8,128)S(1)} %get-tuple-element.14.key_total, ...), custom_call_target="tpu_custom_call" | custom-call | flops 1610612736 | bytes 3145728 | tf_op jit(solution)/shard_map/attend/pallas_call | solution.py:272
  (69 shorter events, 0.2 us)
Async XLA Ops:
  0.0 54.2 %copy-start = (s32[16]{0:T(128)S(1)}, s32[16]{0:T(128)}, u32[]{:S(2)}) copy-start(s32[16]{0:T(128)} %param.13) | copy-start | bytes 196
  1.0 7.9 %collective-permute-start.11 = (bf16[4,8,2560]{2,1,0:T(8,128)(2,1)S(1)}, bf16[4,8,2560]{2,1,0:T(8,128)(2,1)S(1)}, u32[]{:S(2)}, u32[]{:S(2)}) collective-permute-start(bf16[4,8,2560]{2,1,0:T(8,128)(2,1)S(1)} %get-tuple-element.17.text), channel_id=1, source_target_pairs={{0,8},{8,16},{16,24},{24,0},{1,9},{9,17},{17,25},{25,1},{2,10},{10... | collective-permute-start | bytes 491528 | tf_op jit(solution)/shard_map/ppermute | solution.py:309
  3.2 5.9 %collective-permute-start.12 = (bf16[4,8,2560]{2,1,0:T(8,128)(2,1)S(1)}, bf16[4,8,2560]{2,1,0:T(8,128)(2,1)S(1)}, u32[]{:S(2)}, u32[]{:S(2)}) collective-permute-start(bf16[4,8,2560]{2,1,0:T(8,128)(2,1)S(1)} %get-tuple-element.17.text), channel_id=1, source_target_pairs={{0,24},{8,0},{16,8},{24,16},{1,25},{9,1},{17,9},{25,17},{2,26},{10... | collective-permute-start | bytes 491528 | tf_op jit(solution)/shard_map/ppermute | solution.py:310
  4.5 7.3 %collective-permute-start = (bf16[4,8,2560]{2,1,0:T(8,128)(2,1)S(1)}, bf16[4,8,2560]{2,1,0:T(8,128)(2,1)S(1)}, u32[]{:S(2)}, u32[]{:S(2)}) collective-permute-start(bf16[4,8,2560]{2,1,0:T(8,128)(2,1)S(1)} %get-tuple-element.18.text), channel_id=1, source_target_pairs={{0,8},{8,16},{16,24},{24,0},{1,9},{9,17},{17,25},{25,1},{2,10},{10... | collective-permute-start | bytes 491528 | tf_op jit(solution)/shard_map/ppermute | solution.py:309
  4.6 7.3 %collective-permute-start.1 = (bf16[4,8,2560]{2,1,0:T(8,128)(2,1)S(1)}, bf16[4,8,2560]{2,1,0:T(8,128)(2,1)S(1)}, u32[]{:S(2)}, u32[]{:S(2)}) collective-permute-start(bf16[4,8,2560]{2,1,0:T(8,128)(2,1)S(1)} %get-tuple-element.18.text), channel_id=1, source_target_pairs={{0,24},{8,0},{16,8},{24,16},{1,25},{9,1},{17,9},{25,17},{2,26},{10... | collective-permute-start | bytes 491528 | tf_op jit(solution)/shard_map/ppermute | solution.py:310
  9.0 6.5 %collective-permute-start.13 = (bf16[2,8,2560]{2,1,0:T(8,128)(2,1)S(1)}, bf16[2,8,2560]{2,1,0:T(8,128)(2,1)S(1)}, u32[]{:S(2)}, u32[]{:S(2)}) collective-permute-start(bf16[2,8,2560]{2,1,0:T(8,128)(2,1)S(1)} %slice.28), channel_id=1, source_target_pairs={{0,8},{8,16},{16,24},{24,0},{1,9},{9,17},{17,25},{25,1},{2,10},{10... | collective-permute-start | bytes 245768 | tf_op jit(solution)/shard_map/ppermute | solution.py:311
  9.1 6.3 %collective-permute-start.14 = (bf16[2,8,2560]{2,1,0:T(8,128)(2,1)S(1)}, bf16[2,8,2560]{2,1,0:T(8,128)(2,1)S(1)}, u32[]{:S(2)}, u32[]{:S(2)}) collective-permute-start(bf16[2,8,2560]{2,1,0:T(8,128)(2,1)S(1)} %slice.29), channel_id=1, source_target_pairs={{0,24},{8,0},{16,8},{24,16},{1,25},{9,1},{17,9},{25,17},{2,26},{10... | collective-permute-start | bytes 245768 | tf_op jit(solution)/shard_map/ppermute | solution.py:312
  11.9 10.3 %collective-permute-start.2 = (bf16[2,8,2560]{2,1,0:T(8,128)(2,1)S(1)}, bf16[2,8,2560]{2,1,0:T(8,128)(2,1)S(1)}, u32[]{:S(2)}, u32[]{:S(2)}) collective-permute-start(bf16[2,8,2560]{2,1,0:T(8,128)(2,1)S(1)} %slice.26), channel_id=1, source_target_pairs={{0,8},{8,16},{16,24},{24,0},{1,9},{9,17},{17,25},{25,1},{2,10},{10... | collective-permute-start | bytes 245768 | tf_op jit(solution)/shard_map/ppermute | solution.py:311
  12.0 10.2 %collective-permute-start.3 = (bf16[2,8,2560]{2,1,0:T(8,128)(2,1)S(1)}, bf16[2,8,2560]{2,1,0:T(8,128)(2,1)S(1)}, u32[]{:S(2)}, u32[]{:S(2)}) collective-permute-start(bf16[2,8,2560]{2,1,0:T(8,128)(2,1)S(1)} %slice.27), channel_id=1, source_target_pairs={{0,24},{8,0},{16,8},{24,16},{1,25},{9,1},{17,9},{25,17},{2,26},{10... | collective-permute-start | bytes 245768 | tf_op jit(solution)/shard_map/ppermute | solution.py:312
  16.4 37.1 %copy-start.2 = (bf16[4,8,2688]{2,1,0:T(8,128)(2,1)}, bf16[4,8,2688]{2,1,0:T(8,128)(2,1)S(1)}, u32[]{:S(2)}) copy-start(bf16[4,8,2688]{2,1,0:T(8,128)(2,1)S(1)} %pick.3) | copy-start | bytes 516100
  16.4 8.1 %collective-permute-start.18 = (bf16[32,2688]{1,0:T(8,128)(2,1)S(1)}, bf16[32,2688]{1,0:T(8,128)(2,1)S(1)}, u32[]{:S(2)}, u32[]{:S(2)}) collective-permute-start(bf16[32,2688]{1,0:T(8,128)(2,1)S(1)} %bitcast.13), channel_id=1, source_target_pairs={{0,224},{32,0},{64,32},{96,64},{128,96},{160,128},{192,160},{224,1... | collective-permute-start | bytes 516104 | tf_op jit(solution)/shard_map/ppermute | solution.py:323
  23.1 30.4 %copy-start.3 = (bf16[4,8,2560]{2,1,0:T(8,128)(2,1)}, bf16[4,8,2560]{2,1,0:T(8,128)(2,1)S(1)}, u32[]{:S(2)}) copy-start(bf16[4,8,2560]{2,1,0:T(8,128)(2,1)S(1)} %pick.2) | copy-start | bytes 491524
  23.1 5.5 %collective-permute-start.4 = (bf16[32,2560]{1,0:T(8,128)(2,1)S(1)}, bf16[32,2560]{1,0:T(8,128)(2,1)S(1)}, u32[]{:S(2)}, u32[]{:S(2)}) collective-permute-start(bf16[32,2560]{1,0:T(8,128)(2,1)S(1)} %bitcast.16), channel_id=1, source_target_pairs={{0,32},{32,64},{64,96},{96,128},{128,160},{160,192},{192,224},{224... | collective-permute-start | bytes 491528 | tf_op jit(solution)/shard_map/ppermute | solution.py:321
  23.2 7.2 %collective-permute-start.15 = (bf16[32,2688]{1,0:T(8,128)(2,1)S(1)}, bf16[32,2688]{1,0:T(8,128)(2,1)S(1)}, u32[]{:S(2)}, u32[]{:S(2)}) collective-permute-start(bf16[32,2688]{1,0:T(8,128)(2,1)S(1)} %bitcast.14), channel_id=1, source_target_pairs={{0,32},{32,64},{64,96},{96,128},{128,160},{160,192},{192,224},{224... | collective-permute-start | bytes 516104 | tf_op jit(solution)/shard_map/ppermute | solution.py:321
  24.5 29.0 %copy-start.7 = (bf16[32,2688]{1,0:T(8,128)(2,1)}, bf16[32,2688]{1,0:T(8,128)(2,1)S(1)}, u32[]{:S(2)}) copy-start(bf16[32,2688]{1,0:T(8,128)(2,1)S(1)} %collective-permute-done.18.refs_13_) | copy-start | bytes 516100
  24.5 5.9 %collective-permute-start.19 = (bf16[32,2688]{1,0:T(8,128)(2,1)S(1)}, bf16[32,2688]{1,0:T(8,128)(2,1)S(1)}, u32[]{:S(2)}, u32[]{:S(2)}) collective-permute-start(bf16[32,2688]{1,0:T(8,128)(2,1)S(1)} %collective-permute-done.18.refs_13_), channel_id=1, source_target_pairs={{0,224},{32,0},{64,32},{96,64},{128,96},{160,128},{192,160},{224,1... | collective-permute-start | bytes 516104 | tf_op jit(solution)/shard_map/ppermute | solution.py:323
  27.7 5.5 %collective-permute-start.8 = (bf16[32,2560]{1,0:T(8,128)(2,1)S(1)}, bf16[32,2560]{1,0:T(8,128)(2,1)S(1)}, u32[]{:S(2)}, u32[]{:S(2)}) collective-permute-start(bf16[32,2560]{1,0:T(8,128)(2,1)S(1)} %bitcast.17), channel_id=1, source_target_pairs={{0,224},{32,0},{64,32},{96,64},{128,96},{160,128},{192,160},{224,1... | collective-permute-start | bytes 491528 | tf_op jit(solution)/shard_map/ppermute | solution.py:323
  28.6 24.9 %copy-start.14 = (bf16[32,2560]{1,0:T(8,128)(2,1)}, bf16[32,2560]{1,0:T(8,128)(2,1)S(1)}, u32[]{:S(2)}) copy-start(bf16[32,2560]{1,0:T(8,128)(2,1)S(1)} %collective-permute-done.4.refs_1_) | copy-start | bytes 491524
  28.6 7.5 %collective-permute-start.5 = (bf16[32,2560]{1,0:T(8,128)(2,1)S(1)}, bf16[32,2560]{1,0:T(8,128)(2,1)S(1)}, u32[]{:S(2)}, u32[]{:S(2)}) collective-permute-start(bf16[32,2560]{1,0:T(8,128)(2,1)S(1)} %collective-permute-done.4.refs_1_), channel_id=1, source_target_pairs={{0,32},{32,64},{64,96},{96,128},{128,160},{160,192},{192,224},{224... | collective-permute-start | bytes 491528 | tf_op jit(solution)/shard_map/ppermute | solution.py:321
  30.5 23.1 %copy-start.8 = (bf16[32,2688]{1,0:T(8,128)(2,1)}, bf16[32,2688]{1,0:T(8,128)(2,1)S(1)}, u32[]{:S(2)}) copy-start(bf16[32,2688]{1,0:T(8,128)(2,1)S(1)} %collective-permute-done.15.refs_9_) | copy-start | bytes 516100
  30.5 12.6 %collective-permute-start.16 = (bf16[32,2688]{1,0:T(8,128)(2,1)S(1)}, bf16[32,2688]{1,0:T(8,128)(2,1)S(1)}, u32[]{:S(2)}, u32[]{:S(2)}) collective-permute-start(bf16[32,2688]{1,0:T(8,128)(2,1)S(1)} %collective-permute-done.15.refs_9_), channel_id=1, source_target_pairs={{0,32},{32,64},{64,96},{96,128},{128,160},{160,192},{192,224},{224... | collective-permute-start | bytes 516104 | tf_op jit(solution)/shard_map/ppermute | solution.py:321
  30.5 23.1 %copy-start.9 = (bf16[32,2688]{1,0:T(8,128)(2,1)}, bf16[32,2688]{1,0:T(8,128)(2,1)S(1)}, u32[]{:S(2)}) copy-start(bf16[32,2688]{1,0:T(8,128)(2,1)S(1)} %collective-permute-done.19.refs_14_) | copy-start | bytes 516100
  30.5 12.7 %collective-permute-start.20 = (bf16[32,2688]{1,0:T(8,128)(2,1)S(1)}, bf16[32,2688]{1,0:T(8,128)(2,1)S(1)}, u32[]{:S(2)}, u32[]{:S(2)}) collective-permute-start(bf16[32,2688]{1,0:T(8,128)(2,1)S(1)} %collective-permute-done.19.refs_14_), channel_id=1, source_target_pairs={{0,224},{32,0},{64,32},{96,64},{128,96},{160,128},{192,160},{224,1... | collective-permute-start | bytes 516104 | tf_op jit(solution)/shard_map/ppermute | solution.py:323
  33.1 20.4 %copy-start.15 = (bf16[32,2560]{1,0:T(8,128)(2,1)}, bf16[32,2560]{1,0:T(8,128)(2,1)S(1)}, u32[]{:S(2)}) copy-start(bf16[32,2560]{1,0:T(8,128)(2,1)S(1)} %collective-permute-done.8.refs_5_) | copy-start | bytes 491524
  33.1 6.7 %collective-permute-start.9 = (bf16[32,2560]{1,0:T(8,128)(2,1)S(1)}, bf16[32,2560]{1,0:T(8,128)(2,1)S(1)}, u32[]{:S(2)}, u32[]{:S(2)}) collective-permute-start(bf16[32,2560]{1,0:T(8,128)(2,1)S(1)} %collective-permute-done.8.refs_5_), channel_id=1, source_target_pairs={{0,224},{32,0},{64,32},{96,64},{128,96},{160,128},{192,160},{224,1... | collective-permute-start | bytes 491528 | tf_op jit(solution)/shard_map/ppermute | solution.py:323
  36.1 17.4 %copy-start.16 = (bf16[32,2560]{1,0:T(8,128)(2,1)}, bf16[32,2560]{1,0:T(8,128)(2,1)S(1)}, u32[]{:S(2)}) copy-start(bf16[32,2560]{1,0:T(8,128)(2,1)S(1)} %collective-permute-done.5.refs_2_) | copy-start | bytes 491524
  36.1 6.9 %collective-permute-start.6 = (bf16[32,2560]{1,0:T(8,128)(2,1)S(1)}, bf16[32,2560]{1,0:T(8,128)(2,1)S(1)}, u32[]{:S(2)}, u32[]{:S(2)}) collective-permute-start(bf16[32,2560]{1,0:T(8,128)(2,1)S(1)} %collective-permute-done.5.refs_2_), channel_id=1, source_target_pairs={{0,32},{32,64},{64,96},{96,128},{128,160},{160,192},{192,224},{224... | collective-permute-start | bytes 491528 | tf_op jit(solution)/shard_map/ppermute | solution.py:321
  39.9 13.7 %copy-start.17 = (bf16[32,2560]{1,0:T(8,128)(2,1)}, bf16[32,2560]{1,0:T(8,128)(2,1)S(1)}, u32[]{:S(2)}) copy-start(bf16[32,2560]{1,0:T(8,128)(2,1)S(1)} %collective-permute-done.9.refs_6_) | copy-start | bytes 491524
  39.9 15.5 %collective-permute-start.10 = (bf16[32,2560]{1,0:T(8,128)(2,1)S(1)}, bf16[32,2560]{1,0:T(8,128)(2,1)S(1)}, u32[]{:S(2)}, u32[]{:S(2)}) collective-permute-start(bf16[32,2560]{1,0:T(8,128)(2,1)S(1)} %collective-permute-done.9.refs_6_), channel_id=1, source_target_pairs={{0,224},{32,0},{64,32},{96,64},{128,96},{160,128},{192,160},{224,1... | collective-permute-start | bytes 491528 | tf_op jit(solution)/shard_map/ppermute | solution.py:323
  43.0 10.6 %copy-start.10 = (bf16[32,2688]{1,0:T(8,128)(2,1)}, bf16[32,2688]{1,0:T(8,128)(2,1)S(1)}, u32[]{:S(2)}) copy-start(bf16[32,2688]{1,0:T(8,128)(2,1)S(1)} %collective-permute-done.16.refs_10_) | copy-start | bytes 516100
  43.0 12.4 %collective-permute-start.17 = (bf16[32,2688]{1,0:T(8,128)(2,1)S(1)}, bf16[32,2688]{1,0:T(8,128)(2,1)S(1)}, u32[]{:S(2)}, u32[]{:S(2)}) collective-permute-start(bf16[32,2688]{1,0:T(8,128)(2,1)S(1)} %collective-permute-done.16.refs_10_), channel_id=1, source_target_pairs={{0,32},{32,64},{64,96},{96,128},{128,160},{160,192},{192,224},{224... | collective-permute-start | bytes 516104 | tf_op jit(solution)/shard_map/ppermute | solution.py:321
  43.0 10.5 %copy-start.18 = (bf16[32,2560]{1,0:T(8,128)(2,1)}, bf16[32,2560]{1,0:T(8,128)(2,1)S(1)}, u32[]{:S(2)}) copy-start(bf16[32,2560]{1,0:T(8,128)(2,1)S(1)} %collective-permute-done.6.refs_3_) | copy-start | bytes 491524
  43.0 12.4 %collective-permute-start.7 = (bf16[32,2560]{1,0:T(8,128)(2,1)S(1)}, bf16[32,2560]{1,0:T(8,128)(2,1)S(1)}, u32[]{:S(2)}, u32[]{:S(2)}) collective-permute-start(bf16[32,2560]{1,0:T(8,128)(2,1)S(1)} %collective-permute-done.6.refs_3_), channel_id=1, source_target_pairs={{0,32},{32,64},{64,96},{96,128},{128,160},{160,192},{192,224},{224... | collective-permute-start | bytes 491528 | tf_op jit(solution)/shard_map/ppermute | solution.py:321
  43.1 10.4 %copy-start.11 = (bf16[32,2688]{1,0:T(8,128)(2,1)}, bf16[32,2688]{1,0:T(8,128)(2,1)S(1)}, u32[]{:S(2)}) copy-start(bf16[32,2688]{1,0:T(8,128)(2,1)S(1)} %collective-permute-done.20.refs_15_) | copy-start | bytes 516100
  43.2 12.3 %collective-permute-start.21 = (bf16[32,2688]{1,0:T(8,128)(2,1)S(1)}, bf16[32,2688]{1,0:T(8,128)(2,1)S(1)}, u32[]{:S(2)}, u32[]{:S(2)}) collective-permute-start(bf16[32,2688]{1,0:T(8,128)(2,1)S(1)} %collective-permute-done.20.refs_15_), channel_id=1, source_target_pairs={{0,224},{32,0},{64,32},{96,64},{128,96},{160,128},{192,160},{224,1... | collective-permute-start | bytes 516104 | tf_op jit(solution)/shard_map/ppermute | solution.py:323
  45.8 7.8 %copy-start.21 = (f32[384]{0:T(512)S(1)}, f32[384]{0:T(512)}, u32[]{:S(2)}) copy-start(f32[384]{0:T(512)} %param.12) | copy-start | bytes 4612
  55.4 0.7 copy-start.19
  55.4 0.8 copy-start.12
  55.4 0.7 copy-start.20
  56.1 0.7 copy-start.13
  56.8 45.6 %copy-start.22 = (f32[384]{0:T(512)S(1)}, f32[384]{0:T(512)}, u32[]{:S(2)}) copy-start(f32[384]{0:T(512)} %param.11) | copy-start | bytes 4612
  56.8 45.6 %copy-start.23 = (s32[1,16]{1,0:T(1,128)S(1)}, s32[1,16]{1,0:T(1,128)}, u32[]{:S(2)}) copy-start(s32[1,16]{1,0:T(1,128)} %param.15) | copy-start | bytes 196
  56.8 47.0 %copy-start.1 = (bf16[2048,384]{1,0:T(8,128)(2,1)S(1)}, bf16[2048,384]{1,0:T(8,128)(2,1)}, u32[]{:S(2)}) copy-start(bf16[2048,384]{1,0:T(8,128)(2,1)} %queries.1) | copy-start | bytes 4718596
  56.8 47.0 %copy-start.6 = (s32[6]{0:T(128)S(1)}, s32[6]{0:T(128)}, u32[]{:S(2)}) copy-start(s32[6]{0:T(128)} %pad_add_fusion.info) | copy-start | bytes 76
  64.2 29.0 %collective-permute-start.22 = (bf16[4,64,768]{2,1,0:T(8,128)(2,1)}, bf16[4,64,768]{2,1,0:T(8,128)(2,1)S(1)}, u32[]{:S(2)}, u32[]{:S(2)}) collective-permute-start(bf16[4,64,768]{2,1,0:T(8,128)(2,1)} %bitcast.19), channel_id=1, source_target_pairs={{0,2},{1,3},{2,4},{3,5},{4,6},{5,7},{6,0},{7,1},{8,10},{9,11},{10,... | collective-permute-start | bytes 1179656 | tf_op jit(solution)/shard_map/ppermute | solution.py:328
  65.6 27.6 %collective-permute-start.23 = (bf16[4,64,768]{2,1,0:T(8,128)(2,1)}, bf16[4,64,768]{2,1,0:T(8,128)(2,1)S(1)}, u32[]{:S(2)}, u32[]{:S(2)}) collective-permute-start(bf16[4,64,768]{2,1,0:T(8,128)(2,1)} %bitcast.20), channel_id=1, source_target_pairs={{0,6},{1,7},{2,0},{3,1},{4,2},{5,3},{6,4},{7,5},{8,14},{9,15},{10,... | collective-permute-start | bytes 1179656 | tf_op jit(solution)/shard_map/ppermute | solution.py:329
  68.6 24.6 %all-to-all-start = ((f32[64,1,256]{2,1,0:T(1,128)}), f32[64,1,256]{2,1,0:T(1,128)S(1)}, u32[]{:S(2)}, u32[]{:S(2)}) async-start(f32[64,1,256]{2,1,0:T(1,128)} %copy.10), calls=%async_computation | async-start | bytes 131072 | tf_op jit(solution)/shard_map/all_to_all | solution.py:330
  83.1 19.4 %collective-permute-start.26 = (bf16[4,64,768]{2,1,0:T(8,128)(2,1)}, bf16[4,64,768]{2,1,0:T(8,128)(2,1)S(1)}, u32[]{:S(2)}, u32[]{:S(2)}) collective-permute-start(bf16[4,64,768]{2,1,0:T(8,128)(2,1)} %bitcast.21), channel_id=1, source_target_pairs={{0,1},{1,0},{2,3},{3,2},{4,5},{5,4},{6,7},{7,6},{8,9},{9,8},{10,11... | collective-permute-start | bytes 1179656 | tf_op jit(solution)/shard_map/ppermute | solution.py:335
  93.8 7.4 %collective-permute-start.24 = (bf16[2,64,768]{2,1,0:T(8,128)(2,1)S(1)}, bf16[2,64,768]{2,1,0:T(8,128)(2,1)S(1)}, u32[]{:S(2)}, u32[]{:S(2)}) collective-permute-start(bf16[2,64,768]{2,1,0:T(8,128)(2,1)S(1)} %get-tuple-element.15), channel_id=1, source_target_pairs={{0,2},{1,3},{2,4},{3,5},{4,6},{5,7},{6,0},{7,1},{8,10},{9,11},{10,... | collective-permute-start | bytes 589832 | tf_op jit(solution)/shard_map/ppermute | solution.py:332
  94.0 8.4 %collective-permute-start.25 = (bf16[2,64,768]{2,1,0:T(8,128)(2,1)S(1)}, bf16[2,64,768]{2,1,0:T(8,128)(2,1)S(1)}, u32[]{:S(2)}, u32[]{:S(2)}) collective-permute-start(bf16[2,64,768]{2,1,0:T(8,128)(2,1)S(1)} %get-tuple-element.16), channel_id=1, source_target_pairs={{0,6},{1,7},{2,0},{3,1},{4,2},{5,3},{6,4},{7,5},{8,14},{9,15},{10,... | collective-permute-start | bytes 589832 | tf_op jit(solution)/shard_map/ppermute | solution.py:333
  96.5 7.3 %collective-permute-start.27 = (bf16[4,64,768]{2,1,0:T(8,128)(2,1)S(1)}, bf16[4,64,768]{2,1,0:T(8,128)(2,1)S(1)}, u32[]{:S(2)}, u32[]{:S(2)}) collective-permute-start(bf16[4,64,768]{2,1,0:T(8,128)(2,1)S(1)} %collective-permute-done.22.ahead.refs_1_), channel_id=1, source_target_pairs={{0,1},{1,0},{2,3},{3,2},{4,5},{5,4},{6,7},{7,6},{8,9},{9,8},{10,11... | collective-permute-start | bytes 1179656 | tf_op jit(solution)/shard_map/ppermute | solution.py:335
  97.5 6.3 %collective-permute-start.28 = (bf16[4,64,768]{2,1,0:T(8,128)(2,1)S(1)}, bf16[4,64,768]{2,1,0:T(8,128)(2,1)S(1)}, u32[]{:S(2)}, u32[]{:S(2)}) collective-permute-start(bf16[4,64,768]{2,1,0:T(8,128)(2,1)S(1)} %collective-permute-done.23.behind.refs_2_), channel_id=1, source_target_pairs={{0,1},{1,0},{2,3},{3,2},{4,5},{5,4},{6,7},{7,6},{8,9},{9,8},{10,11... | collective-permute-start | bytes 1179656 | tf_op jit(solution)/shard_map/ppermute | solution.py:335
  101.1 2.3 %collective-permute-start.29 = (bf16[2,64,768]{2,1,0:T(8,128)(2,1)S(1)}, bf16[2,64,768]{2,1,0:T(8,128)(2,1)S(1)}, u32[]{:S(2)}, u32[]{:S(2)}) collective-permute-start(bf16[2,64,768]{2,1,0:T(8,128)(2,1)S(1)} %collective-permute-done.24.refs_3_), channel_id=1, source_target_pairs={{0,1},{1,0},{2,3},{3,2},{4,5},{5,4},{6,7},{7,6},{8,9},{9,8},{10,11... | collective-permute-start | bytes 589832 | tf_op jit(solution)/shard_map/ppermute | solution.py:335
  102.4 1.4 %collective-permute-start.30 = (bf16[2,64,768]{2,1,0:T(8,128)(2,1)S(1)}, bf16[2,64,768]{2,1,0:T(8,128)(2,1)S(1)}, u32[]{:S(2)}, u32[]{:S(2)}) collective-permute-start(bf16[2,64,768]{2,1,0:T(8,128)(2,1)S(1)} %collective-permute-done.25.refs_4_), channel_id=1, source_target_pairs={{0,1},{1,0},{2,3},{3,2},{4,5},{5,4},{6,7},{7,6},{8,9},{9,8},{10,11... | collective-permute-start | bytes 589832 | tf_op jit(solution)/shard_map/ppermute | solution.py:335
  103.8 1.0 copy-start.4
  104.8 0.7 copy-start.5

commit v3 on v2

v3 whole, which is shorter than its diff:
```python
import functools
import math

import jax
import jax.numpy as jnp
from jax import lax
from jax.experimental import pallas as pl
from jax.experimental.pallas import tpu as pltpu
from jax.sharding import PartitionSpec as P

HD = 128
FRAME = 128
V_DOWN = 2.0 ** -12
MIB = 1024 * 1024
CHUNK = 512
GROUP = 4
PLANES = (0, -1, -2, -3, 4, 1, 2, 3)

SMEM = pl.BlockSpec(memory_space=pltpu.SMEM)
VMEM = pl.BlockSpec(memory_space=pltpu.VMEM)
HBM = pl.BlockSpec(memory_space=pl.ANY)


def ring(n, k):
    return [(i, (i + k) % n) for i in range(n)]


Y_UP = [(s, (s + 2) % 8) for s in range(8)]
Y_DOWN = [(s, (s - 2) % 8) for s in range(8)]
Y_FAR = [(s, (s + 4) % 8) for s in range(8)]
CORE = [(s, s ^ 1) for s in range(8)]


def pick_kernel(info, *refs):
    sources, out, sem = refs[:4], refs[-2], refs[-1]
    rows, width = sources[0].shape[1:]
    copies = []
    for j in range(out.shape[0]):
        target = out.at[j] if out.shape[2] == width else out.at[j, :, pl.ds(0, width)]
        step, slot = info[6 + j] // 4, info[6 + j] % 4

        def send(source, index, target=target, j=j):
            pltpu.make_async_copy(source.at[index], target, sem.at[j]).start()

        for i, source in enumerate(sources):
            pl.when(step == i)(functools.partial(send, source, slot))
        copies.append(pltpu.make_async_copy(sources[0].at[0], target, sem.at[j]))
    if out.shape[2] > width:
        square = refs[4]
        for j in range(2):
            part = square[j * rows:(j + 1) * rows, :]
            upper = part.astype(out.dtype)
            out[j, :, width:] = upper
            out[2 + j, :, width:] = (part - upper.astype(jnp.float32)).astype(out.dtype)
    for copy in copies:
        copy.wait()


def pick(info, parts, square=None):
    extra = 0 if square is None else HD
    n, rows, width = parts[0].shape
    return pl.pallas_call(
        pick_kernel,
        out_shape=jax.ShapeDtypeStruct((n, rows, width + extra), parts[0].dtype),
        in_specs=[SMEM] + [HBM] * 4 + [VMEM] * (extra // HD),
        out_specs=VMEM,
        scratch_shapes=[pltpu.SemaphoreType.DMA((n,))],
        compiler_params=pltpu.CompilerParams(vmem_limit_bytes=4 * MIB),
        name="pick",
    )(info, *parts, *([] if square is None else [square]))


def project_kernel(info, gain, *refs):
    n = len(PLANES)
    halves, weight = (refs[:n], refs[n:2 * n]), refs[2 * n]
    out, squares, query_total, weight_buf, total, raw, weight_sem = refs[-7:]
    width = weight.shape[0] // 2
    steps = [(half, k) for half in range(2) for k in range(0, width, CHUNK)]
    loads = [
        pltpu.make_async_copy(weight.at[pl.ds(half * width + k, CHUNK)], weight_buf.at[i], weight_sem.at[i])
        for i, (half, k) in enumerate(steps)
    ]
    for load in loads:
        load.start()
    for i, (half, k) in enumerate(steps):
        rows = jnp.concatenate([block[:, k:k + CHUNK] for block in halves[half]], axis=0)
        loads[i].wait()
        part = jnp.dot(rows, weight_buf[i], preferred_element_type=jnp.float32)
        if i == 0:
            total[...] = part
        else:
            total[...] += part
    riders = [block[:, width:].astype(jnp.float32) for block in halves[1]]
    query_total[...] = sum(rider[:16] + rider[16:] for rider in riders)
    columns = out.shape[-1] // 2
    enc, seq = info[0], info[1]
    place = lax.broadcasted_iota(jnp.int32, (8, columns), 0)
    for i, offset in enumerate(PLANES):
        plane = lax.rem(enc + offset + 8, 8)
        for t in range(4):
            both = total[32 * i + 8 * t:32 * i + 8 * t + 8, :]
            live = plane * 64 + seq * 8 + place < info[2 + t]
            raw[t, plane] = both[:, :columns]
            out[t, plane, :, :columns] = (both[:, :columns] * gain[...][None, :]).astype(out.dtype)
            out[t, plane, :, columns:] = jnp.where(
                live, both[:, columns:] * V_DOWN, 0.0
            ).astype(out.dtype)
    square = raw[...].reshape(256, columns)
    square = square * square
    upper = square.astype(jnp.bfloat16)
    lower = (square - upper.astype(jnp.float32)).astype(jnp.bfloat16)
    ones = jnp.ones((8, columns), jnp.bfloat16)
    across = (((1,), (1,)), ((), ()))
    summed = lax.dot_general(
        ones, upper, across, preferred_element_type=jnp.float32
    ) + lax.dot_general(ones, lower, across, preferred_element_type=jnp.float32)
    for i in range(0, squares.shape[0], 8):
        squares[i:i + 8] = summed.reshape(8, 1, 256)


def project(info, gain, blocks, weight):
    width, both = weight.shape
    return pl.pallas_call(
        project_kernel,
        out_shape=(
            jax.ShapeDtypeStruct((4, 8, 8, both), jnp.bfloat16),
            jax.ShapeDtypeStruct((64, 1, 256), jnp.float32),
            jax.ShapeDtypeStruct((16, HD), jnp.float32),
        ),
        in_specs=[SMEM] + [VMEM] * (len(blocks) + 1) + [HBM],
        out_specs=[VMEM] * 3,
        scratch_shapes=[
            pltpu.VMEM((width // CHUNK, CHUNK, both), jnp.bfloat16),
            pltpu.VMEM((256, both), jnp.float32),
            pltpu.VMEM((4, 8, 8, both // 2), jnp.float32),
            pltpu.SemaphoreType.DMA((width // CHUNK,)),
        ],
        compiler_params=pltpu.CompilerParams(vmem_limit_bytes=48 * MIB),
        cost_estimate=pl.CostEstimate(
            flops=2 * 256 * width * both, bytes_accessed=2 * (256 * width + width * both), transcendentals=0
        ),
        name="project",
    )(info, gain, *blocks, weight)


def total_kernel(piece, squares, out, total, sem):
    copy = pltpu.make_async_copy(piece, out, sem)
    copy.start()
    for i in range(8):
        row = squares[i]
        for plane in range(1, 8):
            row = row + squares[8 * plane + i]
        total[i:i + 1, :] = row
    copy.wait()


def key_sums(piece, squares):
    return pl.pallas_call(
        total_kernel,
        out_shape=(jax.ShapeDtypeStruct(piece.shape, piece.dtype), jax.ShapeDtypeStruct((8, 256), jnp.float32)),
        in_specs=[HBM, VMEM],
        out_specs=[VMEM] * 2,
        scratch_shapes=[pltpu.SemaphoreType.DMA],
        compiler_params=pltpu.CompilerParams(vmem_limit_bytes=4 * MIB),
        name="key_sums",
    )(piece, squares)


def attend_kernel(width, info, bounds, queries, gain, query_total, key_total, *refs):
    parts, out = refs[:8], refs[8]
    raw_buf, q_buf, o_buf, k_buf, v_buf, scale_buf, sem, query_sem = refs[9:]
    seq, heads = info[1], queries.shape[1] // HD
    columns = heads * HD
    frames = queries.shape[0] // FRAME
    load = pltpu.make_async_copy(queries, raw_buf, query_sem)
    load.start()

    def piece_seq(piece):
        y, c = seq // 2, seq % 2
        kind = piece % 4
        shift = jnp.where(kind == 0, 0, jnp.where(kind == 1, 3, jnp.where(kind == 2, 1, 2)))
        return 2 * ((y + shift) % 4) + (c + piece // 4) % 2

    def position(shape, axis):
        key = lax.broadcasted_iota(jnp.int32, shape, axis)
        return key // 8 % 8 * 64 + piece_seq(key // 64) * 8 + key % 8

    down, across = position((512, HD), 0), position((1, 512), 1)
    totals = [key_total[pl.ds(piece_seq(p), 1), :] for p in range(8)]
    scales = [lax.rsqrt(total / width + 1e-06) * math.log2(math.e) for total in totals]
    for t in range(4):
        live = jnp.where(down < info[2 + t], 1.0, 0.0).astype(v_buf.dtype)
        row = jnp.concatenate([scale[:, t * 64:t * 64 + 64] for scale in scales], axis=1)
        scale_buf[t:t + 1, :] = jnp.where(across < info[2 + t], row, 0.0)
        for p in range(8):
            spot = slice(64 * p, 64 * p + 64)
            k_buf[t, spot, :] = parts[p][t, :, :columns]
            for h in range(heads):
                v_buf[h, t, spot, :HD] = parts[p][t, :, columns + h * HD:columns + (h + 1) * HD]
        for h in range(heads):
            v_buf[h, t, :, HD:] = live

    query_scale = jnp.transpose(lax.rsqrt(query_total[...] / width + 1e-06))
    load.wait()
    for f in range(frames):
        rows = slice(f * FRAME, (f + 1) * FRAME)
        q_buf[rows, :] = (
            raw_buf[rows, :].astype(jnp.float32) * query_scale[:, f:f + 1] * gain[...][None, :] * HD ** (-0.5)
        ).astype(q_buf.dtype)

    def frame_copy(f):
        rows = pl.ds(pl.multiple_of(f * FRAME, FRAME), FRAME)
        return pltpu.make_async_copy(o_buf.at[rows], out.at[rows], sem.at[f])

    for t in range(4):
        first, last = bounds[t], bounds[t + 1]

        def one(i, carry, t=t, first=first, last=last):
            frame = first + GROUP * i
            base = jnp.minimum(frame, frames - GROUP)
            rows = pl.ds(pl.multiple_of(base * FRAME, FRAME), GROUP * FRAME)
            places = [
                pl.ds(pl.multiple_of(jnp.where(base + g < frame, frames, base + g) * FRAME, FRAME), FRAME)
                for g in range(GROUP)
            ]
            for h in range(heads):
                lanes = slice(h * HD, (h + 1) * HD)
                scores = lax.dot_general(
                    q_buf[rows, lanes], k_buf[t, :, lanes], (((1,), (1,)), ((), ())),
                    preferred_element_type=jnp.float32,
                )
                raised = jnp.exp2(scores * scale_buf[t:t + 1, :]).astype(jnp.bfloat16)
                mixed = jnp.dot(raised, v_buf[h, t], preferred_element_type=jnp.float32)
                result = (mixed[:, :HD] * (1.0 / mixed[:, HD:]) * (1.0 / V_DOWN)).astype(o_buf.dtype)
                for g, place in enumerate(places):
                    o_buf[place, lanes] = result[g * FRAME:(g + 1) * FRAME]
            for g in range(GROUP):

                @pl.when(frame + g < last)
                def _(g=g):
                    frame_copy(frame + g).start()

            return carry

        lax.fori_loop(0, (last - first + GROUP - 1) // GROUP, one, 0)
    for f in range(frames):
        frame_copy(f).wait()


def attend(width, info, bounds, queries, gain, query_total, key_total, parts):
    rows, columns = queries.shape
    return pl.pallas_call(
        functools.partial(attend_kernel, width),
        out_shape=jax.ShapeDtypeStruct((rows, columns), queries.dtype),
        in_specs=[SMEM, SMEM, HBM] + [VMEM] * 11,
        out_specs=HBM,
        scratch_shapes=[
            pltpu.VMEM((rows, columns), queries.dtype),
            pltpu.VMEM((rows, columns), queries.dtype),
            pltpu.VMEM((rows + FRAME, columns), queries.dtype),
            pltpu.VMEM((4, 512, columns), queries.dtype),
            pltpu.VMEM((columns // HD, 4, 512, 2 * HD), queries.dtype),
            pltpu.VMEM((8, 512), jnp.float32),
            pltpu.SemaphoreType.DMA((rows // FRAME,)),
            pltpu.SemaphoreType.DMA,
        ],
        compiler_params=pltpu.CompilerParams(vmem_limit_bytes=20 * MIB),
        cost_estimate=pl.CostEstimate(flops=4 * rows * columns * 512, bytes_accessed=4 * rows * columns, transcendentals=0),
        name="attend",
    )(info, bounds, queries, gain, query_total, key_total, *parts)


def local(queries, text, kv_weight, query_gain, key_gain, prompt_len, served, frame_slot):
    columns = queries.shape[1]
    full_width = columns * 8
    enc, rep, seq = (lax.axis_index(a) for a in ("enc", "rep", "seq"))
    mine = lax.dynamic_slice_in_dim(served, rep * 4, 4)
    code = (mine // 4 - rep + 4) % 4 * 4 + mine % 4
    info = jnp.concatenate([jnp.stack([enc, seq]).astype(jnp.int32), prompt_len[mine], code])
    bounds = jnp.sum(frame_slot.reshape(1, -1) < jnp.arange(5, dtype=jnp.int32)[:, None], axis=1, dtype=jnp.int32)
    query_float = queries.astype(jnp.float32)
    query_square = jnp.sum(query_float * query_float, axis=-1).reshape(-1, HD)
    half = text.shape[2] // 2
    weight = kv_weight.reshape(kv_weight.shape[0], 2 * columns)

    blocks = []
    for n in range(2):
        part = text[:, :, n * half:(n + 1) * half]
        parts = [part] + [lax.ppermute(part, "rep", ring(4, k)) for k in (-1, 2, 1)]
        picked = pick(info, parts, query_square if n == 1 else None)
        blocks.append(picked.reshape(32, picked.shape[2]))

    ups, downs = [[b] for b in blocks], [[b] for b in blocks]
    for i in range(4):
        for n in range(2):
            if n == 0 or i < 3:
                ups[n].append(lax.ppermute(ups[n][-1], "enc", ring(8, 1)))
            if n == 1 or i < 3:
                downs[n].append(lax.ppermute(downs[n][-1], "enc", ring(8, -1)))
    held = ups[0] + downs[0][1:] + ups[1] + [downs[1][4]] + downs[1][1:4]
    pair, squares, query_total = project(info, key_gain, held, weight)
    pair = pair.reshape(4, 64, 2 * columns)

    squares = lax.all_to_all(squares, ("enc", "seq"), 0, 0, tiled=True)
    ahead, behind, far = (lax.ppermute(pair, "seq", p) for p in (Y_UP, Y_DOWN, Y_FAR))
    far, key_total = key_sums(far, squares)
    parts = [pair, ahead, behind, far]
    parts = parts + [lax.ppermute(part, "seq", CORE) for part in parts]
    return attend(full_width, info, bounds, queries, query_gain, query_total, key_total, parts)


def solution(mesh):
    placed = (
        P(("rep", "seq"), "enc"),
        P("rep", ("enc", "seq"), None),
        P(None, None, "enc"),
        P("enc"),
        P("enc"),
        P(),
        P(),
        P("rep", "seq"),
    )
    return jax.shard_map(
        local, mesh=mesh, in_specs=placed, out_specs=P(("rep", "seq"), "enc"), check_vma=False
    )
```

time: 114 us -> 102 us (0.89)
  starting transfers between devices: 54.7 us -> 47.5 us
  local copies, waits for them, and re-layouts: 14.6 us -> 10 us
    ppermute x7, waiting for transfers between devices: 3.45 us -> 8.51 us  [local(): ups[n].append(lax.ppermute(ups[n][-1], 'enc', ring(8, 1)))]
    ppermute x7, waiting for transfers between devices: 5.01 us -> 0.02 us  [local(): downs[n].append(lax.ppermute(downs[n][-1], 'enc', ring(8, -1)))]
    ppermute x12 -> x9, starting transfers between devices: 17.4 us -> 13.6 us  [the longest x6 7.9 us: local(): parts = [part] + [lax.ppermute(part, 'rep', ring(4, k)) for k in (-1, 2, 1)]]
    ppermute x7, starting transfers between devices: 0.78 us -> 3.57 us  [local(): ups[n].append(lax.ppermute(ups[n][-1], 'enc', ring(8, 1)))]
    ppermute x7, starting transfers between devices: 19.1 us -> 16.5 us  [local(): downs[n].append(lax.ppermute(downs[n][-1], 'enc', ring(8, -1)))]
    unnamed x50 -> x9, local copies, waits for them, and re-layouts: 10.8 us -> 8.35 us
    all_to_all x1, starting transfers between devices: 14.5 us -> 12.3 us  [local(): squares = lax.all_to_all(squares, ('enc', 'seq'), 0, 0, tiled=True)]
    all_to_all x1 -> x0, local copies, waits for them, and re-layouts: 1.53 us -> none  [local(): squares = lax.all_to_all(squares, ('enc', 'seq'), 0, 0, tiled=True)]
  transfers between devices with their start and end apart: 32 -> 28, of which waited for: 9 -> 8; matrix products, arithmetic and copies ran while one was open for 12% -> 11% of each run, Pallas kernels for 2% -> 3%
where the time goes in v3:
time: 102 us
  starting transfers between devices  47.5 us (47%)
  waiting for transfers between devices  23.8 us (23%)
  Pallas kernels  16.7 us (16%)
  local copies, waits for them, and re-layouts  10 us (10%)
  other arithmetic  3.39 us (3%)
    ppermute x7, starting transfers between devices, local(): downs[n].append(lax.ppermute(downs[n][-1], 'enc', ring(8, -1)))  16.5 us
    all_to_all x1, starting transfers between devices, local(): squares = lax.all_to_all(squares, ('enc', 'seq'), 0, 0, tiled=True)  12.3 us
    all_to_all x1, waiting for transfers between devices, local(): squares = lax.all_to_all(squares, ('enc', 'seq'), 0, 0, tiled=True)  9.39 us
    ppermute x7, waiting for transfers between devices, local(): ups[n].append(lax.ppermute(ups[n][-1], 'enc', ring(8, 1)))  8.51 us
    unnamed x9, local copies, waits for them, and re-layouts  8.35 us
    ppermute x6, starting transfers between devices, local(): parts = [part] + [lax.ppermute(part, 'rep', ring(4, k)) for k in (-1, 2, 1)]  7.9 us
    pallas_call x1, Pallas kernels, attend(): pl.pallas_call(functools.partial(attend_kernel, width), out_shape=jax.Sha...  7.51 us
    pallas_call x1, Pallas kernels, project(): pl.pallas_call(project_kernel, out_shape=(jax.ShapeDtypeStruct((4, 8, 8,...  6.33 us
  transfers between devices with their start and end apart: 28, of which 8 were waited for; matrix products, arithmetic and copies ran while one was open for 11% of the time, Pallas kernels for 3%

profile of v3, /device:TPU:1, one launch (start us, length us, event | category | flops | bytes accessed | tf_op | source)
XLA Modules:
  0.0 101.7 jit_solution(13673640487100995345)
XLA Ops:
  0.0 1.0 %fusion.3 = (bf16[4,8,2560]{2,1,0:T(8,128)(2,1)S(1)}, bf16[4,8,2560]{2,1,0:T(8,128)(2,1)S(1)}) fusion(bf16[4,8,5120]{2,1,0:T(8,128)(2,1)} %param.9), kind=kLoop, calls=%fused_computation.18 | loop fusion | bytes 655360 | tf_op jit(solution)/shard_map/slice | solution.py:288
  1.0 3.4 %collective-permute-start.10 = (bf16[4,8,2560]{2,1,0:T(8,128)(2,1)S(1)}, bf16[4,8,2560]{2,1,0:T(8,128)(2,1)S(1)}, u32[]{:S(2)}, u32[]{:S(2)}) collective-permute-start(bf16[4,8,2560]{2,1,0:T(8,128)(2,1)S(1)} %get-tuple-element.15.refs_0_), channel_id=1, source_target_pairs={{0,24},{8,0},{16,8},{24,16},{1,25},{9,1},{17,9},{25,17},{2,26},{10... | collective-permute-start | bytes 491528 | tf_op jit(solution)/shard_map/ppermute | solution.py:289
  4.4 0.5 collective-permute-start.11
  4.9 0.6 collective-permute-start.12
  5.5 2.1 %collective-permute-start = (bf16[4,8,2560]{2,1,0:T(8,128)(2,1)S(1)}, bf16[4,8,2560]{2,1,0:T(8,128)(2,1)S(1)}, u32[]{:S(2)}, u32[]{:S(2)}) collective-permute-start(bf16[4,8,2560]{2,1,0:T(8,128)(2,1)S(1)} %get-tuple-element.16.refs_0_), channel_id=1, source_target_pairs={{0,24},{8,0},{16,8},{24,16},{1,25},{9,1},{17,9},{25,17},{2,26},{10... | collective-permute-start | bytes 491528 | tf_op jit(solution)/shard_map/ppermute | solution.py:289
  7.6 1.2 %collective-permute-start.1 = (bf16[4,8,2560]{2,1,0:T(8,128)(2,1)S(1)}, bf16[4,8,2560]{2,1,0:T(8,128)(2,1)S(1)}, u32[]{:S(2)}, u32[]{:S(2)}) collective-permute-start(bf16[4,8,2560]{2,1,0:T(8,128)(2,1)S(1)} %get-tuple-element.16.refs_0_), channel_id=1, source_target_pairs={{0,16},{8,24},{16,0},{24,8},{1,17},{9,25},{17,1},{25,9},{2,18},{10... | collective-permute-start | bytes 491528 | tf_op jit(solution)/shard_map/ppermute | solution.py:289
  8.9 0.7 compare_select_fusion.5
  9.6 1.8 %multiply_reduce_fusion = f32[2048]{0:T(1024)S(1)} fusion(bf16[2048,384]{1,0:T(8,128)(2,1)} %queries.1), kind=kLoop, calls=%fused_computation.1 | loop fusion | flops 2357248 | bytes 1581056 | tf_op jit(solution)/shard_map/reduce_sum | solution.py:282
  11.4 0.0 collective-permute-done.10.refs_1_
  11.4 0.1 collective-permute-start.2
  11.5 0.6 gather_fusion
  12.2 0.1 pad_add_fusion.info
  12.2 0.0 collective-permute-done.11.refs_2_
  12.2 4.6 %collective-permute-done.12.refs_3_ = bf16[4,8,2560]{2,1,0:T(8,128)(2,1)S(1)} collective-permute-done((bf16[4,8,2560]{2,1,0:T(8,128)(2,1)S(1)}, bf16[4,8,2560]{2,1,0:T(8,128)(2,1)S(1)}, u32[]{:S(2)}, u32[]{:S(2)}) %collective-permute-start.12) | collective-permute-done | bytes 163872 | tf_op jit(solution)/shard_map/ppermute | solution.py:289
  16.9 0.9 pick.3
  17.8 5.7 %collective-permute-start.16 = (bf16[32,2688]{1,0:T(8,128)(2,1)S(1)}, bf16[32,2688]{1,0:T(8,128)(2,1)S(1)}, u32[]{:S(2)}, u32[]{:S(2)}) collective-permute-start(bf16[32,2688]{1,0:T(8,128)(2,1)S(1)} %bitcast.9), channel_id=1, source_target_pairs={{0,224},{32,0},{64,32},{96,64},{128,96},{160,128},{192,160},{224,1... | collective-permute-start | bytes 516104 | tf_op jit(solution)/shard_map/ppermute | solution.py:299
  23.5 0.0 collective-permute-done.refs_1_
  23.5 0.0 collective-permute-done.1.refs_2_
  23.5 0.0 collective-permute-done.2.refs_3_
  23.5 0.9 pick.2
  24.4 0.5 collective-permute-start.3
  24.9 1.6 %collective-permute-start.13 = (bf16[32,2688]{1,0:T(8,128)(2,1)S(1)}, bf16[32,2688]{1,0:T(8,128)(2,1)S(1)}, u32[]{:S(2)}, u32[]{:S(2)}) collective-permute-start(bf16[32,2688]{1,0:T(8,128)(2,1)S(1)} %bitcast.10), channel_id=1, source_target_pairs={{0,32},{32,64},{64,96},{96,128},{128,160},{160,192},{192,224},{224... | collective-permute-start | bytes 516104 | tf_op jit(solution)/shard_map/ppermute | solution.py:297
  26.6 0.0 collective-permute-done.16.refs_13_
  26.6 2.7 %collective-permute-start.17 = (bf16[32,2688]{1,0:T(8,128)(2,1)S(1)}, bf16[32,2688]{1,0:T(8,128)(2,1)S(1)}, u32[]{:S(2)}, u32[]{:S(2)}) collective-permute-start(bf16[32,2688]{1,0:T(8,128)(2,1)S(1)} %collective-permute-done.16.refs_13_), channel_id=1, source_target_pairs={{0,224},{32,0},{64,32},{96,64},{128,96},{160,128},{192,160},{224,1... | collective-permute-start | bytes 516104 | tf_op jit(solution)/shard_map/ppermute | solution.py:299
  29.2 1.2 %collective-permute-start.7 = (bf16[32,2560]{1,0:T(8,128)(2,1)S(1)}, bf16[32,2560]{1,0:T(8,128)(2,1)S(1)}, u32[]{:S(2)}, u32[]{:S(2)}) collective-permute-start(bf16[32,2560]{1,0:T(8,128)(2,1)S(1)} %bitcast.13), channel_id=1, source_target_pairs={{0,224},{32,0},{64,32},{96,64},{128,96},{160,128},{192,160},{224,1... | collective-permute-start | bytes 491528 | tf_op jit(solution)/shard_map/ppermute | solution.py:299
  30.4 2.2 %collective-permute-done.3.refs_1_ = bf16[32,2560]{1,0:T(8,128)(2,1)S(1)} collective-permute-done((bf16[32,2560]{1,0:T(8,128)(2,1)S(1)}, bf16[32,2560]{1,0:T(8,128)(2,1)S(1)}, u32[]{:S(2)}, u32[]{:S(2)}) %collective-permute-start.3) | collective-permute-done | bytes 163872 | tf_op jit(solution)/shard_map/ppermute | solution.py:297
  32.7 0.0 collective-permute-start.4
  32.7 3.7 %collective-permute-done.13.refs_9_ = bf16[32,2688]{1,0:T(8,128)(2,1)S(1)} collective-permute-done((bf16[32,2688]{1,0:T(8,128)(2,1)S(1)}, bf16[32,2688]{1,0:T(8,128)(2,1)S(1)}, u32[]{:S(2)}, u32[]{:S(2)}) %collective-permute-start.13) | collective-permute-done | bytes 172064 | tf_op jit(solution)/shard_map/ppermute | solution.py:297
  36.4 0.0 collective-permute-start.14
  36.4 0.0 collective-permute-done.17.refs_14_
  36.4 2.7 %collective-permute-start.18 = (bf16[32,2688]{1,0:T(8,128)(2,1)S(1)}, bf16[32,2688]{1,0:T(8,128)(2,1)S(1)}, u32[]{:S(2)}, u32[]{:S(2)}) collective-permute-start(bf16[32,2688]{1,0:T(8,128)(2,1)S(1)} %collective-permute-done.17.refs_14_), channel_id=1, source_target_pairs={{0,224},{32,0},{64,32},{96,64},{128,96},{160,128},{192,160},{224,1... | collective-permute-start | bytes 516104 | tf_op jit(solution)/shard_map/ppermute | solution.py:299
  39.0 0.0 collective-permute-done.7.refs_5_
  39.0 0.1 collective-permute-start.8
  39.1 1.4 %collective-permute-start.5 = (bf16[32,2560]{1,0:T(8,128)(2,1)S(1)}, bf16[32,2560]{1,0:T(8,128)(2,1)S(1)}, u32[]{:S(2)}, u32[]{:S(2)}) collective-permute-start(bf16[32,2560]{1,0:T(8,128)(2,1)S(1)} %collective-permute-done.4.refs_2_), channel_id=1, source_target_pairs={{0,32},{32,64},{64,96},{96,128},{128,160},{160,192},{192,224},{224... | collective-permute-start | bytes 491528 | tf_op jit(solution)/shard_map/ppermute | solution.py:297
  40.5 2.6 %collective-permute-done.14.refs_10_ = bf16[32,2688]{1,0:T(8,128)(2,1)S(1)} collective-permute-done((bf16[32,2688]{1,0:T(8,128)(2,1)S(1)}, bf16[32,2688]{1,0:T(8,128)(2,1)S(1)}, u32[]{:S(2)}, u32[]{:S(2)}) %collective-permute-start.14) | collective-permute-done | bytes 172064 | tf_op jit(solution)/shard_map/ppermute | solution.py:297
  43.1 0.0 collective-permute-start.15
  43.1 0.0 collective-permute-done.18.refs_15_
  43.1 2.7 %collective-permute-start.19 = (bf16[32,2688]{1,0:T(8,128)(2,1)S(1)}, bf16[32,2688]{1,0:T(8,128)(2,1)S(1)}, u32[]{:S(2)}, u32[]{:S(2)}) collective-permute-start(bf16[32,2688]{1,0:T(8,128)(2,1)S(1)} %collective-permute-done.18.refs_15_), channel_id=1, source_target_pairs={{0,224},{32,0},{64,32},{96,64},{128,96},{160,128},{192,160},{224,1... | collective-permute-start | bytes 516104 | tf_op jit(solution)/shard_map/ppermute | solution.py:299
  45.8 1.6 %collective-permute-start.9 = (bf16[32,2560]{1,0:T(8,128)(2,1)S(1)}, bf16[32,2560]{1,0:T(8,128)(2,1)S(1)}, u32[]{:S(2)}, u32[]{:S(2)}) collective-permute-start(bf16[32,2560]{1,0:T(8,128)(2,1)S(1)} %collective-permute-done.8.refs_6_), channel_id=1, source_target_pairs={{0,224},{32,0},{64,32},{96,64},{128,96},{160,128},{192,160},{224,1... | collective-permute-start | bytes 491528 | tf_op jit(solution)/shard_map/ppermute | solution.py:299
  47.4 7.7 %copy.9 = bf16[640,8,2,384]{3,1,2,0:T(8,128)(2,1)} copy(bf16[640,8,2,384]{3,2,1,0:T(2,128)(2,1)} %bitcast.22) | data formatting | bytes 15728640
  55.0 0.0 collective-permute-done.9.refs_7_
  55.0 0.0 collective-permute-done.15.refs_11_
  55.0 0.0 collective-permute-done.6.refs_4_
  55.0 0.0 collective-permute-done.19.refs_12_
  55.0 0.0 copy-start.1
  55.0 6.3 %project.1 = (bf16[4,8,8,768]{3,2,1,0:T(8,128)(2,1)S(1)}, f32[64,1,256]{2,1,0:T(1,128)}, f32[16,128]{1,0:T(8,128)S(1)}) custom-call(s32[10]{0:T(128)S(1)} %pad_add_fusion.info, f32[384]{0:T(512)S(1)} %copy-done.3, bf16[32,2560]{1,0:T(8,128)(2,1)S(1)} %bitcast.14, bf16[32,2560]{1,0:T(8,128)(2,1)S(1)} %collective-permute-done.3.refs_1_, ...), custom_call_target="tpu_custom_call" | custom-call | flops 2013265920 | bytes 10485760 | tf_op jit(solution)/shard_map/project/pallas_call | solution.py:123
  61.4 3.0 %collective-permute-start.20 = (bf16[4,64,768]{2,1,0:T(8,128)(2,1)S(1)}, bf16[4,64,768]{2,1,0:T(8,128)(2,1)S(1)}, u32[]{:S(2)}, u32[]{:S(2)}) collective-permute-start(bf16[4,64,768]{2,1,0:T(8,128)(2,1)S(1)} %bitcast.15), channel_id=1, source_target_pairs={{0,4},{1,5},{2,6},{3,7},{4,0},{5,1},{6,2},{7,3},{8,12},{9,13},{10,... | collective-permute-start | bytes 1179656 | tf_op jit(solution)/shard_map/ppermute | solution.py:305
  64.4 0.4 collective-permute-start.21
  64.8 2.3 %collective-permute-start.22 = (bf16[4,64,768]{2,1,0:T(8,128)(2,1)S(1)}, bf16[4,64,768]{2,1,0:T(8,128)(2,1)S(1)}, u32[]{:S(2)}, u32[]{:S(2)}) collective-permute-start(bf16[4,64,768]{2,1,0:T(8,128)(2,1)S(1)} %bitcast.17), channel_id=1, source_target_pairs={{0,6},{1,7},{2,0},{3,1},{4,2},{5,3},{6,4},{7,5},{8,14},{9,15},{10,... | collective-permute-start | bytes 1179656 | tf_op jit(solution)/shard_map/ppermute | solution.py:305
  67.1 12.3 %all-to-all-start = ((f32[64,1,256]{2,1,0:T(1,128)}), f32[64,1,256]{2,1,0:T(1,128)}, u32[]{:S(2)}, u32[]{:S(2)}) async-start(f32[64,1,256]{2,1,0:T(1,128)} %get-tuple-element.12), calls=%async_computation | async-start | bytes 131072 | tf_op jit(solution)/shard_map/all_to_all | solution.py:304
  79.3 0.6 collective-permute-start.23
  80.0 9.4 %all-to-all-done.squares = f32[64,1,256]{2,1,0:T(1,128)} async-done(((f32[64,1,256]{2,1,0:T(1,128)}), f32[64,1,256]{2,1,0:T(1,128)}, u32[]{:S(2)}, u32[]{:S(2)}) %all-to-all-start) | async-done | bytes 65568 | tf_op jit(solution)/shard_map/all_to_all | solution.py:304
  89.3 0.0 collective-permute-done.20.piece
  89.4 1.0 %key_sums.1 = (bf16[4,64,768]{2,1,0:T(8,128)(2,1)S(1)}, f32[8,256]{1,0:T(8,128)S(1)}) custom-call(bf16[4,64,768]{2,1,0:T(8,128)(2,1)S(1)} %collective-permute-done.20.piece, f32[64,1,256]{2,1,0:T(1,128)} %all-to-all-done.squares), custom_call_target="tpu_custom_call" | custom-call | tf_op jit(solution)/shard_map/key_sums/pallas_call | solution.py:158
  90.4 0.5 collective-permute-start.26
  90.9 0.0 collective-permute-done.21.refs_1_
  90.9 0.1 collective-permute-start.24
  91.0 0.4 collective-permute-start.25
  91.4 0.8 convert_reduce_fusion.bounds
  92.2 0.1 collective-permute-done.26.refs_7_
  92.2 0.6 collective-permute-done.24.refs_5_
  92.8 0.6 collective-permute-done.25.refs_6_
  93.4 0.7 copy-done.2
  94.1 7.5 %attend.1 = bf16[2048,384]{1,0:T(8,128)(2,1)} custom-call(s32[10]{0:T(128)S(1)} %pad_add_fusion.info, s32[5]{0:T(128)S(1)} %convert_reduce_fusion.bounds, bf16[2048,384]{1,0:T(8,128)(2,1)S(1)} %copy-done.1, f32[384]{0:T(512)S(1)} %copy-done.2, f32[16,128]{1,0:T(8,128)S(1)} %get-tuple-element.10.query_total, f32[8,256]{1,0:T(8,128)S(1)} %get-tuple-element.13.key_total, ...), custom_call_target="tpu_custom_call" | custom-call | flops 1610612736 | bytes 3145728 | tf_op jit(solution)/shard_map/attend/pallas_call | solution.py:252
  (13 shorter events, 0.0 us)
Async XLA Ops:
  0.0 11.5 %copy-start = (s32[16]{0:T(128)S(1)}, s32[16]{0:T(128)}, u32[]{:S(2)}) copy-start(s32[16]{0:T(128)} %param.13) | copy-start | bytes 196
  1.0 10.4 %collective-permute-start.10 = (bf16[4,8,2560]{2,1,0:T(8,128)(2,1)S(1)}, bf16[4,8,2560]{2,1,0:T(8,128)(2,1)S(1)}, u32[]{:S(2)}, u32[]{:S(2)}) collective-permute-start(bf16[4,8,2560]{2,1,0:T(8,128)(2,1)S(1)} %get-tuple-element.15.refs_0_), channel_id=1, source_target_pairs={{0,24},{8,0},{16,8},{24,16},{1,25},{9,1},{17,9},{25,17},{2,26},{10... | collective-permute-start | bytes 491528 | tf_op jit(solution)/shard_map/ppermute | solution.py:289
  4.4 7.8 %collective-permute-start.11 = (bf16[4,8,2560]{2,1,0:T(8,128)(2,1)S(1)}, bf16[4,8,2560]{2,1,0:T(8,128)(2,1)S(1)}, u32[]{:S(2)}, u32[]{:S(2)}) collective-permute-start(bf16[4,8,2560]{2,1,0:T(8,128)(2,1)S(1)} %get-tuple-element.15.refs_0_), channel_id=1, source_target_pairs={{0,16},{8,24},{16,0},{24,8},{1,17},{9,25},{17,1},{25,9},{2,18},{10... | collective-permute-start | bytes 491528 | tf_op jit(solution)/shard_map/ppermute | solution.py:289
  4.9 11.9 %collective-permute-start.12 = (bf16[4,8,2560]{2,1,0:T(8,128)(2,1)S(1)}, bf16[4,8,2560]{2,1,0:T(8,128)(2,1)S(1)}, u32[]{:S(2)}, u32[]{:S(2)}) collective-permute-start(bf16[4,8,2560]{2,1,0:T(8,128)(2,1)S(1)} %get-tuple-element.15.refs_0_), channel_id=1, source_target_pairs={{0,8},{8,16},{16,24},{24,0},{1,9},{9,17},{17,25},{25,1},{2,10},{10... | collective-permute-start | bytes 491528 | tf_op jit(solution)/shard_map/ppermute | solution.py:289
  5.5 17.9 %collective-permute-start = (bf16[4,8,2560]{2,1,0:T(8,128)(2,1)S(1)}, bf16[4,8,2560]{2,1,0:T(8,128)(2,1)S(1)}, u32[]{:S(2)}, u32[]{:S(2)}) collective-permute-start(bf16[4,8,2560]{2,1,0:T(8,128)(2,1)S(1)} %get-tuple-element.16.refs_0_), channel_id=1, source_target_pairs={{0,24},{8,0},{16,8},{24,16},{1,25},{9,1},{17,9},{25,17},{2,26},{10... | collective-permute-start | bytes 491528 | tf_op jit(solution)/shard_map/ppermute | solution.py:289
  7.6 15.8 %collective-permute-start.1 = (bf16[4,8,2560]{2,1,0:T(8,128)(2,1)S(1)}, bf16[4,8,2560]{2,1,0:T(8,128)(2,1)S(1)}, u32[]{:S(2)}, u32[]{:S(2)}) collective-permute-start(bf16[4,8,2560]{2,1,0:T(8,128)(2,1)S(1)} %get-tuple-element.16.refs_0_), channel_id=1, source_target_pairs={{0,16},{8,24},{16,0},{24,8},{1,17},{9,25},{17,1},{25,9},{2,18},{10... | collective-permute-start | bytes 491528 | tf_op jit(solution)/shard_map/ppermute | solution.py:289
  11.4 12.1 %collective-permute-start.2 = (bf16[4,8,2560]{2,1,0:T(8,128)(2,1)S(1)}, bf16[4,8,2560]{2,1,0:T(8,128)(2,1)S(1)}, u32[]{:S(2)}, u32[]{:S(2)}) collective-permute-start(bf16[4,8,2560]{2,1,0:T(8,128)(2,1)S(1)} %get-tuple-element.16.refs_0_), channel_id=1, source_target_pairs={{0,8},{8,16},{16,24},{24,0},{1,9},{9,17},{17,25},{25,1},{2,10},{10... | collective-permute-start | bytes 491528 | tf_op jit(solution)/shard_map/ppermute | solution.py:289
  17.8 8.8 %collective-permute-start.16 = (bf16[32,2688]{1,0:T(8,128)(2,1)S(1)}, bf16[32,2688]{1,0:T(8,128)(2,1)S(1)}, u32[]{:S(2)}, u32[]{:S(2)}) collective-permute-start(bf16[32,2688]{1,0:T(8,128)(2,1)S(1)} %bitcast.9), channel_id=1, source_target_pairs={{0,224},{32,0},{64,32},{96,64},{128,96},{160,128},{192,160},{224,1... | collective-permute-start | bytes 516104 | tf_op jit(solution)/shard_map/ppermute | solution.py:299
  24.4 8.3 %collective-permute-start.3 = (bf16[32,2560]{1,0:T(8,128)(2,1)S(1)}, bf16[32,2560]{1,0:T(8,128)(2,1)S(1)}, u32[]{:S(2)}, u32[]{:S(2)}) collective-permute-start(bf16[32,2560]{1,0:T(8,128)(2,1)S(1)} %bitcast.12), channel_id=1, source_target_pairs={{0,32},{32,64},{64,96},{96,128},{128,160},{160,192},{192,224},{224... | collective-permute-start | bytes 491528 | tf_op jit(solution)/shard_map/ppermute | solution.py:297
  24.9 11.4 %collective-permute-start.13 = (bf16[32,2688]{1,0:T(8,128)(2,1)S(1)}, bf16[32,2688]{1,0:T(8,128)(2,1)S(1)}, u32[]{:S(2)}, u32[]{:S(2)}) collective-permute-start(bf16[32,2688]{1,0:T(8,128)(2,1)S(1)} %bitcast.10), channel_id=1, source_target_pairs={{0,32},{32,64},{64,96},{96,128},{128,160},{160,192},{192,224},{224... | collective-permute-start | bytes 516104 | tf_op jit(solution)/shard_map/ppermute | solution.py:297
  26.6 9.8 %collective-permute-start.17 = (bf16[32,2688]{1,0:T(8,128)(2,1)S(1)}, bf16[32,2688]{1,0:T(8,128)(2,1)S(1)}, u32[]{:S(2)}, u32[]{:S(2)}) collective-permute-start(bf16[32,2688]{1,0:T(8,128)(2,1)S(1)} %collective-permute-done.16.refs_13_), channel_id=1, source_target_pairs={{0,224},{32,0},{64,32},{96,64},{128,96},{160,128},{192,160},{224,1... | collective-permute-start | bytes 516104 | tf_op jit(solution)/shard_map/ppermute | solution.py:299
  29.2 9.8 %collective-permute-start.7 = (bf16[32,2560]{1,0:T(8,128)(2,1)S(1)}, bf16[32,2560]{1,0:T(8,128)(2,1)S(1)}, u32[]{:S(2)}, u32[]{:S(2)}) collective-permute-start(bf16[32,2560]{1,0:T(8,128)(2,1)S(1)} %bitcast.13), channel_id=1, source_target_pairs={{0,224},{32,0},{64,32},{96,64},{128,96},{160,128},{192,160},{224,1... | collective-permute-start | bytes 491528 | tf_op jit(solution)/shard_map/ppermute | solution.py:299
  32.7 6.5 %collective-permute-start.4 = (bf16[32,2560]{1,0:T(8,128)(2,1)S(1)}, bf16[32,2560]{1,0:T(8,128)(2,1)S(1)}, u32[]{:S(2)}, u32[]{:S(2)}) collective-permute-start(bf16[32,2560]{1,0:T(8,128)(2,1)S(1)} %collective-permute-done.3.refs_1_), channel_id=1, source_target_pairs={{0,32},{32,64},{64,96},{96,128},{128,160},{160,192},{192,224},{224... | collective-permute-start | bytes 491528 | tf_op jit(solution)/shard_map/ppermute | solution.py:297
  36.4 6.7 %collective-permute-start.14 = (bf16[32,2688]{1,0:T(8,128)(2,1)S(1)}, bf16[32,2688]{1,0:T(8,128)(2,1)S(1)}, u32[]{:S(2)}, u32[]{:S(2)}) collective-permute-start(bf16[32,2688]{1,0:T(8,128)(2,1)S(1)} %collective-permute-done.13.refs_9_), channel_id=1, source_target_pairs={{0,32},{32,64},{64,96},{96,128},{128,160},{160,192},{192,224},{224... | collective-permute-start | bytes 516104 | tf_op jit(solution)/shard_map/ppermute | solution.py:297
  36.4 6.7 %collective-permute-start.18 = (bf16[32,2688]{1,0:T(8,128)(2,1)S(1)}, bf16[32,2688]{1,0:T(8,128)(2,1)S(1)}, u32[]{:S(2)}, u32[]{:S(2)}) collective-permute-start(bf16[32,2688]{1,0:T(8,128)(2,1)S(1)} %collective-permute-done.17.refs_14_), channel_id=1, source_target_pairs={{0,224},{32,0},{64,32},{96,64},{128,96},{160,128},{192,160},{224,1... | collective-permute-start | bytes 516104 | tf_op jit(solution)/shard_map/ppermute | solution.py:299
  39.0 6.7 %collective-permute-start.8 = (bf16[32,2560]{1,0:T(8,128)(2,1)S(1)}, bf16[32,2560]{1,0:T(8,128)(2,1)S(1)}, u32[]{:S(2)}, u32[]{:S(2)}) collective-permute-start(bf16[32,2560]{1,0:T(8,128)(2,1)S(1)} %collective-permute-done.7.refs_5_), channel_id=1, source_target_pairs={{0,224},{32,0},{64,32},{96,64},{128,96},{160,128},{192,160},{224,1... | collective-permute-start | bytes 491528 | tf_op jit(solution)/shard_map/ppermute | solution.py:299
  39.1 8.2 %collective-permute-start.5 = (bf16[32,2560]{1,0:T(8,128)(2,1)S(1)}, bf16[32,2560]{1,0:T(8,128)(2,1)S(1)}, u32[]{:S(2)}, u32[]{:S(2)}) collective-permute-start(bf16[32,2560]{1,0:T(8,128)(2,1)S(1)} %collective-permute-done.4.refs_2_), channel_id=1, source_target_pairs={{0,32},{32,64},{64,96},{96,128},{128,160},{160,192},{192,224},{224... | collective-permute-start | bytes 491528 | tf_op jit(solution)/shard_map/ppermute | solution.py:297
  43.1 11.9 %collective-permute-start.15 = (bf16[32,2688]{1,0:T(8,128)(2,1)S(1)}, bf16[32,2688]{1,0:T(8,128)(2,1)S(1)}, u32[]{:S(2)}, u32[]{:S(2)}) collective-permute-start(bf16[32,2688]{1,0:T(8,128)(2,1)S(1)} %collective-permute-done.14.refs_10_), channel_id=1, source_target_pairs={{0,32},{32,64},{64,96},{96,128},{128,160},{160,192},{192,224},{224... | collective-permute-start | bytes 516104 | tf_op jit(solution)/shard_map/ppermute | solution.py:297
  43.1 11.9 %collective-permute-start.19 = (bf16[32,2688]{1,0:T(8,128)(2,1)S(1)}, bf16[32,2688]{1,0:T(8,128)(2,1)S(1)}, u32[]{:S(2)}, u32[]{:S(2)}) collective-permute-start(bf16[32,2688]{1,0:T(8,128)(2,1)S(1)} %collective-permute-done.18.refs_15_), channel_id=1, source_target_pairs={{0,224},{32,0},{64,32},{96,64},{128,96},{160,128},{192,160},{224,1... | collective-permute-start | bytes 516104 | tf_op jit(solution)/shard_map/ppermute | solution.py:299
  45.8 9.2 %collective-permute-start.9 = (bf16[32,2560]{1,0:T(8,128)(2,1)S(1)}, bf16[32,2560]{1,0:T(8,128)(2,1)S(1)}, u32[]{:S(2)}, u32[]{:S(2)}) collective-permute-start(bf16[32,2560]{1,0:T(8,128)(2,1)S(1)} %collective-permute-done.8.refs_6_), channel_id=1, source_target_pairs={{0,224},{32,0},{64,32},{96,64},{128,96},{160,128},{192,160},{224,1... | collective-permute-start | bytes 491528 | tf_op jit(solution)/shard_map/ppermute | solution.py:299
  47.3 7.7 %collective-permute-start.6 = (bf16[32,2560]{1,0:T(8,128)(2,1)S(1)}, bf16[32,2560]{1,0:T(8,128)(2,1)S(1)}, u32[]{:S(2)}, u32[]{:S(2)}) collective-permute-start(bf16[32,2560]{1,0:T(8,128)(2,1)S(1)} %collective-permute-done.5.refs_3_), channel_id=1, source_target_pairs={{0,32},{32,64},{64,96},{96,128},{128,160},{160,192},{192,224},{224... | collective-permute-start | bytes 491528 | tf_op jit(solution)/shard_map/ppermute | solution.py:297
  47.3 7.7 %copy-start.3 = (f32[384]{0:T(512)S(1)}, f32[384]{0:T(512)}, u32[]{:S(2)}) copy-start(f32[384]{0:T(512)} %gain.2) | copy-start | bytes 4612
  55.0 38.3 %copy-start.1 = (bf16[2048,384]{1,0:T(8,128)(2,1)S(1)}, bf16[2048,384]{1,0:T(8,128)(2,1)}, u32[]{:S(2)}) copy-start(bf16[2048,384]{1,0:T(8,128)(2,1)} %queries.1) | copy-start | bytes 4718596
  61.4 28.0 %collective-permute-start.20 = (bf16[4,64,768]{2,1,0:T(8,128)(2,1)S(1)}, bf16[4,64,768]{2,1,0:T(8,128)(2,1)S(1)}, u32[]{:S(2)}, u32[]{:S(2)}) collective-permute-start(bf16[4,64,768]{2,1,0:T(8,128)(2,1)S(1)} %bitcast.15), channel_id=1, source_target_pairs={{0,4},{1,5},{2,6},{3,7},{4,0},{5,1},{6,2},{7,3},{8,12},{9,13},{10,... | collective-permute-start | bytes 1179656 | tf_op jit(solution)/shard_map/ppermute | solution.py:305
  64.4 26.5 %collective-permute-start.21 = (bf16[4,64,768]{2,1,0:T(8,128)(2,1)S(1)}, bf16[4,64,768]{2,1,0:T(8,128)(2,1)S(1)}, u32[]{:S(2)}, u32[]{:S(2)}) collective-permute-start(bf16[4,64,768]{2,1,0:T(8,128)(2,1)S(1)} %bitcast.16), channel_id=1, source_target_pairs={{0,2},{1,3},{2,4},{3,5},{4,6},{5,7},{6,0},{7,1},{8,10},{9,11},{10,... | collective-permute-start | bytes 1179656 | tf_op jit(solution)/shard_map/ppermute | solution.py:305
  64.8 26.2 %collective-permute-start.22 = (bf16[4,64,768]{2,1,0:T(8,128)(2,1)S(1)}, bf16[4,64,768]{2,1,0:T(8,128)(2,1)S(1)}, u32[]{:S(2)}, u32[]{:S(2)}) collective-permute-start(bf16[4,64,768]{2,1,0:T(8,128)(2,1)S(1)} %bitcast.17), channel_id=1, source_target_pairs={{0,6},{1,7},{2,0},{3,1},{4,2},{5,3},{6,4},{7,5},{8,14},{9,15},{10,... | collective-permute-start | bytes 1179656 | tf_op jit(solution)/shard_map/ppermute | solution.py:305
  67.1 22.3 %all-to-all-start = ((f32[64,1,256]{2,1,0:T(1,128)}), f32[64,1,256]{2,1,0:T(1,128)}, u32[]{:S(2)}, u32[]{:S(2)}) async-start(f32[64,1,256]{2,1,0:T(1,128)} %get-tuple-element.12), calls=%async_computation | async-start | bytes 131072 | tf_op jit(solution)/shard_map/all_to_all | solution.py:304
  79.3 12.8 %collective-permute-start.23 = (bf16[4,64,768]{2,1,0:T(8,128)(2,1)S(1)}, bf16[4,64,768]{2,1,0:T(8,128)(2,1)S(1)}, u32[]{:S(2)}, u32[]{:S(2)}) collective-permute-start(bf16[4,64,768]{2,1,0:T(8,128)(2,1)S(1)} %bitcast.18), channel_id=1, source_target_pairs={{0,1},{1,0},{2,3},{3,2},{4,5},{5,4},{6,7},{7,6},{8,9},{9,8},{10,11... | collective-permute-start | bytes 1179656 | tf_op jit(solution)/shard_map/ppermute | solution.py:308
  90.4 1.8 %collective-permute-start.26 = (bf16[4,64,768]{2,1,0:T(8,128)(2,1)S(1)}, bf16[4,64,768]{2,1,0:T(8,128)(2,1)S(1)}, u32[]{:S(2)}, u32[]{:S(2)}) collective-permute-start(bf16[4,64,768]{2,1,0:T(8,128)(2,1)S(1)} %get-tuple-element.14.refs_3_), channel_id=1, source_target_pairs={{0,1},{1,0},{2,3},{3,2},{4,5},{5,4},{6,7},{7,6},{8,9},{9,8},{10,11... | collective-permute-start | bytes 1179656 | tf_op jit(solution)/shard_map/ppermute | solution.py:308
  90.9 1.9 %collective-permute-start.24 = (bf16[4,64,768]{2,1,0:T(8,128)(2,1)S(1)}, bf16[4,64,768]{2,1,0:T(8,128)(2,1)S(1)}, u32[]{:S(2)}, u32[]{:S(2)}) collective-permute-start(bf16[4,64,768]{2,1,0:T(8,128)(2,1)S(1)} %collective-permute-done.21.refs_1_), channel_id=1, source_target_pairs={{0,1},{1,0},{2,3},{3,2},{4,5},{5,4},{6,7},{7,6},{8,9},{9,8},{10,11... | collective-permute-start | bytes 1179656 | tf_op jit(solution)/shard_map/ppermute | solution.py:308
  91.0 2.4 %collective-permute-start.25 = (bf16[4,64,768]{2,1,0:T(8,128)(2,1)S(1)}, bf16[4,64,768]{2,1,0:T(8,128)(2,1)S(1)}, u32[]{:S(2)}, u32[]{:S(2)}) collective-permute-start(bf16[4,64,768]{2,1,0:T(8,128)(2,1)S(1)} %collective-permute-done.22.refs_2_), channel_id=1, source_target_pairs={{0,1},{1,0},{2,3},{3,2},{4,5},{5,4},{6,7},{7,6},{8,9},{9,8},{10,11... | collective-permute-start | bytes 1179656 | tf_op jit(solution)/shard_map/ppermute | solution.py:308
  93.4 0.7 copy-start.2

commit v4 on v3

v4 whole, which is shorter than its diff:
```python
import functools
import math

import jax
import jax.numpy as jnp
from jax import lax
from jax.experimental import pallas as pl
from jax.experimental.pallas import tpu as pltpu
from jax.sharding import PartitionSpec as P

HD = 128
FRAME = 128
V_DOWN = 2.0 ** -12
MIB = 1024 * 1024
CHUNK = 512
GROUP = 4
RING = 8
PLANES = (0, -1, -2, -3, 4, 1, 2, 3)

SMEM = pl.BlockSpec(memory_space=pltpu.SMEM)
VMEM = pl.BlockSpec(memory_space=pltpu.VMEM)
HBM = pl.BlockSpec(memory_space=pl.ANY)


def ring(n, k):
    return [(i, (i + k) % n) for i in range(n)]


def planes(k):
    return [(i * 8 + s, (i + k * (1 - 2 * (s % 2))) % RING * 8 + s) for i in range(RING) for s in range(8)]


Y_UP = [(s, (s + 2) % 8) for s in range(8)]
Y_DOWN = [(s, (s - 2) % 8) for s in range(8)]
Y_FAR = [(s, (s + 4) % 8) for s in range(8)]
CORE = [(s, s ^ 1) for s in range(8)]


def pick_kernel(info, *refs):
    sources, square = refs[:4], refs[4]
    out_a, out_b, sem = refs[-3:]
    tenants, rows, width = out_a.shape
    copies = []
    for j in range(tenants):
        step, slot = info[6 + j] // 4, info[6 + j] % 4
        for n, target in enumerate((out_a.at[j], out_b.at[j, :, pl.ds(0, width)])):
            span = pl.ds(n * width, width)

            def send(source, index, target=target, span=span, j=j, n=n):
                pltpu.make_async_copy(source.at[index, :, span], target, sem.at[n, j]).start()

            for i, source in enumerate(sources):
                pl.when(step == i)(functools.partial(send, source, slot))
            copies.append(pltpu.make_async_copy(sources[0].at[0, :, span], target, sem.at[n, j]))
    for j in range(2):
        part = square[j * rows:(j + 1) * rows, :]
        upper = part.astype(out_b.dtype)
        out_b[j, :, width:] = upper
        out_b[2 + j, :, width:] = (part - upper.astype(jnp.float32)).astype(out_b.dtype)
    for copy in copies:
        copy.wait()


def pick(info, parts, square, weight):
    n, rows, width = parts[0].shape
    return pl.pallas_call(
        pick_kernel,
        out_shape=(
            jax.ShapeDtypeStruct((n, rows, width // 2), parts[0].dtype),
            jax.ShapeDtypeStruct((n, rows, width // 2 + HD), parts[0].dtype),
        ),
        in_specs=[SMEM] + [HBM] * 4 + [VMEM, HBM],
        out_specs=[VMEM] * 2,
        scratch_shapes=[pltpu.SemaphoreType.DMA((2, n))],
        compiler_params=pltpu.CompilerParams(vmem_limit_bytes=48 * MIB),
        name="pick",
    )(info, *parts, square, weight)


def multiply(blocks, weight, start, total, weight_buf, sem):
    steps = range(weight_buf.shape[0])
    loads = [
        pltpu.make_async_copy(weight.at[pl.ds(start + i * CHUNK, CHUNK)], weight_buf.at[i], sem.at[i])
        for i in steps
    ]
    for load in loads:
        load.start()
    for i in steps:
        rows = jnp.concatenate([block[:, i * CHUNK:(i + 1) * CHUNK] for block in blocks], axis=0)
        loads[i].wait()
        total[...] += jnp.dot(rows, weight_buf[i], preferred_element_type=jnp.float32)


def first_kernel(*refs):
    total, weight_buf, sem = refs[-3:]
    total[...] = jnp.zeros_like(total)
    multiply(refs[:RING], refs[RING], 0, total, weight_buf, sem)


def project_first(blocks, weight):
    width, both = weight.shape
    rows = RING * blocks[0].shape[0]
    return pl.pallas_call(
        first_kernel,
        out_shape=jax.ShapeDtypeStruct((rows, both), jnp.float32),
        in_specs=[VMEM] * len(blocks) + [HBM],
        out_specs=VMEM,
        scratch_shapes=[
            pltpu.VMEM((width // 2 // CHUNK, CHUNK, both), jnp.bfloat16),
            pltpu.SemaphoreType.DMA((width // 2 // CHUNK,)),
        ],
        compiler_params=pltpu.CompilerParams(vmem_limit_bytes=48 * MIB),
        cost_estimate=pl.CostEstimate(flops=rows * width * both, bytes_accessed=width * both, transcendentals=0),
        name="project_first",
    )(*blocks, weight)


def project_kernel(info, gain, *refs):
    n = RING
    blocks, weight, first = refs[:n], refs[n], refs[n + 1]
    out, squares, query_total, weight_buf, total, raw, weight_sem = refs[-7:]
    width = weight.shape[0] // 2
    total[...] = first[...]
    multiply(blocks, weight, width, total, weight_buf, weight_sem)
    riders = [block[:, width:].astype(jnp.float32) for block in blocks]
    query_total[...] = sum(rider[:16] + rider[16:] for rider in riders)
    columns = out.shape[-1] // 2
    enc, seq = info[0], info[1]
    place = lax.broadcasted_iota(jnp.int32, (8, columns), 0)
    way = 1 - 2 * lax.rem(seq, 2)
    for i, offset in enumerate(PLANES):
        plane = lax.rem(enc + way * offset + RING, RING)
        for t in range(4):
            both = total[32 * i + 8 * t:32 * i + 8 * t + 8, :]
            live = plane * 64 + seq * 8 + place < info[2 + t]
            raw[t, plane] = both[:, :columns]
            out[t, plane, :, :columns] = (both[:, :columns] * gain[...][None, :]).astype(out.dtype)
            out[t, plane, :, columns:] = jnp.where(
                live, both[:, columns:] * V_DOWN, 0.0
            ).astype(out.dtype)
    square = raw[...].reshape(256, columns)
    square = square * square
    upper = square.astype(jnp.bfloat16)
    lower = (square - upper.astype(jnp.float32)).astype(jnp.bfloat16)
    ones = jnp.ones((8, columns), jnp.bfloat16)
    across = (((1,), (1,)), ((), ()))
    summed = lax.dot_general(
        ones, upper, across, preferred_element_type=jnp.float32
    ) + lax.dot_general(ones, lower, across, preferred_element_type=jnp.float32)
    for i in range(0, squares.shape[0], 8):
        squares[i:i + 8] = summed.reshape(8, 1, 256)


def project(info, gain, blocks, weight, first):
    width, both = weight.shape
    return pl.pallas_call(
        project_kernel,
        out_shape=(
            jax.ShapeDtypeStruct((4, 8, 8, both), jnp.bfloat16),
            jax.ShapeDtypeStruct((64, 1, 256), jnp.float32),
            jax.ShapeDtypeStruct((16, HD), jnp.float32),
        ),
        in_specs=[SMEM] + [VMEM] * (len(blocks) + 1) + [HBM, VMEM],
        out_specs=[VMEM] * 3,
        scratch_shapes=[
            pltpu.VMEM((width // 2 // CHUNK, CHUNK, both), jnp.bfloat16),
            pltpu.VMEM((256, both), jnp.float32),
            pltpu.VMEM((4, 8, 8, both // 2), jnp.float32),
            pltpu.SemaphoreType.DMA((width // 2 // CHUNK,)),
        ],
        compiler_params=pltpu.CompilerParams(vmem_limit_bytes=48 * MIB),
        cost_estimate=pl.CostEstimate(
            flops=256 * width * both, bytes_accessed=width * both, transcendentals=0
        ),
        name="project",
    )(info, gain, *blocks, weight, first)


def total_kernel(piece, squares, out, total):
    for i in range(8):
        row = squares[i]
        for plane in range(1, 8):
            row = row + squares[8 * plane + i]
        total[i:i + 1, :] = row


def key_sums(piece, squares):
    return pl.pallas_call(
        total_kernel,
        out_shape=(jax.ShapeDtypeStruct(piece.shape, piece.dtype), jax.ShapeDtypeStruct((8, 256), jnp.float32)),
        in_specs=[HBM, VMEM],
        out_specs=[HBM, VMEM],
        input_output_aliases={0: 0},
        compiler_params=pltpu.CompilerParams(vmem_limit_bytes=4 * MIB),
        name="key_sums",
    )(piece, squares)


def scale_kernel(width, queries, gain, query_total, out):
    scale = jnp.transpose(lax.rsqrt(query_total[...] / width + 1e-06))
    for f in range(queries.shape[0] // FRAME):
        rows = slice(f * FRAME, (f + 1) * FRAME)
        out[rows, :] = (
            queries[rows, :].astype(jnp.float32) * scale[:, f:f + 1] * gain[...][None, :] * HD ** (-0.5)
        ).astype(out.dtype)


def scale_queries(width, queries, gain, query_total):
    return pl.pallas_call(
        functools.partial(scale_kernel, width),
        out_shape=jax.ShapeDtypeStruct(queries.shape, queries.dtype),
        in_specs=[VMEM] * 3,
        out_specs=VMEM,
        compiler_params=pltpu.CompilerParams(vmem_limit_bytes=12 * MIB),
        name="scale_queries",
    )(queries, gain, query_total)


def attend_kernel(width, info, q_buf, key_total, *refs):
    parts, out = refs[:8], refs[8]
    o_buf, k_buf, v_buf, scale_buf, sem = refs[9:]
    seq, heads = info[1], q_buf.shape[1] // HD
    columns = heads * HD
    frames = q_buf.shape[0] // FRAME

    def piece_seq(piece):
        y, c = seq // 2, seq % 2
        kind = piece % 4
        shift = jnp.where(kind == 0, 0, jnp.where(kind == 1, 3, jnp.where(kind == 2, 1, 2)))
        return 2 * ((y + shift) % 4) + (c + piece // 4) % 2

    def position(shape, axis):
        key = lax.broadcasted_iota(jnp.int32, shape, axis)
        return key // 8 % 8 * 64 + piece_seq(key // 64) * 8 + key % 8

    down, across = position((512, HD), 0), position((1, 512), 1)
    totals = [key_total[pl.ds(piece_seq(p), 1), :] for p in range(8)]
    scales = [lax.rsqrt(total / width + 1e-06) * math.log2(math.e) for total in totals]
    for t in range(4):
        live = jnp.where(down < info[2 + t], 1.0, 0.0).astype(v_buf.dtype)
        row = jnp.concatenate([scale[:, t * 64:t * 64 + 64] for scale in scales], axis=1)
        scale_buf[t:t + 1, :] = jnp.where(across < info[2 + t], row, 0.0)
        for p in range(8):
            spot = slice(64 * p, 64 * p + 64)
            k_buf[t, spot, :] = parts[p][t, :, :columns]
            for h in range(heads):
                v_buf[h, t, spot, :HD] = parts[p][t, :, columns + h * HD:columns + (h + 1) * HD]
        for h in range(heads):
            v_buf[h, t, :, HD:] = live

    def frame_copy(f):
        rows = pl.ds(pl.multiple_of(f * FRAME, FRAME), FRAME)
        return pltpu.make_async_copy(o_buf.at[rows], out.at[rows], sem.at[f])

    for t in range(4):
        first, last = info[10 + t], info[11 + t]

        def one(i, carry, t=t, first=first, last=last):
            frame = first + GROUP * i
            base = jnp.minimum(frame, frames - GROUP)
            rows = pl.ds(pl.multiple_of(base * FRAME, FRAME), GROUP * FRAME)
            places = [
                pl.ds(pl.multiple_of(jnp.where(base + g < frame, frames, base + g) * FRAME, FRAME), FRAME)
                for g in range(GROUP)
            ]
            for h in range(heads):
                lanes = slice(h * HD, (h + 1) * HD)
                scores = lax.dot_general(
                    q_buf[rows, lanes], k_buf[t, :, lanes], (((1,), (1,)), ((), ())),
                    preferred_element_type=jnp.float32,
                )
                raised = jnp.exp2(scores * scale_buf[t:t + 1, :]).astype(jnp.bfloat16)
                mixed = jnp.dot(raised, v_buf[h, t], preferred_element_type=jnp.float32)
                result = (mixed[:, :HD] * (1.0 / mixed[:, HD:]) * (1.0 / V_DOWN)).astype(o_buf.dtype)
                for g, place in enumerate(places):
                    o_buf[place, lanes] = result[g * FRAME:(g + 1) * FRAME]
            for g in range(GROUP):

                @pl.when(frame + g < last)
                def _(g=g):
                    frame_copy(frame + g).start()

            return carry

        lax.fori_loop(0, (last - first + GROUP - 1) // GROUP, one, 0)
    for f in range(frames):
        frame_copy(f).wait()


def attend(width, info, queries, key_total, parts):
    rows, columns = queries.shape
    return pl.pallas_call(
        functools.partial(attend_kernel, width),
        out_shape=jax.ShapeDtypeStruct((rows, columns), queries.dtype),
        in_specs=[SMEM] + [VMEM] * 10,
        out_specs=HBM,
        scratch_shapes=[
            pltpu.VMEM((rows + FRAME, columns), queries.dtype),
            pltpu.VMEM((4, 512, columns), queries.dtype),
            pltpu.VMEM((columns // HD, 4, 512, 2 * HD), queries.dtype),
            pltpu.VMEM((8, 512), jnp.float32),
            pltpu.SemaphoreType.DMA((rows // FRAME,)),
        ],
        compiler_params=pltpu.CompilerParams(vmem_limit_bytes=20 * MIB),
        cost_estimate=pl.CostEstimate(flops=4 * rows * columns * 512, bytes_accessed=4 * rows * columns, transcendentals=0),
        name="attend",
    )(info, queries, key_total, *parts)


def local(queries, text, kv_weight, query_gain, key_gain, prompt_len, served, frame_slot):
    columns = queries.shape[1]
    full_width = columns * 8
    enc, rep, seq = (lax.axis_index(a) for a in ("enc", "rep", "seq"))
    mine = lax.dynamic_slice_in_dim(served, rep * 4, 4)
    code = (mine // 4 - rep + 4) % 4 * 4 + mine % 4
    bounds = jnp.sum(frame_slot.reshape(1, -1) < jnp.arange(5, dtype=jnp.int32)[:, None], axis=1, dtype=jnp.int32)
    info = jnp.concatenate([jnp.stack([enc, seq]).astype(jnp.int32), prompt_len[mine], code, bounds])
    query_float = queries.astype(jnp.float32)
    query_square = jnp.sum(query_float * query_float, axis=-1).reshape(-1, HD)
    weight = kv_weight.reshape(kv_weight.shape[0], 2 * columns)

    parts = [text] + [lax.ppermute(text, "rep", ring(4, k)) for k in (-1, 2, 1)]
    blocks = [picked.reshape(32, picked.shape[2]) for picked in pick(info, parts, query_square, weight)]

    ups, downs = [[b] for b in blocks], [[b] for b in blocks]
    for i in range(4):
        for n in range(2):
            if n == 0 or i < 3:
                ups[n].append(lax.ppermute(ups[n][-1], ("enc", "seq"), planes(1)))
            if n == 1 or i < 3:
                downs[n].append(lax.ppermute(downs[n][-1], ("enc", "seq"), planes(-1)))
    first = project_first(ups[0] + downs[0][1:], weight)
    held = ups[1] + [downs[1][4]] + downs[1][1:4]
    pair, squares, query_total = project(info, key_gain, held, weight, first)
    pair = pair.reshape(4, 64, 2 * columns)

    squares = lax.all_to_all(squares, ("enc", "seq"), 0, 0, tiled=True)
    ahead, behind, far = (lax.ppermute(pair, "seq", p) for p in (Y_UP, Y_DOWN, Y_FAR))
    far, key_total = key_sums(far, squares)
    parts = [pair, ahead, behind, far]
    parts = parts + [lax.ppermute(part, "seq", CORE) for part in parts]
    scaled = scale_queries(full_width, queries, query_gain, query_total)
    return attend(full_width, info, scaled, key_total, parts)


def solution(mesh):
    placed = (
        P(("rep", "seq"), "enc"),
        P("rep", ("enc", "seq"), None),
        P(None, None, "enc"),
        P("enc"),
        P("enc"),
        P(),
        P(),
        P("rep", "seq"),
    )
    return jax.shard_map(
        local, mesh=mesh, in_specs=placed, out_specs=P(("rep", "seq"), "enc"), check_vma=False
    )
```

time: 102 us -> 96.4 us (0.945)
  waiting for transfers between devices: 23.8 us -> 14.7 us
  starting transfers between devices: 47.5 us -> 52.4 us
  other arithmetic: 3.39 us -> 1.26 us
  Pallas kernels: 16.7 us -> 18.8 us
    all_to_all x1, waiting for transfers between devices: 9.39 us -> 2.15 us  [local(): squares = lax.all_to_all(squares, ('enc', 'seq'), 0, 0, tiled=True)]
    ppermute x4, starting transfers between devices: 1.61 us -> 8.54 us  [local(): parts = parts + [lax.ppermute(part, 'seq', CORE) for part in parts]]
    pallas_call x2 -> x3, Pallas kernels: 1.82 us -> 4.96 us  [the longest x1 3.11 us: project_first(): pl.pallas_call(first_kernel, out_shape=jax.ShapeDtypeStruct((rows, both),...]
    pallas_call x1, Pallas kernels: 6.33 us -> 4.56 us  [project(): pl.pallas_call(project_kernel, out_shape=(jax.ShapeDtypeStruct((4, 8, 8,...]
    reduce_sum x1, other arithmetic: 1.79 us -> 0.39 us  [local(): query_square = jnp.sum(query_float * query_float, axis=-1).reshape(-1, HD)]
    ppermute x3, starting transfers between devices: 5.68 us -> 4.46 us  [local(): lax.ppermute(pair, 'seq', p)]
    ppermute x4, waiting for transfers between devices: 1.18 us -> 0.02 us  [local(): parts = parts + [lax.ppermute(part, 'seq', CORE) for part in parts]]
    slice x1 -> x0, local copies, waits for them, and re-layouts: 1.03 us -> none  [local(): part = text[:, :, n * half:(n + 1) * half]]
  transfers between devices with their start and end apart: 28 -> 25, of which waited for: 8 -> 8; matrix products, arithmetic and copies ran while one was open for 11% -> 10% of each run, Pallas kernels for 3% -> 5%
where the time goes in v4:
time: 96.4 us; the launch traced here: 96.7 us
  starting transfers between devices  52.4 us (54%)
  Pallas kernels  18.8 us (20%)
  waiting for transfers between devices  14.7 us (15%)
  local copies, waits for them, and re-layouts  9.2 us (10%)
  other arithmetic  1.26 us (1%)
    ppermute x7, starting transfers between devices, local(): ups[n].append(lax.ppermute(ups[n][-1], ('enc', 'seq'), planes(1)))  20.6 us
    all_to_all x1, starting transfers between devices, local(): squares = lax.all_to_all(squares, ('enc', 'seq'), 0, 0, tiled=True)  12.1 us
    ppermute x4, starting transfers between devices, local(): parts = parts + [lax.ppermute(part, 'seq', CORE) for part in parts]  8.54 us
    unnamed x13, local copies, waits for them, and re-layouts  8.49 us
    pallas_call x1, Pallas kernels, attend(): pl.pallas_call(functools.partial(attend_kernel, width), out_shape=jax.Sha...  8.46 us
    ppermute x7, waiting for transfers between devices, local(): downs[n].append(lax.ppermute(downs[n][-1], ('enc', 'seq'), planes(-1)))  5.23 us
    ppermute x3, starting transfers between devices, local(): parts = [text] + [lax.ppermute(text, 'rep', ring(4, k)) for k in (-1, 2, 1)]  5.04 us
    pallas_call x1, Pallas kernels, project(): pl.pallas_call(project_kernel, out_shape=(jax.ShapeDtypeStruct((4, 8, 8,...  4.56 us
  transfers between devices with their start and end apart: 25, of which 8 were waited for; matrix products, arithmetic and copies ran while one was open for 10% of the time, Pallas kernels for 5%

profile of v4, /device:TPU:1, one launch (start us, length us, event | category | flops | bytes accessed | tf_op | source)
XLA Modules:
  0.0 96.7 jit_solution(11679823623077626665)
XLA Ops:
  0.0 3.6 %collective-permute-start.1 = (bf16[4,8,5120]{2,1,0:T(8,128)(2,1)}, bf16[4,8,5120]{2,1,0:T(8,128)(2,1)S(1)}, u32[]{:S(2)}, u32[]{:S(2)}) collective-permute-start(bf16[4,8,5120]{2,1,0:T(8,128)(2,1)} %refs_0_.1), channel_id=1, source_target_pairs={{0,16},{8,24},{16,0},{24,8},{1,17},{9,25},{17,1},{25,9},{2,18},{10... | collective-permute-start | bytes 983048 | tf_op jit(solution)/shard_map/ppermute | solution.py:322
  3.6 0.9 collective-permute-start
  4.4 0.6 collective-permute-start.2
  5.0 0.7 fusion
  5.8 0.0 copy-start.5
  5.8 0.0 copy-start.1
  5.8 0.0 copy-start.2
  5.8 7.8 %copy.10 = bf16[640,8,2,384]{3,1,2,0:T(8,128)(2,1)} copy(bf16[640,8,2,384]{3,2,1,0:T(2,128)(2,1)} %bitcast.24) | data formatting | bytes 15728640
  13.6 0.6 gather_fusion
  14.3 0.1 convert_reduce_fusion
  14.4 0.1 concatenate.3.info
  14.5 0.4 multiply_reduce_fusion
  14.9 0.0 collective-permute-done.1.refs_2_
  14.9 3.5 %collective-permute-done.refs_1_ = bf16[4,8,5120]{2,1,0:T(8,128)(2,1)S(1)} collective-permute-done((bf16[4,8,5120]{2,1,0:T(8,128)(2,1)}, bf16[4,8,5120]{2,1,0:T(8,128)(2,1)S(1)}, u32[]{:S(2)}, u32[]{:S(2)}) %collective-permute-start) | collective-permute-done | bytes 327712 | tf_op jit(solution)/shard_map/ppermute | solution.py:322
  18.4 0.0 collective-permute-done.2.refs_3_
  18.4 1.2 %pick.1 = (bf16[4,8,2560]{2,1,0:T(8,128)(2,1)S(1)}, bf16[4,8,2688]{2,1,0:T(8,128)(2,1)S(1)}) custom-call(s32[15]{0:T(128)S(1)} %concatenate.3.info, bf16[4,8,5120]{2,1,0:T(8,128)(2,1)S(1)} %copy-done.2, bf16[4,8,5120]{2,1,0:T(8,128)(2,1)S(1)} %collective-permute-done.refs_1_, bf16[4,8,5120]{2,1,0:T(8,128)(2,1)S(1)} %collective-permute-done.1.refs_2_, ...), custom_call_target="tpu_custom_call" | custom-call | tf_op jit(solution)/shard_map/pick/pallas_call | solution.py:66
  19.6 6.5 %collective-permute-start.10 = (bf16[32,2560]{1,0:T(8,128)(2,1)S(1)}, bf16[32,2560]{1,0:T(8,128)(2,1)S(1)}, u32[]{:S(2)}, u32[]{:S(2)}) collective-permute-start(bf16[32,2560]{1,0:T(8,128)(2,1)S(1)} %bitcast.17), channel_id=1, source_target_pairs={{0,32},{1,225},{2,34},{3,227},{4,36},{5,229},{6,38},{7,231},{32,64... | collective-permute-start | bytes 491528 | tf_op jit(solution)/shard_map/ppermute | solution.py:329
  26.1 0.0 collective-permute-start.6
  26.1 0.0 collective-permute-start.14
  26.1 2.8 %collective-permute-done.10.refs_1_ = bf16[32,2560]{1,0:T(8,128)(2,1)S(1)} collective-permute-done((bf16[32,2560]{1,0:T(8,128)(2,1)S(1)}, bf16[32,2560]{1,0:T(8,128)(2,1)S(1)}, u32[]{:S(2)}, u32[]{:S(2)}) %collective-permute-start.10) | collective-permute-done | bytes 163872 | tf_op jit(solution)/shard_map/ppermute | solution.py:329
  28.9 3.4 %collective-permute-start.11 = (bf16[32,2560]{1,0:T(8,128)(2,1)S(1)}, bf16[32,2560]{1,0:T(8,128)(2,1)S(1)}, u32[]{:S(2)}, u32[]{:S(2)}) collective-permute-start(bf16[32,2560]{1,0:T(8,128)(2,1)S(1)} %collective-permute-done.10.refs_1_), channel_id=1, source_target_pairs={{0,32},{1,225},{2,34},{3,227},{4,36},{5,229},{6,38},{7,231},{32,64... | collective-permute-start | bytes 491528 | tf_op jit(solution)/shard_map/ppermute | solution.py:329
  32.3 0.0 collective-permute-start.3
  32.3 0.0 collective-permute-done.6.refs_5_
  32.3 1.4 %collective-permute-start.7 = (bf16[32,2688]{1,0:T(8,128)(2,1)S(1)}, bf16[32,2688]{1,0:T(8,128)(2,1)S(1)}, u32[]{:S(2)}, u32[]{:S(2)}) collective-permute-start(bf16[32,2688]{1,0:T(8,128)(2,1)S(1)} %collective-permute-done.6.refs_5_), channel_id=1, source_target_pairs={{0,224},{1,33},{2,226},{3,35},{4,228},{5,37},{6,230},{7,39},{32,0}... | collective-permute-start | bytes 516104 | tf_op jit(solution)/shard_map/ppermute | solution.py:331
  33.8 0.0 collective-permute-done.14.refs_5_
  33.8 0.1 collective-permute-start.15
  33.9 0.7 collective-permute-done.11.refs_2_
  34.6 3.1 %collective-permute-start.12 = (bf16[32,2560]{1,0:T(8,128)(2,1)S(1)}, bf16[32,2560]{1,0:T(8,128)(2,1)S(1)}, u32[]{:S(2)}, u32[]{:S(2)}) collective-permute-start(bf16[32,2560]{1,0:T(8,128)(2,1)S(1)} %collective-permute-done.11.refs_2_), channel_id=1, source_target_pairs={{0,32},{1,225},{2,34},{3,227},{4,36},{5,229},{6,38},{7,231},{32,64... | collective-permute-start | bytes 491528 | tf_op jit(solution)/shard_map/ppermute | solution.py:329
  37.7 0.3 collective-permute-done.3.refs_1_
  38.0 3.2 %collective-permute-start.4 = (bf16[32,2688]{1,0:T(8,128)(2,1)S(1)}, bf16[32,2688]{1,0:T(8,128)(2,1)S(1)}, u32[]{:S(2)}, u32[]{:S(2)}) collective-permute-start(bf16[32,2688]{1,0:T(8,128)(2,1)S(1)} %collective-permute-done.3.refs_1_), channel_id=1, source_target_pairs={{0,32},{1,225},{2,34},{3,227},{4,36},{5,229},{6,38},{7,231},{32,64... | collective-permute-start | bytes 516104 | tf_op jit(solution)/shard_map/ppermute | solution.py:329
  41.2 0.0 collective-permute-done.7.refs_6_
  41.2 0.0 collective-permute-start.8
  41.2 1.1 %collective-permute-done.15.refs_6_ = bf16[32,2560]{1,0:T(8,128)(2,1)S(1)} collective-permute-done((bf16[32,2560]{1,0:T(8,128)(2,1)S(1)}, bf16[32,2560]{1,0:T(8,128)(2,1)S(1)}, u32[]{:S(2)}, u32[]{:S(2)}) %collective-permute-start.15) | collective-permute-done | bytes 163872 | tf_op jit(solution)/shard_map/ppermute | solution.py:331
  42.3 0.0 collective-permute-start.16
  42.3 0.0 collective-permute-done.12.refs_3_
  42.3 2.8 %collective-permute-start.13 = (bf16[32,2560]{1,0:T(8,128)(2,1)S(1)}, bf16[32,2560]{1,0:T(8,128)(2,1)S(1)}, u32[]{:S(2)}, u32[]{:S(2)}) collective-permute-start(bf16[32,2560]{1,0:T(8,128)(2,1)S(1)} %collective-permute-done.12.refs_3_), channel_id=1, source_target_pairs={{0,32},{1,225},{2,34},{3,227},{4,36},{5,229},{6,38},{7,231},{32,64... | collective-permute-start | bytes 491528 | tf_op jit(solution)/shard_map/ppermute | solution.py:329
  45.2 0.0 collective-permute-done.4.refs_2_
  45.2 1.6 %collective-permute-start.5 = (bf16[32,2688]{1,0:T(8,128)(2,1)S(1)}, bf16[32,2688]{1,0:T(8,128)(2,1)S(1)}, u32[]{:S(2)}, u32[]{:S(2)}) collective-permute-start(bf16[32,2688]{1,0:T(8,128)(2,1)S(1)} %collective-permute-done.4.refs_2_), channel_id=1, source_target_pairs={{0,32},{1,225},{2,34},{3,227},{4,36},{5,229},{6,38},{7,231},{32,64... | collective-permute-start | bytes 516104 | tf_op jit(solution)/shard_map/ppermute | solution.py:329
  46.7 1.3 %collective-permute-done.8.refs_7_ = bf16[32,2688]{1,0:T(8,128)(2,1)S(1)} collective-permute-done((bf16[32,2688]{1,0:T(8,128)(2,1)S(1)}, bf16[32,2688]{1,0:T(8,128)(2,1)S(1)}, u32[]{:S(2)}, u32[]{:S(2)}) %collective-permute-start.8) | collective-permute-done | bytes 172064 | tf_op jit(solution)/shard_map/ppermute | solution.py:331
  48.0 0.0 collective-permute-start.9
  48.0 2.8 %collective-permute-done.16.refs_7_ = bf16[32,2560]{1,0:T(8,128)(2,1)S(1)} collective-permute-done((bf16[32,2560]{1,0:T(8,128)(2,1)S(1)}, bf16[32,2560]{1,0:T(8,128)(2,1)S(1)}, u32[]{:S(2)}, u32[]{:S(2)}) %collective-permute-start.16) | collective-permute-done | bytes 163872 | tf_op jit(solution)/shard_map/ppermute | solution.py:331
  50.8 0.0 collective-permute-done.13.refs_4_
  50.8 3.1 %project_first.1.refs_9_ = f32[256,768]{1,0:T(8,128)S(1)} custom-call(bf16[32,2560]{1,0:T(8,128)(2,1)S(1)} %bitcast.19, bf16[32,2560]{1,0:T(8,128)(2,1)S(1)} %collective-permute-done.10.refs_1_, bf16[32,2560]{1,0:T(8,128)(2,1)S(1)} %collective-permute-done.11.refs_2_, bf16[32,2560]{1,0:T(8,128)(2,1)S(1)} %collective-permute-done.12.refs_3_, ...), custom_call_target="tpu_custom_call" | custom-call | flops 1006632960 | bytes 3932160 | tf_op jit(solution)/shard_map/project_first/pallas_call | solution.py:103
  54.0 0.0 collective-permute-done.9.refs_4_
  54.0 4.6 %project.1 = (bf16[4,8,8,768]{3,2,1,0:T(8,128)(2,1)S(1)}, f32[64,1,256]{2,1,0:T(1,128)}, f32[16,128]{1,0:T(8,128)S(1)}) custom-call(s32[15]{0:T(128)S(1)} %concatenate.3.info, f32[384]{0:T(512)S(1)} %copy-done.4, bf16[32,2688]{1,0:T(8,128)(2,1)S(1)} %bitcast.16, bf16[32,2688]{1,0:T(8,128)(2,1)S(1)} %collective-permute-done.3.refs_1_, ...), custom_call_target="tpu_custom_call" | custom-call | flops 1006632960 | bytes 3932160 | tf_op jit(solution)/shard_map/project/pallas_call | solution.py:156
  58.6 2.8 %collective-permute-start.19 = (bf16[4,64,768]{2,1,0:T(8,128)(2,1)S(1)}, bf16[4,64,768]{2,1,0:T(8,128)(2,1)S(1)}, u32[]{:S(2)}, u32[]{:S(2)}) collective-permute-start(bf16[4,64,768]{2,1,0:T(8,128)(2,1)S(1)} %bitcast.9), channel_id=1, source_target_pairs={{0,6},{1,7},{2,0},{3,1},{4,2},{5,3},{6,4},{7,5},{8,14},{9,15},{10,... | collective-permute-start | bytes 1179656 | tf_op jit(solution)/shard_map/ppermute | solution.py:338
  61.4 0.0 collective-permute-start.18
  61.4 1.6 %collective-permute-start.17 = (bf16[4,64,768]{2,1,0:T(8,128)(2,1)S(1)}, bf16[4,64,768]{2,1,0:T(8,128)(2,1)S(1)}, u32[]{:S(2)}, u32[]{:S(2)}) collective-permute-start(bf16[4,64,768]{2,1,0:T(8,128)(2,1)S(1)} %bitcast.11), channel_id=1, source_target_pairs={{0,4},{1,5},{2,6},{3,7},{4,0},{5,1},{6,2},{7,3},{8,12},{9,13},{10,... | collective-permute-start | bytes 1179656 | tf_op jit(solution)/shard_map/ppermute | solution.py:338
  63.0 12.1 %all-to-all-start = ((f32[64,1,256]{2,1,0:T(1,128)}), f32[64,1,256]{2,1,0:T(1,128)}, u32[]{:S(2)}, u32[]{:S(2)}) async-start(f32[64,1,256]{2,1,0:T(1,128)} %get-tuple-element.16), calls=%async_computation | async-start | bytes 131072 | tf_op jit(solution)/shard_map/all_to_all | solution.py:337
  75.2 0.6 collective-permute-start.20
  75.8 0.0 collective-permute-done.19.refs_2_
  75.8 3.7 %collective-permute-start.22 = (bf16[4,64,768]{2,1,0:T(8,128)(2,1)S(1)}, bf16[4,64,768]{2,1,0:T(8,128)(2,1)}, u32[]{:S(2)}, u32[]{:S(2)}) collective-permute-start(bf16[4,64,768]{2,1,0:T(8,128)(2,1)S(1)} %collective-permute-done.19.refs_2_), channel_id=1, source_target_pairs={{0,1},{1,0},{2,3},{3,2},{4,5},{5,4},{6,7},{7,6},{8,9},{9,8},{10,11... | collective-permute-start | bytes 1179656 | tf_op jit(solution)/shard_map/ppermute | solution.py:341
  79.5 0.0 collective-permute-done.18.refs_1_
  79.5 3.6 %collective-permute-start.21 = (bf16[4,64,768]{2,1,0:T(8,128)(2,1)S(1)}, bf16[4,64,768]{2,1,0:T(8,128)(2,1)}, u32[]{:S(2)}, u32[]{:S(2)}) collective-permute-start(bf16[4,64,768]{2,1,0:T(8,128)(2,1)S(1)} %collective-permute-done.18.refs_1_), channel_id=1, source_target_pairs={{0,1},{1,0},{2,3},{3,2},{4,5},{5,4},{6,7},{7,6},{8,9},{9,8},{10,11... | collective-permute-start | bytes 1179656 | tf_op jit(solution)/shard_map/ppermute | solution.py:341
  83.0 2.2 %all-to-all-done.squares = f32[64,1,256]{2,1,0:T(1,128)} async-done(((f32[64,1,256]{2,1,0:T(1,128)}), f32[64,1,256]{2,1,0:T(1,128)}, u32[]{:S(2)}, u32[]{:S(2)}) %all-to-all-start) | async-done | bytes 65568 | tf_op jit(solution)/shard_map/all_to_all | solution.py:337
  85.2 0.0 collective-permute-done.17.piece
  85.2 0.9 key_sums.1
  86.0 0.7 collective-permute-start.23
  86.8 0.7 copy-done.3
  87.4 0.6 scale_queries.1.q_buf
  88.1 0.0 collective-permute-done.20.refs_4_
  88.1 0.0 collective-permute-done.22.refs_6_
  88.1 0.0 collective-permute-done.23.refs_7_
  88.1 8.5 %attend.1 = bf16[2048,384]{1,0:T(8,128)(2,1)} custom-call(s32[15]{0:T(128)S(1)} %concatenate.3.info, bf16[2048,384]{1,0:T(8,128)(2,1)S(1)} %scale_queries.1.q_buf, f32[8,256]{1,0:T(8,128)S(1)} %get-tuple-element.17.key_total, bf16[4,64,768]{2,1,0:T(8,128)(2,1)S(1)} %bitcast.13, bf16[4,64,768]{2,1,0:T(8,128)(2,1)S(1)} %collective-permute-done.18.refs_1_, ...), custom_call_target="tpu_custom_call" | custom-call | flops 1610612736 | bytes 3145728 | tf_op jit(solution)/shard_map/attend/pallas_call | solution.py:292
  (11 shorter events, 0.0 us)
Async XLA Ops:
  0.0 13.6 %copy-start = (s32[16]{0:T(128)S(1)}, s32[16]{0:T(128)}, u32[]{:S(2)}) copy-start(s32[16]{0:T(128)} %param.13) | copy-start | bytes 196
  0.0 14.9 %collective-permute-start.1 = (bf16[4,8,5120]{2,1,0:T(8,128)(2,1)}, bf16[4,8,5120]{2,1,0:T(8,128)(2,1)S(1)}, u32[]{:S(2)}, u32[]{:S(2)}) collective-permute-start(bf16[4,8,5120]{2,1,0:T(8,128)(2,1)} %refs_0_.1), channel_id=1, source_target_pairs={{0,16},{8,24},{16,0},{24,8},{1,17},{9,25},{17,1},{25,9},{2,18},{10... | collective-permute-start | bytes 983048 | tf_op jit(solution)/shard_map/ppermute | solution.py:322
  3.6 14.8 %collective-permute-start = (bf16[4,8,5120]{2,1,0:T(8,128)(2,1)}, bf16[4,8,5120]{2,1,0:T(8,128)(2,1)S(1)}, u32[]{:S(2)}, u32[]{:S(2)}) collective-permute-start(bf16[4,8,5120]{2,1,0:T(8,128)(2,1)} %refs_0_.1), channel_id=1, source_target_pairs={{0,24},{8,0},{16,8},{24,16},{1,25},{9,1},{17,9},{25,17},{2,26},{10... | collective-permute-start | bytes 983048 | tf_op jit(solution)/shard_map/ppermute | solution.py:322
  4.4 13.9 %collective-permute-start.2 = (bf16[4,8,5120]{2,1,0:T(8,128)(2,1)}, bf16[4,8,5120]{2,1,0:T(8,128)(2,1)S(1)}, u32[]{:S(2)}, u32[]{:S(2)}) collective-permute-start(bf16[4,8,5120]{2,1,0:T(8,128)(2,1)} %refs_0_.1), channel_id=1, source_target_pairs={{0,8},{8,16},{16,24},{24,0},{1,9},{9,17},{17,25},{25,1},{2,10},{10... | collective-permute-start | bytes 983048 | tf_op jit(solution)/shard_map/ppermute | solution.py:322
  5.8 8.5 %copy-start.5 = (s32[1,16]{1,0:T(1,128)S(1)}, s32[1,16]{1,0:T(1,128)}, u32[]{:S(2)}) copy-start(s32[1,16]{1,0:T(1,128)} %param.15) | copy-start | bytes 196
  5.8 8.6 %copy-start.1 = (bf16[2048,384]{1,0:T(8,128)(2,1)S(1)}, bf16[2048,384]{1,0:T(8,128)(2,1)}, u32[]{:S(2)}) copy-start(bf16[2048,384]{1,0:T(8,128)(2,1)} %queries.1) | copy-start | bytes 4718596
  5.8 12.5 %copy-start.2 = (bf16[4,8,5120]{2,1,0:T(8,128)(2,1)S(1)}, bf16[4,8,5120]{2,1,0:T(8,128)(2,1)}, u32[]{:S(2)}) copy-start(bf16[4,8,5120]{2,1,0:T(8,128)(2,1)} %refs_0_.1) | copy-start | bytes 983044
  19.6 9.3 %collective-permute-start.10 = (bf16[32,2560]{1,0:T(8,128)(2,1)S(1)}, bf16[32,2560]{1,0:T(8,128)(2,1)S(1)}, u32[]{:S(2)}, u32[]{:S(2)}) collective-permute-start(bf16[32,2560]{1,0:T(8,128)(2,1)S(1)} %bitcast.17), channel_id=1, source_target_pairs={{0,32},{1,225},{2,34},{3,227},{4,36},{5,229},{6,38},{7,231},{32,64... | collective-permute-start | bytes 491528 | tf_op jit(solution)/shard_map/ppermute | solution.py:329
  26.1 27.9 %copy-start.4 = (f32[384]{0:T(512)S(1)}, f32[384]{0:T(512)}, u32[]{:S(2)}) copy-start(f32[384]{0:T(512)} %gain.2) | copy-start | bytes 4612
  26.1 6.3 %collective-permute-start.6 = (bf16[32,2688]{1,0:T(8,128)(2,1)S(1)}, bf16[32,2688]{1,0:T(8,128)(2,1)S(1)}, u32[]{:S(2)}, u32[]{:S(2)}) collective-permute-start(bf16[32,2688]{1,0:T(8,128)(2,1)S(1)} %bitcast.14), channel_id=1, source_target_pairs={{0,224},{1,33},{2,226},{3,35},{4,228},{5,37},{6,230},{7,39},{32,0}... | collective-permute-start | bytes 516104 | tf_op jit(solution)/shard_map/ppermute | solution.py:331
  26.1 7.7 %collective-permute-start.14 = (bf16[32,2560]{1,0:T(8,128)(2,1)S(1)}, bf16[32,2560]{1,0:T(8,128)(2,1)S(1)}, u32[]{:S(2)}, u32[]{:S(2)}) collective-permute-start(bf16[32,2560]{1,0:T(8,128)(2,1)S(1)} %bitcast.18), channel_id=1, source_target_pairs={{0,224},{1,33},{2,226},{3,35},{4,228},{5,37},{6,230},{7,39},{32,0}... | collective-permute-start | bytes 491528 | tf_op jit(solution)/shard_map/ppermute | solution.py:331
  28.9 5.7 %collective-permute-start.11 = (bf16[32,2560]{1,0:T(8,128)(2,1)S(1)}, bf16[32,2560]{1,0:T(8,128)(2,1)S(1)}, u32[]{:S(2)}, u32[]{:S(2)}) collective-permute-start(bf16[32,2560]{1,0:T(8,128)(2,1)S(1)} %collective-permute-done.10.refs_1_), channel_id=1, source_target_pairs={{0,32},{1,225},{2,34},{3,227},{4,36},{5,229},{6,38},{7,231},{32,64... | collective-permute-start | bytes 491528 | tf_op jit(solution)/shard_map/ppermute | solution.py:329
  32.3 5.7 %collective-permute-start.3 = (bf16[32,2688]{1,0:T(8,128)(2,1)S(1)}, bf16[32,2688]{1,0:T(8,128)(2,1)S(1)}, u32[]{:S(2)}, u32[]{:S(2)}) collective-permute-start(bf16[32,2688]{1,0:T(8,128)(2,1)S(1)} %bitcast.15), channel_id=1, source_target_pairs={{0,32},{1,225},{2,34},{3,227},{4,36},{5,229},{6,38},{7,231},{32,64... | collective-permute-start | bytes 516104 | tf_op jit(solution)/shard_map/ppermute | solution.py:329
  32.3 8.9 %collective-permute-start.7 = (bf16[32,2688]{1,0:T(8,128)(2,1)S(1)}, bf16[32,2688]{1,0:T(8,128)(2,1)S(1)}, u32[]{:S(2)}, u32[]{:S(2)}) collective-permute-start(bf16[32,2688]{1,0:T(8,128)(2,1)S(1)} %collective-permute-done.6.refs_5_), channel_id=1, source_target_pairs={{0,224},{1,33},{2,226},{3,35},{4,228},{5,37},{6,230},{7,39},{32,0}... | collective-permute-start | bytes 516104 | tf_op jit(solution)/shard_map/ppermute | solution.py:331
  33.8 8.5 %collective-permute-start.15 = (bf16[32,2560]{1,0:T(8,128)(2,1)S(1)}, bf16[32,2560]{1,0:T(8,128)(2,1)S(1)}, u32[]{:S(2)}, u32[]{:S(2)}) collective-permute-start(bf16[32,2560]{1,0:T(8,128)(2,1)S(1)} %collective-permute-done.14.refs_5_), channel_id=1, source_target_pairs={{0,224},{1,33},{2,226},{3,35},{4,228},{5,37},{6,230},{7,39},{32,0}... | collective-permute-start | bytes 491528 | tf_op jit(solution)/shard_map/ppermute | solution.py:331
  34.6 7.8 %collective-permute-start.12 = (bf16[32,2560]{1,0:T(8,128)(2,1)S(1)}, bf16[32,2560]{1,0:T(8,128)(2,1)S(1)}, u32[]{:S(2)}, u32[]{:S(2)}) collective-permute-start(bf16[32,2560]{1,0:T(8,128)(2,1)S(1)} %collective-permute-done.11.refs_2_), channel_id=1, source_target_pairs={{0,32},{1,225},{2,34},{3,227},{4,36},{5,229},{6,38},{7,231},{32,64... | collective-permute-start | bytes 491528 | tf_op jit(solution)/shard_map/ppermute | solution.py:329
  38.0 7.2 %collective-permute-start.4 = (bf16[32,2688]{1,0:T(8,128)(2,1)S(1)}, bf16[32,2688]{1,0:T(8,128)(2,1)S(1)}, u32[]{:S(2)}, u32[]{:S(2)}) collective-permute-start(bf16[32,2688]{1,0:T(8,128)(2,1)S(1)} %collective-permute-done.3.refs_1_), channel_id=1, source_target_pairs={{0,32},{1,225},{2,34},{3,227},{4,36},{5,229},{6,38},{7,231},{32,64... | collective-permute-start | bytes 516104 | tf_op jit(solution)/shard_map/ppermute | solution.py:329
  41.2 6.8 %collective-permute-start.8 = (bf16[32,2688]{1,0:T(8,128)(2,1)S(1)}, bf16[32,2688]{1,0:T(8,128)(2,1)S(1)}, u32[]{:S(2)}, u32[]{:S(2)}) collective-permute-start(bf16[32,2688]{1,0:T(8,128)(2,1)S(1)} %collective-permute-done.7.refs_6_), channel_id=1, source_target_pairs={{0,224},{1,33},{2,226},{3,35},{4,228},{5,37},{6,230},{7,39},{32,0}... | collective-permute-start | bytes 516104 | tf_op jit(solution)/shard_map/ppermute | solution.py:331
  42.3 8.5 %collective-permute-start.16 = (bf16[32,2560]{1,0:T(8,128)(2,1)S(1)}, bf16[32,2560]{1,0:T(8,128)(2,1)S(1)}, u32[]{:S(2)}, u32[]{:S(2)}) collective-permute-start(bf16[32,2560]{1,0:T(8,128)(2,1)S(1)} %collective-permute-done.15.refs_6_), channel_id=1, source_target_pairs={{0,224},{1,33},{2,226},{3,35},{4,228},{5,37},{6,230},{7,39},{32,0}... | collective-permute-start | bytes 491528 | tf_op jit(solution)/shard_map/ppermute | solution.py:331
  42.3 8.5 %collective-permute-start.13 = (bf16[32,2560]{1,0:T(8,128)(2,1)S(1)}, bf16[32,2560]{1,0:T(8,128)(2,1)S(1)}, u32[]{:S(2)}, u32[]{:S(2)}) collective-permute-start(bf16[32,2560]{1,0:T(8,128)(2,1)S(1)} %collective-permute-done.12.refs_3_), channel_id=1, source_target_pairs={{0,32},{1,225},{2,34},{3,227},{4,36},{5,229},{6,38},{7,231},{32,64... | collective-permute-start | bytes 491528 | tf_op jit(solution)/shard_map/ppermute | solution.py:329
  45.2 8.8 %collective-permute-start.5 = (bf16[32,2688]{1,0:T(8,128)(2,1)S(1)}, bf16[32,2688]{1,0:T(8,128)(2,1)S(1)}, u32[]{:S(2)}, u32[]{:S(2)}) collective-permute-start(bf16[32,2688]{1,0:T(8,128)(2,1)S(1)} %collective-permute-done.4.refs_2_), channel_id=1, source_target_pairs={{0,32},{1,225},{2,34},{3,227},{4,36},{5,229},{6,38},{7,231},{32,64... | collective-permute-start | bytes 516104 | tf_op jit(solution)/shard_map/ppermute | solution.py:329
  48.0 5.9 %collective-permute-start.9 = (bf16[32,2688]{1,0:T(8,128)(2,1)S(1)}, bf16[32,2688]{1,0:T(8,128)(2,1)S(1)}, u32[]{:S(2)}, u32[]{:S(2)}) collective-permute-start(bf16[32,2688]{1,0:T(8,128)(2,1)S(1)} %collective-permute-done.8.refs_7_), channel_id=1, source_target_pairs={{0,224},{1,33},{2,226},{3,35},{4,228},{5,37},{6,230},{7,39},{32,0}... | collective-permute-start | bytes 516104 | tf_op jit(solution)/shard_map/ppermute | solution.py:331
  58.6 17.2 %collective-permute-start.19 = (bf16[4,64,768]{2,1,0:T(8,128)(2,1)S(1)}, bf16[4,64,768]{2,1,0:T(8,128)(2,1)S(1)}, u32[]{:S(2)}, u32[]{:S(2)}) collective-permute-start(bf16[4,64,768]{2,1,0:T(8,128)(2,1)S(1)} %bitcast.9), channel_id=1, source_target_pairs={{0,6},{1,7},{2,0},{3,1},{4,2},{5,3},{6,4},{7,5},{8,14},{9,15},{10,... | collective-permute-start | bytes 1179656 | tf_op jit(solution)/shard_map/ppermute | solution.py:338
  61.4 18.1 %collective-permute-start.18 = (bf16[4,64,768]{2,1,0:T(8,128)(2,1)S(1)}, bf16[4,64,768]{2,1,0:T(8,128)(2,1)S(1)}, u32[]{:S(2)}, u32[]{:S(2)}) collective-permute-start(bf16[4,64,768]{2,1,0:T(8,128)(2,1)S(1)} %bitcast.10), channel_id=1, source_target_pairs={{0,2},{1,3},{2,4},{3,5},{4,6},{5,7},{6,0},{7,1},{8,10},{9,11},{10,... | collective-permute-start | bytes 1179656 | tf_op jit(solution)/shard_map/ppermute | solution.py:338
  61.4 23.8 %collective-permute-start.17 = (bf16[4,64,768]{2,1,0:T(8,128)(2,1)S(1)}, bf16[4,64,768]{2,1,0:T(8,128)(2,1)S(1)}, u32[]{:S(2)}, u32[]{:S(2)}) collective-permute-start(bf16[4,64,768]{2,1,0:T(8,128)(2,1)S(1)} %bitcast.11), channel_id=1, source_target_pairs={{0,4},{1,5},{2,6},{3,7},{4,0},{5,1},{6,2},{7,3},{8,12},{9,13},{10,... | collective-permute-start | bytes 1179656 | tf_op jit(solution)/shard_map/ppermute | solution.py:338
  63.0 22.2 %all-to-all-start = ((f32[64,1,256]{2,1,0:T(1,128)}), f32[64,1,256]{2,1,0:T(1,128)}, u32[]{:S(2)}, u32[]{:S(2)}) async-start(f32[64,1,256]{2,1,0:T(1,128)} %get-tuple-element.16), calls=%async_computation | async-start | bytes 131072 | tf_op jit(solution)/shard_map/all_to_all | solution.py:337
  75.2 12.9 %collective-permute-start.20 = (bf16[4,64,768]{2,1,0:T(8,128)(2,1)S(1)}, bf16[4,64,768]{2,1,0:T(8,128)(2,1)S(1)}, u32[]{:S(2)}, u32[]{:S(2)}) collective-permute-start(bf16[4,64,768]{2,1,0:T(8,128)(2,1)S(1)} %bitcast.12), channel_id=1, source_target_pairs={{0,1},{1,0},{2,3},{3,2},{4,5},{5,4},{6,7},{7,6},{8,9},{9,8},{10,11... | collective-permute-start | bytes 1179656 | tf_op jit(solution)/shard_map/ppermute | solution.py:341
  75.8 12.3 %collective-permute-start.22 = (bf16[4,64,768]{2,1,0:T(8,128)(2,1)S(1)}, bf16[4,64,768]{2,1,0:T(8,128)(2,1)}, u32[]{:S(2)}, u32[]{:S(2)}) collective-permute-start(bf16[4,64,768]{2,1,0:T(8,128)(2,1)S(1)} %collective-permute-done.19.refs_2_), channel_id=1, source_target_pairs={{0,1},{1,0},{2,3},{3,2},{4,5},{5,4},{6,7},{7,6},{8,9},{9,8},{10,11... | collective-permute-start | bytes 1179656 | tf_op jit(solution)/shard_map/ppermute | solution.py:341
  79.5 8.6 %collective-permute-start.21 = (bf16[4,64,768]{2,1,0:T(8,128)(2,1)S(1)}, bf16[4,64,768]{2,1,0:T(8,128)(2,1)}, u32[]{:S(2)}, u32[]{:S(2)}) collective-permute-start(bf16[4,64,768]{2,1,0:T(8,128)(2,1)S(1)} %collective-permute-done.18.refs_1_), channel_id=1, source_target_pairs={{0,1},{1,0},{2,3},{3,2},{4,5},{5,4},{6,7},{7,6},{8,9},{9,8},{10,11... | collective-permute-start | bytes 1179656 | tf_op jit(solution)/shard_map/ppermute | solution.py:341
  86.0 2.1 %collective-permute-start.23 = (bf16[4,64,768]{2,1,0:T(8,128)(2,1)S(1)}, bf16[4,64,768]{2,1,0:T(8,128)(2,1)S(1)}, u32[]{:S(2)}, u32[]{:S(2)}) collective-permute-start(bf16[4,64,768]{2,1,0:T(8,128)(2,1)S(1)} %get-tuple-element.18.refs_3_), channel_id=1, source_target_pairs={{0,1},{1,0},{2,3},{3,2},{4,5},{5,4},{6,7},{7,6},{8,9},{9,8},{10,11... | collective-permute-start | bytes 1179656 | tf_op jit(solution)/shard_map/ppermute | solution.py:341
  86.7 0.7 copy-start.3

commit v5 on v4

--- a/solution.py
+++ b/solution.py
@@ -157,7 +157,7 @@
         project_kernel,
         out_shape=(
             jax.ShapeDtypeStruct((4, 8, 8, both), jnp.bfloat16),
-            jax.ShapeDtypeStruct((64, 1, 256), jnp.float32),
+            jax.ShapeDtypeStruct((32, 1, 256), jnp.float32),
             jax.ShapeDtypeStruct((16, HD), jnp.float32),
         ),
         in_specs=[SMEM] + [VMEM] * (len(blocks) + 1) + [HBM, VMEM],
@@ -177,11 +177,12 @@
 
 
 def total_kernel(piece, squares, out, total):
-    for i in range(8):
+    for i in range(4):
         row = squares[i]
         for plane in range(1, 8):
-            row = row + squares[8 * plane + i]
+            row = row + squares[4 * plane + i]
         total[i:i + 1, :] = row
+        total[i + 4:i + 5, :] = row
 
 
 def key_sums(piece, squares):
@@ -211,12 +212,12 @@
         out_shape=jax.ShapeDtypeStruct(queries.shape, queries.dtype),
         in_specs=[VMEM] * 3,
         out_specs=VMEM,
-        compiler_params=pltpu.CompilerParams(vmem_limit_bytes=12 * MIB),
+        compiler_params=pltpu.CompilerParams(vmem_limit_bytes=6 * MIB),
         name="scale_queries",
     )(queries, gain, query_total)
 
 
-def attend_kernel(width, info, q_buf, key_total, *refs):
+def attend_kernel(width, info, q_buf, key_total, core_total, *refs):
     parts, out = refs[:8], refs[8]
     o_buf, k_buf, v_buf, scale_buf, sem = refs[9:]
     seq, heads = info[1], q_buf.shape[1] // HD
@@ -234,7 +235,7 @@
         return key // 8 % 8 * 64 + piece_seq(key // 64) * 8 + key % 8
 
     down, across = position((512, HD), 0), position((1, 512), 1)
-    totals = [key_total[pl.ds(piece_seq(p), 1), :] for p in range(8)]
+    totals = [(core_total if p >= 4 else key_total)[pl.ds(piece_seq(p) // 2, 1), :] for p in range(8)]
     scales = [lax.rsqrt(total / width + 1e-06) * math.log2(math.e) for total in totals]
     for t in range(4):
         live = jnp.where(down < info[2 + t], 1.0, 0.0).astype(v_buf.dtype)
@@ -287,12 +288,12 @@
         frame_copy(f).wait()
 
 
-def attend(width, info, queries, key_total, parts):
+def attend(width, info, queries, key_total, core_total, parts):
     rows, columns = queries.shape
     return pl.pallas_call(
         functools.partial(attend_kernel, width),
         out_shape=jax.ShapeDtypeStruct((rows, columns), queries.dtype),
-        in_specs=[SMEM] + [VMEM] * 10,
+        in_specs=[SMEM] + [VMEM] * 11,
         out_specs=HBM,
         scratch_shapes=[
             pltpu.VMEM((rows + FRAME, columns), queries.dtype),
@@ -301,10 +302,10 @@
             pltpu.VMEM((8, 512), jnp.float32),
             pltpu.SemaphoreType.DMA((rows // FRAME,)),
         ],
-        compiler_params=pltpu.CompilerParams(vmem_limit_bytes=20 * MIB),
+        compiler_params=pltpu.CompilerParams(vmem_limit_bytes=12 * MIB),
         cost_estimate=pl.CostEstimate(flops=4 * rows * columns * 512, bytes_accessed=4 * rows * columns, transcendentals=0),
         name="attend",
-    )(info, queries, key_total, *parts)
+    )(info, queries, key_total, core_total, *parts)
 
 
 def local(queries, text, kv_weight, query_gain, key_gain, prompt_len, served, frame_slot):
@@ -334,13 +335,14 @@
     pair, squares, query_total = project(info, key_gain, held, weight, first)
     pair = pair.reshape(4, 64, 2 * columns)
 
-    squares = lax.all_to_all(squares, ("enc", "seq"), 0, 0, tiled=True)
+    same_core = [[e * 8 + 2 * y + c for e in range(8) for y in range(4)] for c in range(2)]
+    squares = lax.all_to_all(squares, ("enc", "seq"), 0, 0, axis_index_groups=same_core, tiled=True)
     ahead, behind, far = (lax.ppermute(pair, "seq", p) for p in (Y_UP, Y_DOWN, Y_FAR))
     far, key_total = key_sums(far, squares)
     parts = [pair, ahead, behind, far]
     parts = parts + [lax.ppermute(part, "seq", CORE) for part in parts]
     scaled = scale_queries(full_width, queries, query_gain, query_total)
-    return attend(full_width, info, scaled, key_total, parts)
+    return attend(full_width, info, scaled, key_total, lax.ppermute(key_total, "seq", CORE), parts)
 
 
 def solution(mesh):

time: 96.4 us -> 95.3 us (0.989)
  waiting for transfers between devices: 14.7 us -> 12.6 us
  starting transfers between devices: 52.4 us -> 53.8 us
  Pallas kernels: 18.8 us -> 17.7 us
    ppermute x4, starting transfers between devices: 8.54 us -> 16.6 us  [local(): parts = parts + [lax.ppermute(part, 'seq', CORE) for part in parts]]
    all_to_all x1, starting transfers between devices: 12.1 us -> 5.2 us  [local(): lax.all_to_all(squares, ('enc', 'seq'), 0, 0, axis_index_groups=same_core...]
    all_to_all x1, waiting for transfers between devices: 2.15 us -> 0.01 us  [local(): lax.all_to_all(squares, ('enc', 'seq'), 0, 0, axis_index_groups=same_core...]
    pallas_call x1, Pallas kernels: 8.46 us -> 7.46 us  [attend(): pl.pallas_call(functools.partial(attend_kernel, width), out_shape=jax.Sha...]
  transfers between devices with their start and end apart: 25 -> 26, of which waited for: 8 -> 7; matrix products, arithmetic and copies ran while one was open for 10% -> 10% of each run, Pallas kernels for 5% -> 5%
where the time goes in v5:
time: 95.3 us; the launch traced here: 94.9 us
  starting transfers between devices  53.8 us (56%)
  Pallas kernels  17.7 us (19%)
  waiting for transfers between devices  12.6 us (13%)
  local copies, waits for them, and re-layouts  9.2 us (10%)
  other arithmetic  1.26 us (1%)
    ppermute x7, starting transfers between devices, local(): ups[n].append(lax.ppermute(ups[n][-1], ('enc', 'seq'), planes(1)))  20.6 us
    ppermute x4, starting transfers between devices, local(): parts = parts + [lax.ppermute(part, 'seq', CORE) for part in parts]  16.6 us
    unnamed x13, local copies, waits for them, and re-layouts  8.48 us
    pallas_call x1, Pallas kernels, attend(): pl.pallas_call(functools.partial(attend_kernel, width), out_shape=jax.Sha...  7.46 us
    ppermute x7, waiting for transfers between devices, local(): downs[n].append(lax.ppermute(downs[n][-1], ('enc', 'seq'), planes(-1)))  5.23 us
    all_to_all x1, starting transfers between devices, local(): lax.all_to_all(squares, ('enc', 'seq'), 0, 0, axis_index_groups=same_core...  5.2 us
    ppermute x3, starting transfers between devices, local(): parts = [text] + [lax.ppermute(text, 'rep', ring(4, k)) for k in (-1, 2, 1)]  5.04 us
    pallas_call x1, Pallas kernels, project(): pl.pallas_call(project_kernel, out_shape=(jax.ShapeDtypeStruct((4, 8, 8,...  4.54 us
  transfers between devices with their start and end apart: 26, of which 7 were waited for; matrix products, arithmetic and copies ran while one was open for 10% of the time, Pallas kernels for 5%

profile of v5, /device:TPU:1, one launch (start us, length us, event | category | flops | bytes accessed | tf_op | source)
XLA Modules:
  0.0 94.9 jit_solution(546701755084635238)
XLA Ops:
  0.0 3.6 %collective-permute-start.1 = (bf16[4,8,5120]{2,1,0:T(8,128)(2,1)}, bf16[4,8,5120]{2,1,0:T(8,128)(2,1)S(1)}, u32[]{:S(2)}, u32[]{:S(2)}) collective-permute-start(bf16[4,8,5120]{2,1,0:T(8,128)(2,1)} %refs_0_.1), channel_id=1, source_target_pairs={{0,16},{8,24},{16,0},{24,8},{1,17},{9,25},{17,1},{25,9},{2,18},{10... | collective-permute-start | bytes 983048 | tf_op jit(solution)/shard_map/ppermute | solution.py:323
  3.6 0.9 collective-permute-start
  4.4 0.6 collective-permute-start.2
  5.0 0.7 fusion
  5.8 0.0 copy-start.5
  5.8 0.0 copy-start.1
  5.8 0.0 copy-start.2
  5.8 7.8 %copy.10 = bf16[640,8,2,384]{3,1,2,0:T(8,128)(2,1)} copy(bf16[640,8,2,384]{3,2,1,0:T(2,128)(2,1)} %bitcast.24) | data formatting | bytes 15728640
  13.6 0.6 gather_fusion
  14.3 0.1 convert_reduce_fusion
  14.4 0.1 concatenate.3.info
  14.5 0.4 multiply_reduce_fusion
  14.9 0.0 collective-permute-done.1.refs_2_
  14.9 3.5 %collective-permute-done.refs_1_ = bf16[4,8,5120]{2,1,0:T(8,128)(2,1)S(1)} collective-permute-done((bf16[4,8,5120]{2,1,0:T(8,128)(2,1)}, bf16[4,8,5120]{2,1,0:T(8,128)(2,1)S(1)}, u32[]{:S(2)}, u32[]{:S(2)}) %collective-permute-start) | collective-permute-done | bytes 327712 | tf_op jit(solution)/shard_map/ppermute | solution.py:323
  18.4 0.0 collective-permute-done.2.refs_3_
  18.4 1.2 %pick.1 = (bf16[4,8,2560]{2,1,0:T(8,128)(2,1)S(1)}, bf16[4,8,2688]{2,1,0:T(8,128)(2,1)S(1)}) custom-call(s32[15]{0:T(128)S(1)} %concatenate.3.info, bf16[4,8,5120]{2,1,0:T(8,128)(2,1)S(1)} %copy-done.2, bf16[4,8,5120]{2,1,0:T(8,128)(2,1)S(1)} %collective-permute-done.refs_1_, bf16[4,8,5120]{2,1,0:T(8,128)(2,1)S(1)} %collective-permute-done.1.refs_2_, ...), custom_call_target="tpu_custom_call" | custom-call | tf_op jit(solution)/shard_map/pick/pallas_call | solution.py:66
  19.6 6.5 %collective-permute-start.10 = (bf16[32,2560]{1,0:T(8,128)(2,1)S(1)}, bf16[32,2560]{1,0:T(8,128)(2,1)S(1)}, u32[]{:S(2)}, u32[]{:S(2)}) collective-permute-start(bf16[32,2560]{1,0:T(8,128)(2,1)S(1)} %bitcast.17), channel_id=1, source_target_pairs={{0,32},{1,225},{2,34},{3,227},{4,36},{5,229},{6,38},{7,231},{32,64... | collective-permute-start | bytes 491528 | tf_op jit(solution)/shard_map/ppermute | solution.py:330
  26.1 0.0 collective-permute-start.6
  26.1 0.0 collective-permute-start.14
  26.1 2.8 %collective-permute-done.10.refs_1_ = bf16[32,2560]{1,0:T(8,128)(2,1)S(1)} collective-permute-done((bf16[32,2560]{1,0:T(8,128)(2,1)S(1)}, bf16[32,2560]{1,0:T(8,128)(2,1)S(1)}, u32[]{:S(2)}, u32[]{:S(2)}) %collective-permute-start.10) | collective-permute-done | bytes 163872 | tf_op jit(solution)/shard_map/ppermute | solution.py:330
  28.9 3.4 %collective-permute-start.11 = (bf16[32,2560]{1,0:T(8,128)(2,1)S(1)}, bf16[32,2560]{1,0:T(8,128)(2,1)S(1)}, u32[]{:S(2)}, u32[]{:S(2)}) collective-permute-start(bf16[32,2560]{1,0:T(8,128)(2,1)S(1)} %collective-permute-done.10.refs_1_), channel_id=1, source_target_pairs={{0,32},{1,225},{2,34},{3,227},{4,36},{5,229},{6,38},{7,231},{32,64... | collective-permute-start | bytes 491528 | tf_op jit(solution)/shard_map/ppermute | solution.py:330
  32.3 0.0 collective-permute-start.3
  32.3 0.0 collective-permute-done.6.refs_5_
  32.3 1.4 %collective-permute-start.7 = (bf16[32,2688]{1,0:T(8,128)(2,1)S(1)}, bf16[32,2688]{1,0:T(8,128)(2,1)S(1)}, u32[]{:S(2)}, u32[]{:S(2)}) collective-permute-start(bf16[32,2688]{1,0:T(8,128)(2,1)S(1)} %collective-permute-done.6.refs_5_), channel_id=1, source_target_pairs={{0,224},{1,33},{2,226},{3,35},{4,228},{5,37},{6,230},{7,39},{32,0}... | collective-permute-start | bytes 516104 | tf_op jit(solution)/shard_map/ppermute | solution.py:332
  33.8 0.0 collective-permute-done.14.refs_5_
  33.8 0.1 collective-permute-start.15
  33.9 0.7 collective-permute-done.11.refs_2_
  34.6 3.1 %collective-permute-start.12 = (bf16[32,2560]{1,0:T(8,128)(2,1)S(1)}, bf16[32,2560]{1,0:T(8,128)(2,1)S(1)}, u32[]{:S(2)}, u32[]{:S(2)}) collective-permute-start(bf16[32,2560]{1,0:T(8,128)(2,1)S(1)} %collective-permute-done.11.refs_2_), channel_id=1, source_target_pairs={{0,32},{1,225},{2,34},{3,227},{4,36},{5,229},{6,38},{7,231},{32,64... | collective-permute-start | bytes 491528 | tf_op jit(solution)/shard_map/ppermute | solution.py:330
  37.7 0.3 collective-permute-done.3.refs_1_
  38.0 3.2 %collective-permute-start.4 = (bf16[32,2688]{1,0:T(8,128)(2,1)S(1)}, bf16[32,2688]{1,0:T(8,128)(2,1)S(1)}, u32[]{:S(2)}, u32[]{:S(2)}) collective-permute-start(bf16[32,2688]{1,0:T(8,128)(2,1)S(1)} %collective-permute-done.3.refs_1_), channel_id=1, source_target_pairs={{0,32},{1,225},{2,34},{3,227},{4,36},{5,229},{6,38},{7,231},{32,64... | collective-permute-start | bytes 516104 | tf_op jit(solution)/shard_map/ppermute | solution.py:330
  41.2 0.0 collective-permute-done.7.refs_6_
  41.2 0.0 collective-permute-start.8
  41.2 1.1 %collective-permute-done.15.refs_6_ = bf16[32,2560]{1,0:T(8,128)(2,1)S(1)} collective-permute-done((bf16[32,2560]{1,0:T(8,128)(2,1)S(1)}, bf16[32,2560]{1,0:T(8,128)(2,1)S(1)}, u32[]{:S(2)}, u32[]{:S(2)}) %collective-permute-start.15) | collective-permute-done | bytes 163872 | tf_op jit(solution)/shard_map/ppermute | solution.py:332
  42.3 0.0 collective-permute-start.16
  42.3 0.0 collective-permute-done.12.refs_3_
  42.3 2.8 %collective-permute-start.13 = (bf16[32,2560]{1,0:T(8,128)(2,1)S(1)}, bf16[32,2560]{1,0:T(8,128)(2,1)S(1)}, u32[]{:S(2)}, u32[]{:S(2)}) collective-permute-start(bf16[32,2560]{1,0:T(8,128)(2,1)S(1)} %collective-permute-done.12.refs_3_), channel_id=1, source_target_pairs={{0,32},{1,225},{2,34},{3,227},{4,36},{5,229},{6,38},{7,231},{32,64... | collective-permute-start | bytes 491528 | tf_op jit(solution)/shard_map/ppermute | solution.py:330
  45.2 1.6 %collective-permute-start.5 = (bf16[32,2688]{1,0:T(8,128)(2,1)S(1)}, bf16[32,2688]{1,0:T(8,128)(2,1)S(1)}, u32[]{:S(2)}, u32[]{:S(2)}) collective-permute-start(bf16[32,2688]{1,0:T(8,128)(2,1)S(1)} %collective-permute-done.4.refs_2_), channel_id=1, source_target_pairs={{0,32},{1,225},{2,34},{3,227},{4,36},{5,229},{6,38},{7,231},{32,64... | collective-permute-start | bytes 516104 | tf_op jit(solution)/shard_map/ppermute | solution.py:330
  46.7 1.3 %collective-permute-done.8.refs_7_ = bf16[32,2688]{1,0:T(8,128)(2,1)S(1)} collective-permute-done((bf16[32,2688]{1,0:T(8,128)(2,1)S(1)}, bf16[32,2688]{1,0:T(8,128)(2,1)S(1)}, u32[]{:S(2)}, u32[]{:S(2)}) %collective-permute-start.8) | collective-permute-done | bytes 172064 | tf_op jit(solution)/shard_map/ppermute | solution.py:332
  48.0 0.0 collective-permute-start.9
  48.0 2.8 %collective-permute-done.16.refs_7_ = bf16[32,2560]{1,0:T(8,128)(2,1)S(1)} collective-permute-done((bf16[32,2560]{1,0:T(8,128)(2,1)S(1)}, bf16[32,2560]{1,0:T(8,128)(2,1)S(1)}, u32[]{:S(2)}, u32[]{:S(2)}) %collective-permute-start.16) | collective-permute-done | bytes 163872 | tf_op jit(solution)/shard_map/ppermute | solution.py:332
  50.8 0.0 collective-permute-done.13.refs_4_
  50.8 3.1 %project_first.1.refs_9_ = f32[256,768]{1,0:T(8,128)S(1)} custom-call(bf16[32,2560]{1,0:T(8,128)(2,1)S(1)} %bitcast.19, bf16[32,2560]{1,0:T(8,128)(2,1)S(1)} %collective-permute-done.10.refs_1_, bf16[32,2560]{1,0:T(8,128)(2,1)S(1)} %collective-permute-done.11.refs_2_, bf16[32,2560]{1,0:T(8,128)(2,1)S(1)} %collective-permute-done.12.refs_3_, ...), custom_call_target="tpu_custom_call" | custom-call | flops 1006632960 | bytes 3932160 | tf_op jit(solution)/shard_map/project_first/pallas_call | solution.py:103
  54.0 0.0 collective-permute-done.5.refs_3_
  54.0 4.5 %project.1 = (bf16[4,8,8,768]{3,2,1,0:T(8,128)(2,1)S(1)}, f32[32,1,256]{2,1,0:T(1,128)}, f32[16,128]{1,0:T(8,128)S(1)}) custom-call(s32[15]{0:T(128)S(1)} %concatenate.3.info, f32[384]{0:T(512)S(1)} %copy-done.4, bf16[32,2688]{1,0:T(8,128)(2,1)S(1)} %bitcast.16, bf16[32,2688]{1,0:T(8,128)(2,1)S(1)} %collective-permute-done.3.refs_1_, ...), custom_call_target="tpu_custom_call" | custom-call | flops 1006632960 | bytes 3932160 | tf_op jit(solution)/shard_map/project/pallas_call | solution.py:156
  58.5 2.8 %collective-permute-start.20 = (bf16[4,64,768]{2,1,0:T(8,128)(2,1)S(1)}, bf16[4,64,768]{2,1,0:T(8,128)(2,1)S(1)}, u32[]{:S(2)}, u32[]{:S(2)}) collective-permute-start(bf16[4,64,768]{2,1,0:T(8,128)(2,1)S(1)} %bitcast.9), channel_id=1, source_target_pairs={{0,6},{1,7},{2,0},{3,1},{4,2},{5,3},{6,4},{7,5},{8,14},{9,15},{10,... | collective-permute-start | bytes 1179656 | tf_op jit(solution)/shard_map/ppermute | solution.py:340
  61.4 1.6 %collective-permute-start.17 = (bf16[4,64,768]{2,1,0:T(8,128)(2,1)S(1)}, bf16[4,64,768]{2,1,0:T(8,128)(2,1)S(1)}, u32[]{:S(2)}, u32[]{:S(2)}) collective-permute-start(bf16[4,64,768]{2,1,0:T(8,128)(2,1)S(1)} %bitcast.11), channel_id=1, source_target_pairs={{0,4},{1,5},{2,6},{3,7},{4,0},{5,1},{6,2},{7,3},{8,12},{9,13},{10,... | collective-permute-start | bytes 1179656 | tf_op jit(solution)/shard_map/ppermute | solution.py:340
  63.0 5.2 %all-to-all-start = ((f32[32,1,256]{2,1,0:T(1,128)}), f32[32,1,256]{2,1,0:T(1,128)}, u32[]{:S(2)}, u32[]{:S(2)}) async-start(f32[32,1,256]{2,1,0:T(1,128)} %get-tuple-element.16), calls=%async_computation | async-start | bytes 65536 | tf_op jit(solution)/shard_map/all_to_all | solution.py:339
  68.2 6.8 %collective-permute-start.21 = (bf16[4,64,768]{2,1,0:T(8,128)(2,1)S(1)}, bf16[4,64,768]{2,1,0:T(8,128)(2,1)S(1)}, u32[]{:S(2)}, u32[]{:S(2)}) collective-permute-start(bf16[4,64,768]{2,1,0:T(8,128)(2,1)S(1)} %bitcast.12), channel_id=1, source_target_pairs={{0,1},{1,0},{2,3},{3,2},{4,5},{5,4},{6,7},{7,6},{8,9},{9,8},{10,11... | collective-permute-start | bytes 1179656 | tf_op jit(solution)/shard_map/ppermute | solution.py:343
  75.0 0.0 collective-permute-done.20.refs_2_
  75.0 4.4 %collective-permute-start.23 = (bf16[4,64,768]{2,1,0:T(8,128)(2,1)S(1)}, bf16[4,64,768]{2,1,0:T(8,128)(2,1)}, u32[]{:S(2)}, u32[]{:S(2)}) collective-permute-start(bf16[4,64,768]{2,1,0:T(8,128)(2,1)S(1)} %collective-permute-done.20.refs_2_), channel_id=1, source_target_pairs={{0,1},{1,0},{2,3},{3,2},{4,5},{5,4},{6,7},{7,6},{8,9},{9,8},{10,11... | collective-permute-start | bytes 1179656 | tf_op jit(solution)/shard_map/ppermute | solution.py:343
  79.4 0.0 collective-permute-done.19.refs_1_
  79.4 3.4 %collective-permute-start.22 = (bf16[4,64,768]{2,1,0:T(8,128)(2,1)S(1)}, bf16[4,64,768]{2,1,0:T(8,128)(2,1)}, u32[]{:S(2)}, u32[]{:S(2)}) collective-permute-start(bf16[4,64,768]{2,1,0:T(8,128)(2,1)S(1)} %collective-permute-done.19.refs_1_), channel_id=1, source_target_pairs={{0,1},{1,0},{2,3},{3,2},{4,5},{5,4},{6,7},{7,6},{8,9},{9,8},{10,11... | collective-permute-start | bytes 1179656 | tf_op jit(solution)/shard_map/ppermute | solution.py:343
  82.8 0.0 all-to-all-done.squares
  82.8 0.0 collective-permute-done.17.piece
  82.8 0.8 key_sums.1
  83.6 2.0 %collective-permute-start.24 = (bf16[4,64,768]{2,1,0:T(8,128)(2,1)S(1)}, bf16[4,64,768]{2,1,0:T(8,128)(2,1)S(1)}, u32[]{:S(2)}, u32[]{:S(2)}) collective-permute-start(bf16[4,64,768]{2,1,0:T(8,128)(2,1)S(1)} %get-tuple-element.18.refs_3_), channel_id=1, source_target_pairs={{0,1},{1,0},{2,3},{3,2},{4,5},{5,4},{6,7},{7,6},{8,9},{9,8},{10,11... | collective-permute-start | bytes 1179656 | tf_op jit(solution)/shard_map/ppermute | solution.py:343
  85.6 0.3 collective-permute-start.18
  85.9 0.7 copy-done.3
  86.6 0.6 scale_queries.1.q_buf
  87.2 0.0 collective-permute-done.21.refs_4_
  87.3 0.0 collective-permute-done.18.core_total
  87.3 0.0 collective-permute-done.22.refs_5_
  87.3 0.0 collective-permute-done.24.refs_7_
  87.3 7.5 %attend.1 = bf16[2048,384]{1,0:T(8,128)(2,1)} custom-call(s32[15]{0:T(128)S(1)} %concatenate.3.info, bf16[2048,384]{1,0:T(8,128)(2,1)S(1)} %scale_queries.1.q_buf, f32[8,256]{1,0:T(8,128)S(1)} %get-tuple-element.17.key_total, f32[8,256]{1,0:T(8,128)S(1)} %collective-permute-done.18.core_total, bf16[4,64,768]{2,1,0:T(8,128)(2,1)S(1)} %bitcast.13, ...), custom_call_target="tpu_custom_call" | custom-call | flops 1610612736 | bytes 3145728 | tf_op jit(solution)/shard_map/attend/pallas_call | solution.py:293
  (13 shorter events, 0.0 us)
Async XLA Ops:
  0.0 13.6 %copy-start = (s32[16]{0:T(128)S(1)}, s32[16]{0:T(128)}, u32[]{:S(2)}) copy-start(s32[16]{0:T(128)} %param.13) | copy-start | bytes 196
  0.0 14.9 %collective-permute-start.1 = (bf16[4,8,5120]{2,1,0:T(8,128)(2,1)}, bf16[4,8,5120]{2,1,0:T(8,128)(2,1)S(1)}, u32[]{:S(2)}, u32[]{:S(2)}) collective-permute-start(bf16[4,8,5120]{2,1,0:T(8,128)(2,1)} %refs_0_.1), channel_id=1, source_target_pairs={{0,16},{8,24},{16,0},{24,8},{1,17},{9,25},{17,1},{25,9},{2,18},{10... | collective-permute-start | bytes 983048 | tf_op jit(solution)/shard_map/ppermute | solution.py:323
  3.6 14.8 %collective-permute-start = (bf16[4,8,5120]{2,1,0:T(8,128)(2,1)}, bf16[4,8,5120]{2,1,0:T(8,128)(2,1)S(1)}, u32[]{:S(2)}, u32[]{:S(2)}) collective-permute-start(bf16[4,8,5120]{2,1,0:T(8,128)(2,1)} %refs_0_.1), channel_id=1, source_target_pairs={{0,24},{8,0},{16,8},{24,16},{1,25},{9,1},{17,9},{25,17},{2,26},{10... | collective-permute-start | bytes 983048 | tf_op jit(solution)/shard_map/ppermute | solution.py:323
  4.4 13.9 %collective-permute-start.2 = (bf16[4,8,5120]{2,1,0:T(8,128)(2,1)}, bf16[4,8,5120]{2,1,0:T(8,128)(2,1)S(1)}, u32[]{:S(2)}, u32[]{:S(2)}) collective-permute-start(bf16[4,8,5120]{2,1,0:T(8,128)(2,1)} %refs_0_.1), channel_id=1, source_target_pairs={{0,8},{8,16},{16,24},{24,0},{1,9},{9,17},{17,25},{25,1},{2,10},{10... | collective-permute-start | bytes 983048 | tf_op jit(solution)/shard_map/ppermute | solution.py:323
  5.8 8.5 %copy-start.5 = (s32[1,16]{1,0:T(1,128)S(1)}, s32[1,16]{1,0:T(1,128)}, u32[]{:S(2)}) copy-start(s32[1,16]{1,0:T(1,128)} %param.15) | copy-start | bytes 196
  5.8 8.6 %copy-start.1 = (bf16[2048,384]{1,0:T(8,128)(2,1)S(1)}, bf16[2048,384]{1,0:T(8,128)(2,1)}, u32[]{:S(2)}) copy-start(bf16[2048,384]{1,0:T(8,128)(2,1)} %queries.1) | copy-start | bytes 4718596
  5.8 12.5 %copy-start.2 = (bf16[4,8,5120]{2,1,0:T(8,128)(2,1)S(1)}, bf16[4,8,5120]{2,1,0:T(8,128)(2,1)}, u32[]{:S(2)}) copy-start(bf16[4,8,5120]{2,1,0:T(8,128)(2,1)} %refs_0_.1) | copy-start | bytes 983044
  19.6 9.3 %collective-permute-start.10 = (bf16[32,2560]{1,0:T(8,128)(2,1)S(1)}, bf16[32,2560]{1,0:T(8,128)(2,1)S(1)}, u32[]{:S(2)}, u32[]{:S(2)}) collective-permute-start(bf16[32,2560]{1,0:T(8,128)(2,1)S(1)} %bitcast.17), channel_id=1, source_target_pairs={{0,32},{1,225},{2,34},{3,227},{4,36},{5,229},{6,38},{7,231},{32,64... | collective-permute-start | bytes 491528 | tf_op jit(solution)/shard_map/ppermute | solution.py:330
  26.1 27.9 %copy-start.4 = (f32[384]{0:T(512)S(1)}, f32[384]{0:T(512)}, u32[]{:S(2)}) copy-start(f32[384]{0:T(512)} %gain.2) | copy-start | bytes 4612
  26.1 6.3 %collective-permute-start.6 = (bf16[32,2688]{1,0:T(8,128)(2,1)S(1)}, bf16[32,2688]{1,0:T(8,128)(2,1)S(1)}, u32[]{:S(2)}, u32[]{:S(2)}) collective-permute-start(bf16[32,2688]{1,0:T(8,128)(2,1)S(1)} %bitcast.14), channel_id=1, source_target_pairs={{0,224},{1,33},{2,226},{3,35},{4,228},{5,37},{6,230},{7,39},{32,0}... | collective-permute-start | bytes 516104 | tf_op jit(solution)/shard_map/ppermute | solution.py:332
  26.1 7.7 %collective-permute-start.14 = (bf16[32,2560]{1,0:T(8,128)(2,1)S(1)}, bf16[32,2560]{1,0:T(8,128)(2,1)S(1)}, u32[]{:S(2)}, u32[]{:S(2)}) collective-permute-start(bf16[32,2560]{1,0:T(8,128)(2,1)S(1)} %bitcast.18), channel_id=1, source_target_pairs={{0,224},{1,33},{2,226},{3,35},{4,228},{5,37},{6,230},{7,39},{32,0}... | collective-permute-start | bytes 491528 | tf_op jit(solution)/shard_map/ppermute | solution.py:332
  28.9 5.7 %collective-permute-start.11 = (bf16[32,2560]{1,0:T(8,128)(2,1)S(1)}, bf16[32,2560]{1,0:T(8,128)(2,1)S(1)}, u32[]{:S(2)}, u32[]{:S(2)}) collective-permute-start(bf16[32,2560]{1,0:T(8,128)(2,1)S(1)} %collective-permute-done.10.refs_1_), channel_id=1, source_target_pairs={{0,32},{1,225},{2,34},{3,227},{4,36},{5,229},{6,38},{7,231},{32,64... | collective-permute-start | bytes 491528 | tf_op jit(solution)/shard_map/ppermute | solution.py:330
  32.3 5.7 %collective-permute-start.3 = (bf16[32,2688]{1,0:T(8,128)(2,1)S(1)}, bf16[32,2688]{1,0:T(8,128)(2,1)S(1)}, u32[]{:S(2)}, u32[]{:S(2)}) collective-permute-start(bf16[32,2688]{1,0:T(8,128)(2,1)S(1)} %bitcast.15), channel_id=1, source_target_pairs={{0,32},{1,225},{2,34},{3,227},{4,36},{5,229},{6,38},{7,231},{32,64... | collective-permute-start | bytes 516104 | tf_op jit(solution)/shard_map/ppermute | solution.py:330
  32.3 8.9 %collective-permute-start.7 = (bf16[32,2688]{1,0:T(8,128)(2,1)S(1)}, bf16[32,2688]{1,0:T(8,128)(2,1)S(1)}, u32[]{:S(2)}, u32[]{:S(2)}) collective-permute-start(bf16[32,2688]{1,0:T(8,128)(2,1)S(1)} %collective-permute-done.6.refs_5_), channel_id=1, source_target_pairs={{0,224},{1,33},{2,226},{3,35},{4,228},{5,37},{6,230},{7,39},{32,0}... | collective-permute-start | bytes 516104 | tf_op jit(solution)/shard_map/ppermute | solution.py:332
  33.8 8.5 %collective-permute-start.15 = (bf16[32,2560]{1,0:T(8,128)(2,1)S(1)}, bf16[32,2560]{1,0:T(8,128)(2,1)S(1)}, u32[]{:S(2)}, u32[]{:S(2)}) collective-permute-start(bf16[32,2560]{1,0:T(8,128)(2,1)S(1)} %collective-permute-done.14.refs_5_), channel_id=1, source_target_pairs={{0,224},{1,33},{2,226},{3,35},{4,228},{5,37},{6,230},{7,39},{32,0}... | collective-permute-start | bytes 491528 | tf_op jit(solution)/shard_map/ppermute | solution.py:332
  34.6 7.8 %collective-permute-start.12 = (bf16[32,2560]{1,0:T(8,128)(2,1)S(1)}, bf16[32,2560]{1,0:T(8,128)(2,1)S(1)}, u32[]{:S(2)}, u32[]{:S(2)}) collective-permute-start(bf16[32,2560]{1,0:T(8,128)(2,1)S(1)} %collective-permute-done.11.refs_2_), channel_id=1, source_target_pairs={{0,32},{1,225},{2,34},{3,227},{4,36},{5,229},{6,38},{7,231},{32,64... | collective-permute-start | bytes 491528 | tf_op jit(solution)/shard_map/ppermute | solution.py:330
  38.0 7.2 %collective-permute-start.4 = (bf16[32,2688]{1,0:T(8,128)(2,1)S(1)}, bf16[32,2688]{1,0:T(8,128)(2,1)S(1)}, u32[]{:S(2)}, u32[]{:S(2)}) collective-permute-start(bf16[32,2688]{1,0:T(8,128)(2,1)S(1)} %collective-permute-done.3.refs_1_), channel_id=1, source_target_pairs={{0,32},{1,225},{2,34},{3,227},{4,36},{5,229},{6,38},{7,231},{32,64... | collective-permute-start | bytes 516104 | tf_op jit(solution)/shard_map/ppermute | solution.py:330
  41.2 6.8 %collective-permute-start.8 = (bf16[32,2688]{1,0:T(8,128)(2,1)S(1)}, bf16[32,2688]{1,0:T(8,128)(2,1)S(1)}, u32[]{:S(2)}, u32[]{:S(2)}) collective-permute-start(bf16[32,2688]{1,0:T(8,128)(2,1)S(1)} %collective-permute-done.7.refs_6_), channel_id=1, source_target_pairs={{0,224},{1,33},{2,226},{3,35},{4,228},{5,37},{6,230},{7,39},{32,0}... | collective-permute-start | bytes 516104 | tf_op jit(solution)/shard_map/ppermute | solution.py:332
  42.3 8.5 %collective-permute-start.16 = (bf16[32,2560]{1,0:T(8,128)(2,1)S(1)}, bf16[32,2560]{1,0:T(8,128)(2,1)S(1)}, u32[]{:S(2)}, u32[]{:S(2)}) collective-permute-start(bf16[32,2560]{1,0:T(8,128)(2,1)S(1)} %collective-permute-done.15.refs_6_), channel_id=1, source_target_pairs={{0,224},{1,33},{2,226},{3,35},{4,228},{5,37},{6,230},{7,39},{32,0}... | collective-permute-start | bytes 491528 | tf_op jit(solution)/shard_map/ppermute | solution.py:332
  42.3 8.5 %collective-permute-start.13 = (bf16[32,2560]{1,0:T(8,128)(2,1)S(1)}, bf16[32,2560]{1,0:T(8,128)(2,1)S(1)}, u32[]{:S(2)}, u32[]{:S(2)}) collective-permute-start(bf16[32,2560]{1,0:T(8,128)(2,1)S(1)} %collective-permute-done.12.refs_3_), channel_id=1, source_target_pairs={{0,32},{1,225},{2,34},{3,227},{4,36},{5,229},{6,38},{7,231},{32,64... | collective-permute-start | bytes 491528 | tf_op jit(solution)/shard_map/ppermute | solution.py:330
  45.2 8.8 %collective-permute-start.5 = (bf16[32,2688]{1,0:T(8,128)(2,1)S(1)}, bf16[32,2688]{1,0:T(8,128)(2,1)S(1)}, u32[]{:S(2)}, u32[]{:S(2)}) collective-permute-start(bf16[32,2688]{1,0:T(8,128)(2,1)S(1)} %collective-permute-done.4.refs_2_), channel_id=1, source_target_pairs={{0,32},{1,225},{2,34},{3,227},{4,36},{5,229},{6,38},{7,231},{32,64... | collective-permute-start | bytes 516104 | tf_op jit(solution)/shard_map/ppermute | solution.py:330
  48.0 5.9 %collective-permute-start.9 = (bf16[32,2688]{1,0:T(8,128)(2,1)S(1)}, bf16[32,2688]{1,0:T(8,128)(2,1)S(1)}, u32[]{:S(2)}, u32[]{:S(2)}) collective-permute-start(bf16[32,2688]{1,0:T(8,128)(2,1)S(1)} %collective-permute-done.8.refs_7_), channel_id=1, source_target_pairs={{0,224},{1,33},{2,226},{3,35},{4,228},{5,37},{6,230},{7,39},{32,0}... | collective-permute-start | bytes 516104 | tf_op jit(solution)/shard_map/ppermute | solution.py:332
  58.5 16.5 %collective-permute-start.20 = (bf16[4,64,768]{2,1,0:T(8,128)(2,1)S(1)}, bf16[4,64,768]{2,1,0:T(8,128)(2,1)S(1)}, u32[]{:S(2)}, u32[]{:S(2)}) collective-permute-start(bf16[4,64,768]{2,1,0:T(8,128)(2,1)S(1)} %bitcast.9), channel_id=1, source_target_pairs={{0,6},{1,7},{2,0},{3,1},{4,2},{5,3},{6,4},{7,5},{8,14},{9,15},{10,... | collective-permute-start | bytes 1179656 | tf_op jit(solution)/shard_map/ppermute | solution.py:340
  61.4 18.0 %collective-permute-start.19 = (bf16[4,64,768]{2,1,0:T(8,128)(2,1)S(1)}, bf16[4,64,768]{2,1,0:T(8,128)(2,1)S(1)}, u32[]{:S(2)}, u32[]{:S(2)}) collective-permute-start(bf16[4,64,768]{2,1,0:T(8,128)(2,1)S(1)} %bitcast.10), channel_id=1, source_target_pairs={{0,2},{1,3},{2,4},{3,5},{4,6},{5,7},{6,0},{7,1},{8,10},{9,11},{10,... | collective-permute-start | bytes 1179656 | tf_op jit(solution)/shard_map/ppermute | solution.py:340
  61.4 21.5 %collective-permute-start.17 = (bf16[4,64,768]{2,1,0:T(8,128)(2,1)S(1)}, bf16[4,64,768]{2,1,0:T(8,128)(2,1)S(1)}, u32[]{:S(2)}, u32[]{:S(2)}) collective-permute-start(bf16[4,64,768]{2,1,0:T(8,128)(2,1)S(1)} %bitcast.11), channel_id=1, source_target_pairs={{0,4},{1,5},{2,6},{3,7},{4,0},{5,1},{6,2},{7,3},{8,12},{9,13},{10,... | collective-permute-start | bytes 1179656 | tf_op jit(solution)/shard_map/ppermute | solution.py:340
  63.0 19.8 %all-to-all-start = ((f32[32,1,256]{2,1,0:T(1,128)}), f32[32,1,256]{2,1,0:T(1,128)}, u32[]{:S(2)}, u32[]{:S(2)}) async-start(f32[32,1,256]{2,1,0:T(1,128)} %get-tuple-element.16), calls=%async_computation | async-start | bytes 65536 | tf_op jit(solution)/shard_map/all_to_all | solution.py:339
  68.2 19.0 %collective-permute-start.21 = (bf16[4,64,768]{2,1,0:T(8,128)(2,1)S(1)}, bf16[4,64,768]{2,1,0:T(8,128)(2,1)S(1)}, u32[]{:S(2)}, u32[]{:S(2)}) collective-permute-start(bf16[4,64,768]{2,1,0:T(8,128)(2,1)S(1)} %bitcast.12), channel_id=1, source_target_pairs={{0,1},{1,0},{2,3},{3,2},{4,5},{5,4},{6,7},{7,6},{8,9},{9,8},{10,11... | collective-permute-start | bytes 1179656 | tf_op jit(solution)/shard_map/ppermute | solution.py:343
  75.0 12.2 %collective-permute-start.23 = (bf16[4,64,768]{2,1,0:T(8,128)(2,1)S(1)}, bf16[4,64,768]{2,1,0:T(8,128)(2,1)}, u32[]{:S(2)}, u32[]{:S(2)}) collective-permute-start(bf16[4,64,768]{2,1,0:T(8,128)(2,1)S(1)} %collective-permute-done.20.refs_2_), channel_id=1, source_target_pairs={{0,1},{1,0},{2,3},{3,2},{4,5},{5,4},{6,7},{7,6},{8,9},{9,8},{10,11... | collective-permute-start | bytes 1179656 | tf_op jit(solution)/shard_map/ppermute | solution.py:343
  79.4 7.9 %collective-permute-start.22 = (bf16[4,64,768]{2,1,0:T(8,128)(2,1)S(1)}, bf16[4,64,768]{2,1,0:T(8,128)(2,1)}, u32[]{:S(2)}, u32[]{:S(2)}) collective-permute-start(bf16[4,64,768]{2,1,0:T(8,128)(2,1)S(1)} %collective-permute-done.19.refs_1_), channel_id=1, source_target_pairs={{0,1},{1,0},{2,3},{3,2},{4,5},{5,4},{6,7},{7,6},{8,9},{9,8},{10,11... | collective-permute-start | bytes 1179656 | tf_op jit(solution)/shard_map/ppermute | solution.py:343
  83.6 3.7 %collective-permute-start.24 = (bf16[4,64,768]{2,1,0:T(8,128)(2,1)S(1)}, bf16[4,64,768]{2,1,0:T(8,128)(2,1)S(1)}, u32[]{:S(2)}, u32[]{:S(2)}) collective-permute-start(bf16[4,64,768]{2,1,0:T(8,128)(2,1)S(1)} %get-tuple-element.18.refs_3_), channel_id=1, source_target_pairs={{0,1},{1,0},{2,3},{3,2},{4,5},{5,4},{6,7},{7,6},{8,9},{9,8},{10,11... | collective-permute-start | bytes 1179656 | tf_op jit(solution)/shard_map/ppermute | solution.py:343
  85.6 1.6 %collective-permute-start.18 = (f32[8,256]{1,0:T(8,128)S(1)}, f32[8,256]{1,0:T(8,128)S(1)}, u32[]{:S(2)}, u32[]{:S(2)}) collective-permute-start(f32[8,256]{1,0:T(8,128)S(1)} %get-tuple-element.17.key_total), channel_id=1, source_target_pairs={{0,1},{1,0},{2,3},{3,2},{4,5},{5,4},{6,7},{7,6},{8,9},{9,8},{10,11... | collective-permute-start | bytes 24584 | tf_op jit(solution)/shard_map/ppermute | solution.py:345
  85.9 0.7 copy-start.3

commit v6 on v5

--- a/solution.py
+++ b/solution.py
@@ -12,7 +12,7 @@
 FRAME = 128
 V_DOWN = 2.0 ** -12
 MIB = 1024 * 1024
-CHUNK = 512
+CHUNK = 1280
 GROUP = 4
 RING = 8
 PLANES = (0, -1, -2, -3, 4, 1, 2, 3)

time: 95.3 us -> 95.5 us (level)
  no operation moved by 1% of the time
where the time goes in v6:
time: 95.5 us; the launch traced here: 94.7 us
  starting transfers between devices  53.6 us (56%)
  Pallas kernels  17.7 us (19%)
  waiting for transfers between devices  12.6 us (13%)
  local copies, waits for them, and re-layouts  9.2 us (10%)
  other arithmetic  1.26 us (1%)
    ppermute x7, starting transfers between devices, local(): ups[n].append(lax.ppermute(ups[n][-1], ('enc', 'seq'), planes(1)))  20.6 us
    ppermute x4, starting transfers between devices, local(): parts = parts + [lax.ppermute(part, 'seq', CORE) for part in parts]  16.7 us
    unnamed x13, local copies, waits for them, and re-layouts  8.48 us
    pallas_call x1, Pallas kernels, attend(): pl.pallas_call(functools.partial(attend_kernel, width), out_shape=jax.Sha...  7.67 us
    ppermute x7, waiting for transfers between devices, local(): downs[n].append(lax.ppermute(downs[n][-1], ('enc', 'seq'), planes(-1)))  5.23 us
    all_to_all x1, starting transfers between devices, local(): lax.all_to_all(squares, ('enc', 'seq'), 0, 0, axis_index_groups=same_core...  5.14 us
    ppermute x3, starting transfers between devices, local(): parts = [text] + [lax.ppermute(text, 'rep', ring(4, k)) for k in (-1, 2, 1)]  5.04 us
    ppermute x3, starting transfers between devices, local(): lax.ppermute(pair, 'seq', p)  4.45 us
  transfers between devices with their start and end apart: 26, of which 7 were waited for; matrix products, arithmetic and copies ran while one was open for 10% of the time, Pallas kernels for 5%

profile of v6, /device:TPU:1, one launch (start us, length us, event | category | flops | bytes accessed | tf_op | source)
XLA Modules:
  0.0 94.7 jit_solution(17205159689545226936)
XLA Ops:
  0.0 3.6 %collective-permute-start.1 = (bf16[4,8,5120]{2,1,0:T(8,128)(2,1)}, bf16[4,8,5120]{2,1,0:T(8,128)(2,1)S(1)}, u32[]{:S(2)}, u32[]{:S(2)}) collective-permute-start(bf16[4,8,5120]{2,1,0:T(8,128)(2,1)} %refs_0_.1), channel_id=1, source_target_pairs={{0,16},{8,24},{16,0},{24,8},{1,17},{9,25},{17,1},{25,9},{2,18},{10... | collective-permute-start | bytes 983048 | tf_op jit(solution)/shard_map/ppermute | solution.py:323
  3.6 0.9 collective-permute-start
  4.4 0.6 collective-permute-start.2
  5.0 0.7 fusion
  5.8 0.0 copy-start.5
  5.8 0.0 copy-start.1
  5.8 0.0 copy-start.2
  5.8 7.8 %copy.10 = bf16[640,8,2,384]{3,1,2,0:T(8,128)(2,1)} copy(bf16[640,8,2,384]{3,2,1,0:T(2,128)(2,1)} %bitcast.24) | data formatting | bytes 15728640
  13.6 0.6 gather_fusion
  14.3 0.1 convert_reduce_fusion
  14.4 0.1 concatenate.3.info
  14.5 0.4 multiply_reduce_fusion
  14.9 0.0 collective-permute-done.1.refs_2_
  14.9 3.5 %collective-permute-done.refs_1_ = bf16[4,8,5120]{2,1,0:T(8,128)(2,1)S(1)} collective-permute-done((bf16[4,8,5120]{2,1,0:T(8,128)(2,1)}, bf16[4,8,5120]{2,1,0:T(8,128)(2,1)S(1)}, u32[]{:S(2)}, u32[]{:S(2)}) %collective-permute-start) | collective-permute-done | bytes 327712 | tf_op jit(solution)/shard_map/ppermute | solution.py:323
  18.4 0.0 collective-permute-done.2.refs_3_
  18.4 1.2 %pick.1 = (bf16[4,8,2560]{2,1,0:T(8,128)(2,1)S(1)}, bf16[4,8,2688]{2,1,0:T(8,128)(2,1)S(1)}) custom-call(s32[15]{0:T(128)S(1)} %concatenate.3.info, bf16[4,8,5120]{2,1,0:T(8,128)(2,1)S(1)} %copy-done.2, bf16[4,8,5120]{2,1,0:T(8,128)(2,1)S(1)} %collective-permute-done.refs_1_, bf16[4,8,5120]{2,1,0:T(8,128)(2,1)S(1)} %collective-permute-done.1.refs_2_, ...), custom_call_target="tpu_custom_call" | custom-call | tf_op jit(solution)/shard_map/pick/pallas_call | solution.py:66
  19.6 6.5 %collective-permute-start.10 = (bf16[32,2560]{1,0:T(8,128)(2,1)S(1)}, bf16[32,2560]{1,0:T(8,128)(2,1)S(1)}, u32[]{:S(2)}, u32[]{:S(2)}) collective-permute-start(bf16[32,2560]{1,0:T(8,128)(2,1)S(1)} %bitcast.17), channel_id=1, source_target_pairs={{0,32},{1,225},{2,34},{3,227},{4,36},{5,229},{6,38},{7,231},{32,64... | collective-permute-start | bytes 491528 | tf_op jit(solution)/shard_map/ppermute | solution.py:330
  26.1 0.0 collective-permute-start.6
  26.1 0.0 collective-permute-start.14
  26.1 2.8 %collective-permute-done.10.refs_1_ = bf16[32,2560]{1,0:T(8,128)(2,1)S(1)} collective-permute-done((bf16[32,2560]{1,0:T(8,128)(2,1)S(1)}, bf16[32,2560]{1,0:T(8,128)(2,1)S(1)}, u32[]{:S(2)}, u32[]{:S(2)}) %collective-permute-start.10) | collective-permute-done | bytes 163872 | tf_op jit(solution)/shard_map/ppermute | solution.py:330
  28.9 3.4 %collective-permute-start.11 = (bf16[32,2560]{1,0:T(8,128)(2,1)S(1)}, bf16[32,2560]{1,0:T(8,128)(2,1)S(1)}, u32[]{:S(2)}, u32[]{:S(2)}) collective-permute-start(bf16[32,2560]{1,0:T(8,128)(2,1)S(1)} %collective-permute-done.10.refs_1_), channel_id=1, source_target_pairs={{0,32},{1,225},{2,34},{3,227},{4,36},{5,229},{6,38},{7,231},{32,64... | collective-permute-start | bytes 491528 | tf_op jit(solution)/shard_map/ppermute | solution.py:330
  32.3 0.0 collective-permute-start.3
  32.3 0.0 collective-permute-done.6.refs_5_
  32.3 1.4 %collective-permute-start.7 = (bf16[32,2688]{1,0:T(8,128)(2,1)S(1)}, bf16[32,2688]{1,0:T(8,128)(2,1)S(1)}, u32[]{:S(2)}, u32[]{:S(2)}) collective-permute-start(bf16[32,2688]{1,0:T(8,128)(2,1)S(1)} %collective-permute-done.6.refs_5_), channel_id=1, source_target_pairs={{0,224},{1,33},{2,226},{3,35},{4,228},{5,37},{6,230},{7,39},{32,0}... | collective-permute-start | bytes 516104 | tf_op jit(solution)/shard_map/ppermute | solution.py:332
  33.8 0.0 collective-permute-done.14.refs_5_
  33.8 0.1 collective-permute-start.15
  33.9 0.7 collective-permute-done.11.refs_2_
  34.6 3.1 %collective-permute-start.12 = (bf16[32,2560]{1,0:T(8,128)(2,1)S(1)}, bf16[32,2560]{1,0:T(8,128)(2,1)S(1)}, u32[]{:S(2)}, u32[]{:S(2)}) collective-permute-start(bf16[32,2560]{1,0:T(8,128)(2,1)S(1)} %collective-permute-done.11.refs_2_), channel_id=1, source_target_pairs={{0,32},{1,225},{2,34},{3,227},{4,36},{5,229},{6,38},{7,231},{32,64... | collective-permute-start | bytes 491528 | tf_op jit(solution)/shard_map/ppermute | solution.py:330
  37.7 0.3 collective-permute-done.3.refs_1_
  38.0 3.2 %collective-permute-start.4 = (bf16[32,2688]{1,0:T(8,128)(2,1)S(1)}, bf16[32,2688]{1,0:T(8,128)(2,1)S(1)}, u32[]{:S(2)}, u32[]{:S(2)}) collective-permute-start(bf16[32,2688]{1,0:T(8,128)(2,1)S(1)} %collective-permute-done.3.refs_1_), channel_id=1, source_target_pairs={{0,32},{1,225},{2,34},{3,227},{4,36},{5,229},{6,38},{7,231},{32,64... | collective-permute-start | bytes 516104 | tf_op jit(solution)/shard_map/ppermute | solution.py:330
  41.2 0.0 collective-permute-done.7.refs_6_
  41.2 0.0 collective-permute-start.8
  41.2 1.1 %collective-permute-done.15.refs_6_ = bf16[32,2560]{1,0:T(8,128)(2,1)S(1)} collective-permute-done((bf16[32,2560]{1,0:T(8,128)(2,1)S(1)}, bf16[32,2560]{1,0:T(8,128)(2,1)S(1)}, u32[]{:S(2)}, u32[]{:S(2)}) %collective-permute-start.15) | collective-permute-done | bytes 163872 | tf_op jit(solution)/shard_map/ppermute | solution.py:332
  42.3 0.0 collective-permute-start.16
  42.3 0.0 collective-permute-done.12.refs_3_
  42.3 2.8 %collective-permute-start.13 = (bf16[32,2560]{1,0:T(8,128)(2,1)S(1)}, bf16[32,2560]{1,0:T(8,128)(2,1)S(1)}, u32[]{:S(2)}, u32[]{:S(2)}) collective-permute-start(bf16[32,2560]{1,0:T(8,128)(2,1)S(1)} %collective-permute-done.12.refs_3_), channel_id=1, source_target_pairs={{0,32},{1,225},{2,34},{3,227},{4,36},{5,229},{6,38},{7,231},{32,64... | collective-permute-start | bytes 491528 | tf_op jit(solution)/shard_map/ppermute | solution.py:330
  45.2 0.0 collective-permute-done.4.refs_2_
  45.2 1.6 %collective-permute-start.5 = (bf16[32,2688]{1,0:T(8,128)(2,1)S(1)}, bf16[32,2688]{1,0:T(8,128)(2,1)S(1)}, u32[]{:S(2)}, u32[]{:S(2)}) collective-permute-start(bf16[32,2688]{1,0:T(8,128)(2,1)S(1)} %collective-permute-done.4.refs_2_), channel_id=1, source_target_pairs={{0,32},{1,225},{2,34},{3,227},{4,36},{5,229},{6,38},{7,231},{32,64... | collective-permute-start | bytes 516104 | tf_op jit(solution)/shard_map/ppermute | solution.py:330
  46.7 1.3 %collective-permute-done.8.refs_7_ = bf16[32,2688]{1,0:T(8,128)(2,1)S(1)} collective-permute-done((bf16[32,2688]{1,0:T(8,128)(2,1)S(1)}, bf16[32,2688]{1,0:T(8,128)(2,1)S(1)}, u32[]{:S(2)}, u32[]{:S(2)}) %collective-permute-start.8) | collective-permute-done | bytes 172064 | tf_op jit(solution)/shard_map/ppermute | solution.py:332
  48.0 0.0 collective-permute-start.9
  48.0 2.8 %collective-permute-done.16.refs_7_ = bf16[32,2560]{1,0:T(8,128)(2,1)S(1)} collective-permute-done((bf16[32,2560]{1,0:T(8,128)(2,1)S(1)}, bf16[32,2560]{1,0:T(8,128)(2,1)S(1)}, u32[]{:S(2)}, u32[]{:S(2)}) %collective-permute-start.16) | collective-permute-done | bytes 163872 | tf_op jit(solution)/shard_map/ppermute | solution.py:332
  50.8 0.0 collective-permute-done.13.refs_4_
  50.8 3.2 %project_first.1.refs_9_ = f32[256,768]{1,0:T(8,128)S(1)} custom-call(bf16[32,2560]{1,0:T(8,128)(2,1)S(1)} %bitcast.19, bf16[32,2560]{1,0:T(8,128)(2,1)S(1)} %collective-permute-done.10.refs_1_, bf16[32,2560]{1,0:T(8,128)(2,1)S(1)} %collective-permute-done.11.refs_2_, bf16[32,2560]{1,0:T(8,128)(2,1)S(1)} %collective-permute-done.12.refs_3_, ...), custom_call_target="tpu_custom_call" | custom-call | flops 1006632960 | bytes 3932160 | tf_op jit(solution)/shard_map/project_first/pallas_call | solution.py:103
  54.0 0.0 collective-permute-done.5.refs_3_
  54.0 0.0 collective-permute-done.9.refs_4_
  54.1 4.3 %project.1 = (bf16[4,8,8,768]{3,2,1,0:T(8,128)(2,1)S(1)}, f32[32,1,256]{2,1,0:T(1,128)}, f32[16,128]{1,0:T(8,128)S(1)}) custom-call(s32[15]{0:T(128)S(1)} %concatenate.3.info, f32[384]{0:T(512)S(1)} %copy-done.4, bf16[32,2688]{1,0:T(8,128)(2,1)S(1)} %bitcast.16, bf16[32,2688]{1,0:T(8,128)(2,1)S(1)} %collective-permute-done.3.refs_1_, ...), custom_call_target="tpu_custom_call" | custom-call | flops 1006632960 | bytes 3932160 | tf_op jit(solution)/shard_map/project/pallas_call | solution.py:156
  58.3 2.8 %collective-permute-start.20 = (bf16[4,64,768]{2,1,0:T(8,128)(2,1)S(1)}, bf16[4,64,768]{2,1,0:T(8,128)(2,1)S(1)}, u32[]{:S(2)}, u32[]{:S(2)}) collective-permute-start(bf16[4,64,768]{2,1,0:T(8,128)(2,1)S(1)} %bitcast.9), channel_id=1, source_target_pairs={{0,6},{1,7},{2,0},{3,1},{4,2},{5,3},{6,4},{7,5},{8,14},{9,15},{10,... | collective-permute-start | bytes 1179656 | tf_op jit(solution)/shard_map/ppermute | solution.py:340
  61.1 1.6 %collective-permute-start.17 = (bf16[4,64,768]{2,1,0:T(8,128)(2,1)S(1)}, bf16[4,64,768]{2,1,0:T(8,128)(2,1)S(1)}, u32[]{:S(2)}, u32[]{:S(2)}) collective-permute-start(bf16[4,64,768]{2,1,0:T(8,128)(2,1)S(1)} %bitcast.11), channel_id=1, source_target_pairs={{0,4},{1,5},{2,6},{3,7},{4,0},{5,1},{6,2},{7,3},{8,12},{9,13},{10,... | collective-permute-start | bytes 1179656 | tf_op jit(solution)/shard_map/ppermute | solution.py:340
  62.8 5.1 %all-to-all-start = ((f32[32,1,256]{2,1,0:T(1,128)}), f32[32,1,256]{2,1,0:T(1,128)}, u32[]{:S(2)}, u32[]{:S(2)}) async-start(f32[32,1,256]{2,1,0:T(1,128)} %get-tuple-element.16), calls=%async_computation | async-start | bytes 65536 | tf_op jit(solution)/shard_map/all_to_all | solution.py:339
  67.9 6.9 %collective-permute-start.21 = (bf16[4,64,768]{2,1,0:T(8,128)(2,1)S(1)}, bf16[4,64,768]{2,1,0:T(8,128)(2,1)S(1)}, u32[]{:S(2)}, u32[]{:S(2)}) collective-permute-start(bf16[4,64,768]{2,1,0:T(8,128)(2,1)S(1)} %bitcast.12), channel_id=1, source_target_pairs={{0,1},{1,0},{2,3},{3,2},{4,5},{5,4},{6,7},{7,6},{8,9},{9,8},{10,11... | collective-permute-start | bytes 1179656 | tf_op jit(solution)/shard_map/ppermute | solution.py:343
  74.8 0.0 collective-permute-done.20.refs_2_
  74.8 4.4 %collective-permute-start.23 = (bf16[4,64,768]{2,1,0:T(8,128)(2,1)S(1)}, bf16[4,64,768]{2,1,0:T(8,128)(2,1)}, u32[]{:S(2)}, u32[]{:S(2)}) collective-permute-start(bf16[4,64,768]{2,1,0:T(8,128)(2,1)S(1)} %collective-permute-done.20.refs_2_), channel_id=1, source_target_pairs={{0,1},{1,0},{2,3},{3,2},{4,5},{5,4},{6,7},{7,6},{8,9},{9,8},{10,11... | collective-permute-start | bytes 1179656 | tf_op jit(solution)/shard_map/ppermute | solution.py:343
  79.2 0.0 collective-permute-done.19.refs_1_
  79.2 3.4 %collective-permute-start.22 = (bf16[4,64,768]{2,1,0:T(8,128)(2,1)S(1)}, bf16[4,64,768]{2,1,0:T(8,128)(2,1)}, u32[]{:S(2)}, u32[]{:S(2)}) collective-permute-start(bf16[4,64,768]{2,1,0:T(8,128)(2,1)S(1)} %collective-permute-done.19.refs_1_), channel_id=1, source_target_pairs={{0,1},{1,0},{2,3},{3,2},{4,5},{5,4},{6,7},{7,6},{8,9},{9,8},{10,11... | collective-permute-start | bytes 1179656 | tf_op jit(solution)/shard_map/ppermute | solution.py:343
  82.6 0.8 key_sums.1
  83.4 2.0 %collective-permute-start.24 = (bf16[4,64,768]{2,1,0:T(8,128)(2,1)S(1)}, bf16[4,64,768]{2,1,0:T(8,128)(2,1)S(1)}, u32[]{:S(2)}, u32[]{:S(2)}) collective-permute-start(bf16[4,64,768]{2,1,0:T(8,128)(2,1)S(1)} %get-tuple-element.18.refs_3_), channel_id=1, source_target_pairs={{0,1},{1,0},{2,3},{3,2},{4,5},{5,4},{6,7},{7,6},{8,9},{9,8},{10,11... | collective-permute-start | bytes 1179656 | tf_op jit(solution)/shard_map/ppermute | solution.py:343
  85.4 0.1 collective-permute-start.18
  85.5 0.7 copy-done.3
  86.2 0.6 scale_queries.1.q_buf
  86.8 0.0 collective-permute-done.21.refs_4_
  86.8 0.0 collective-permute-done.18.core_total
  86.8 0.0 collective-permute-done.22.refs_5_
  86.8 0.0 collective-permute-done.24.refs_7_
  86.9 7.7 %attend.1 = bf16[2048,384]{1,0:T(8,128)(2,1)} custom-call(s32[15]{0:T(128)S(1)} %concatenate.3.info, bf16[2048,384]{1,0:T(8,128)(2,1)S(1)} %scale_queries.1.q_buf, f32[8,256]{1,0:T(8,128)S(1)} %get-tuple-element.17.key_total, f32[8,256]{1,0:T(8,128)S(1)} %collective-permute-done.18.core_total, bf16[4,64,768]{2,1,0:T(8,128)(2,1)S(1)} %bitcast.13, ...), custom_call_target="tpu_custom_call" | custom-call | flops 1610612736 | bytes 3145728 | tf_op jit(solution)/shard_map/attend/pallas_call | solution.py:293
  (13 shorter events, 0.0 us)
Async XLA Ops:
  0.0 13.6 %copy-start = (s32[16]{0:T(128)S(1)}, s32[16]{0:T(128)}, u32[]{:S(2)}) copy-start(s32[16]{0:T(128)} %param.13) | copy-start | bytes 196
  0.0 14.9 %collective-permute-start.1 = (bf16[4,8,5120]{2,1,0:T(8,128)(2,1)}, bf16[4,8,5120]{2,1,0:T(8,128)(2,1)S(1)}, u32[]{:S(2)}, u32[]{:S(2)}) collective-permute-start(bf16[4,8,5120]{2,1,0:T(8,128)(2,1)} %refs_0_.1), channel_id=1, source_target_pairs={{0,16},{8,24},{16,0},{24,8},{1,17},{9,25},{17,1},{25,9},{2,18},{10... | collective-permute-start | bytes 983048 | tf_op jit(solution)/shard_map/ppermute | solution.py:323
  3.6 14.8 %collective-permute-start = (bf16[4,8,5120]{2,1,0:T(8,128)(2,1)}, bf16[4,8,5120]{2,1,0:T(8,128)(2,1)S(1)}, u32[]{:S(2)}, u32[]{:S(2)}) collective-permute-start(bf16[4,8,5120]{2,1,0:T(8,128)(2,1)} %refs_0_.1), channel_id=1, source_target_pairs={{0,24},{8,0},{16,8},{24,16},{1,25},{9,1},{17,9},{25,17},{2,26},{10... | collective-permute-start | bytes 983048 | tf_op jit(solution)/shard_map/ppermute | solution.py:323
  4.4 13.9 %collective-permute-start.2 = (bf16[4,8,5120]{2,1,0:T(8,128)(2,1)}, bf16[4,8,5120]{2,1,0:T(8,128)(2,1)S(1)}, u32[]{:S(2)}, u32[]{:S(2)}) collective-permute-start(bf16[4,8,5120]{2,1,0:T(8,128)(2,1)} %refs_0_.1), channel_id=1, source_target_pairs={{0,8},{8,16},{16,24},{24,0},{1,9},{9,17},{17,25},{25,1},{2,10},{10... | collective-permute-start | bytes 983048 | tf_op jit(solution)/shard_map/ppermute | solution.py:323
  5.8 8.5 %copy-start.5 = (s32[1,16]{1,0:T(1,128)S(1)}, s32[1,16]{1,0:T(1,128)}, u32[]{:S(2)}) copy-start(s32[1,16]{1,0:T(1,128)} %param.15) | copy-start | bytes 196
  5.8 8.6 %copy-start.1 = (bf16[2048,384]{1,0:T(8,128)(2,1)S(1)}, bf16[2048,384]{1,0:T(8,128)(2,1)}, u32[]{:S(2)}) copy-start(bf16[2048,384]{1,0:T(8,128)(2,1)} %queries.1) | copy-start | bytes 4718596
  5.8 12.5 %copy-start.2 = (bf16[4,8,5120]{2,1,0:T(8,128)(2,1)S(1)}, bf16[4,8,5120]{2,1,0:T(8,128)(2,1)}, u32[]{:S(2)}) copy-start(bf16[4,8,5120]{2,1,0:T(8,128)(2,1)} %refs_0_.1) | copy-start | bytes 983044
  19.6 9.3 %collective-permute-start.10 = (bf16[32,2560]{1,0:T(8,128)(2,1)S(1)}, bf16[32,2560]{1,0:T(8,128)(2,1)S(1)}, u32[]{:S(2)}, u32[]{:S(2)}) collective-permute-start(bf16[32,2560]{1,0:T(8,128)(2,1)S(1)} %bitcast.17), channel_id=1, source_target_pairs={{0,32},{1,225},{2,34},{3,227},{4,36},{5,229},{6,38},{7,231},{32,64... | collective-permute-start | bytes 491528 | tf_op jit(solution)/shard_map/ppermute | solution.py:330
  26.1 28.0 %copy-start.4 = (f32[384]{0:T(512)S(1)}, f32[384]{0:T(512)}, u32[]{:S(2)}) copy-start(f32[384]{0:T(512)} %gain.2) | copy-start | bytes 4612
  26.1 6.3 %collective-permute-start.6 = (bf16[32,2688]{1,0:T(8,128)(2,1)S(1)}, bf16[32,2688]{1,0:T(8,128)(2,1)S(1)}, u32[]{:S(2)}, u32[]{:S(2)}) collective-permute-start(bf16[32,2688]{1,0:T(8,128)(2,1)S(1)} %bitcast.14), channel_id=1, source_target_pairs={{0,224},{1,33},{2,226},{3,35},{4,228},{5,37},{6,230},{7,39},{32,0}... | collective-permute-start | bytes 516104 | tf_op jit(solution)/shard_map/ppermute | solution.py:332
  26.1 7.7 %collective-permute-start.14 = (bf16[32,2560]{1,0:T(8,128)(2,1)S(1)}, bf16[32,2560]{1,0:T(8,128)(2,1)S(1)}, u32[]{:S(2)}, u32[]{:S(2)}) collective-permute-start(bf16[32,2560]{1,0:T(8,128)(2,1)S(1)} %bitcast.18), channel_id=1, source_target_pairs={{0,224},{1,33},{2,226},{3,35},{4,228},{5,37},{6,230},{7,39},{32,0}... | collective-permute-start | bytes 491528 | tf_op jit(solution)/shard_map/ppermute | solution.py:332
  28.9 5.7 %collective-permute-start.11 = (bf16[32,2560]{1,0:T(8,128)(2,1)S(1)}, bf16[32,2560]{1,0:T(8,128)(2,1)S(1)}, u32[]{:S(2)}, u32[]{:S(2)}) collective-permute-start(bf16[32,2560]{1,0:T(8,128)(2,1)S(1)} %collective-permute-done.10.refs_1_), channel_id=1, source_target_pairs={{0,32},{1,225},{2,34},{3,227},{4,36},{5,229},{6,38},{7,231},{32,64... | collective-permute-start | bytes 491528 | tf_op jit(solution)/shard_map/ppermute | solution.py:330
  32.3 5.7 %collective-permute-start.3 = (bf16[32,2688]{1,0:T(8,128)(2,1)S(1)}, bf16[32,2688]{1,0:T(8,128)(2,1)S(1)}, u32[]{:S(2)}, u32[]{:S(2)}) collective-permute-start(bf16[32,2688]{1,0:T(8,128)(2,1)S(1)} %bitcast.15), channel_id=1, source_target_pairs={{0,32},{1,225},{2,34},{3,227},{4,36},{5,229},{6,38},{7,231},{32,64... | collective-permute-start | bytes 516104 | tf_op jit(solution)/shard_map/ppermute | solution.py:330
  32.3 8.9 %collective-permute-start.7 = (bf16[32,2688]{1,0:T(8,128)(2,1)S(1)}, bf16[32,2688]{1,0:T(8,128)(2,1)S(1)}, u32[]{:S(2)}, u32[]{:S(2)}) collective-permute-start(bf16[32,2688]{1,0:T(8,128)(2,1)S(1)} %collective-permute-done.6.refs_5_), channel_id=1, source_target_pairs={{0,224},{1,33},{2,226},{3,35},{4,228},{5,37},{6,230},{7,39},{32,0}... | collective-permute-start | bytes 516104 | tf_op jit(solution)/shard_map/ppermute | solution.py:332
  33.8 8.5 %collective-permute-start.15 = (bf16[32,2560]{1,0:T(8,128)(2,1)S(1)}, bf16[32,2560]{1,0:T(8,128)(2,1)S(1)}, u32[]{:S(2)}, u32[]{:S(2)}) collective-permute-start(bf16[32,2560]{1,0:T(8,128)(2,1)S(1)} %collective-permute-done.14.refs_5_), channel_id=1, source_target_pairs={{0,224},{1,33},{2,226},{3,35},{4,228},{5,37},{6,230},{7,39},{32,0}... | collective-permute-start | bytes 491528 | tf_op jit(solution)/shard_map/ppermute | solution.py:332
  34.6 7.8 %collective-permute-start.12 = (bf16[32,2560]{1,0:T(8,128)(2,1)S(1)}, bf16[32,2560]{1,0:T(8,128)(2,1)S(1)}, u32[]{:S(2)}, u32[]{:S(2)}) collective-permute-start(bf16[32,2560]{1,0:T(8,128)(2,1)S(1)} %collective-permute-done.11.refs_2_), channel_id=1, source_target_pairs={{0,32},{1,225},{2,34},{3,227},{4,36},{5,229},{6,38},{7,231},{32,64... | collective-permute-start | bytes 491528 | tf_op jit(solution)/shard_map/ppermute | solution.py:330
  38.0 7.2 %collective-permute-start.4 = (bf16[32,2688]{1,0:T(8,128)(2,1)S(1)}, bf16[32,2688]{1,0:T(8,128)(2,1)S(1)}, u32[]{:S(2)}, u32[]{:S(2)}) collective-permute-start(bf16[32,2688]{1,0:T(8,128)(2,1)S(1)} %collective-permute-done.3.refs_1_), channel_id=1, source_target_pairs={{0,32},{1,225},{2,34},{3,227},{4,36},{5,229},{6,38},{7,231},{32,64... | collective-permute-start | bytes 516104 | tf_op jit(solution)/shard_map/ppermute | solution.py:330
  41.2 6.8 %collective-permute-start.8 = (bf16[32,2688]{1,0:T(8,128)(2,1)S(1)}, bf16[32,2688]{1,0:T(8,128)(2,1)S(1)}, u32[]{:S(2)}, u32[]{:S(2)}) collective-permute-start(bf16[32,2688]{1,0:T(8,128)(2,1)S(1)} %collective-permute-done.7.refs_6_), channel_id=1, source_target_pairs={{0,224},{1,33},{2,226},{3,35},{4,228},{5,37},{6,230},{7,39},{32,0}... | collective-permute-start | bytes 516104 | tf_op jit(solution)/shard_map/ppermute | solution.py:332
  42.3 8.5 %collective-permute-start.16 = (bf16[32,2560]{1,0:T(8,128)(2,1)S(1)}, bf16[32,2560]{1,0:T(8,128)(2,1)S(1)}, u32[]{:S(2)}, u32[]{:S(2)}) collective-permute-start(bf16[32,2560]{1,0:T(8,128)(2,1)S(1)} %collective-permute-done.15.refs_6_), channel_id=1, source_target_pairs={{0,224},{1,33},{2,226},{3,35},{4,228},{5,37},{6,230},{7,39},{32,0}... | collective-permute-start | bytes 491528 | tf_op jit(solution)/shard_map/ppermute | solution.py:332
  42.3 8.5 %collective-permute-start.13 = (bf16[32,2560]{1,0:T(8,128)(2,1)S(1)}, bf16[32,2560]{1,0:T(8,128)(2,1)S(1)}, u32[]{:S(2)}, u32[]{:S(2)}) collective-permute-start(bf16[32,2560]{1,0:T(8,128)(2,1)S(1)} %collective-permute-done.12.refs_3_), channel_id=1, source_target_pairs={{0,32},{1,225},{2,34},{3,227},{4,36},{5,229},{6,38},{7,231},{32,64... | collective-permute-start | bytes 491528 | tf_op jit(solution)/shard_map/ppermute | solution.py:330
  45.2 8.8 %collective-permute-start.5 = (bf16[32,2688]{1,0:T(8,128)(2,1)S(1)}, bf16[32,2688]{1,0:T(8,128)(2,1)S(1)}, u32[]{:S(2)}, u32[]{:S(2)}) collective-permute-start(bf16[32,2688]{1,0:T(8,128)(2,1)S(1)} %collective-permute-done.4.refs_2_), channel_id=1, source_target_pairs={{0,32},{1,225},{2,34},{3,227},{4,36},{5,229},{6,38},{7,231},{32,64... | collective-permute-start | bytes 516104 | tf_op jit(solution)/shard_map/ppermute | solution.py:330
  48.0 6.0 %collective-permute-start.9 = (bf16[32,2688]{1,0:T(8,128)(2,1)S(1)}, bf16[32,2688]{1,0:T(8,128)(2,1)S(1)}, u32[]{:S(2)}, u32[]{:S(2)}) collective-permute-start(bf16[32,2688]{1,0:T(8,128)(2,1)S(1)} %collective-permute-done.8.refs_7_), channel_id=1, source_target_pairs={{0,224},{1,33},{2,226},{3,35},{4,228},{5,37},{6,230},{7,39},{32,0}... | collective-permute-start | bytes 516104 | tf_op jit(solution)/shard_map/ppermute | solution.py:332
  58.3 16.5 %collective-permute-start.20 = (bf16[4,64,768]{2,1,0:T(8,128)(2,1)S(1)}, bf16[4,64,768]{2,1,0:T(8,128)(2,1)S(1)}, u32[]{:S(2)}, u32[]{:S(2)}) collective-permute-start(bf16[4,64,768]{2,1,0:T(8,128)(2,1)S(1)} %bitcast.9), channel_id=1, source_target_pairs={{0,6},{1,7},{2,0},{3,1},{4,2},{5,3},{6,4},{7,5},{8,14},{9,15},{10,... | collective-permute-start | bytes 1179656 | tf_op jit(solution)/shard_map/ppermute | solution.py:340
  61.1 18.0 %collective-permute-start.19 = (bf16[4,64,768]{2,1,0:T(8,128)(2,1)S(1)}, bf16[4,64,768]{2,1,0:T(8,128)(2,1)S(1)}, u32[]{:S(2)}, u32[]{:S(2)}) collective-permute-start(bf16[4,64,768]{2,1,0:T(8,128)(2,1)S(1)} %bitcast.10), channel_id=1, source_target_pairs={{0,2},{1,3},{2,4},{3,5},{4,6},{5,7},{6,0},{7,1},{8,10},{9,11},{10,... | collective-permute-start | bytes 1179656 | tf_op jit(solution)/shard_map/ppermute | solution.py:340
  61.1 21.5 %collective-permute-start.17 = (bf16[4,64,768]{2,1,0:T(8,128)(2,1)S(1)}, bf16[4,64,768]{2,1,0:T(8,128)(2,1)S(1)}, u32[]{:S(2)}, u32[]{:S(2)}) collective-permute-start(bf16[4,64,768]{2,1,0:T(8,128)(2,1)S(1)} %bitcast.11), channel_id=1, source_target_pairs={{0,4},{1,5},{2,6},{3,7},{4,0},{5,1},{6,2},{7,3},{8,12},{9,13},{10,... | collective-permute-start | bytes 1179656 | tf_op jit(solution)/shard_map/ppermute | solution.py:340
  62.8 19.8 %all-to-all-start = ((f32[32,1,256]{2,1,0:T(1,128)}), f32[32,1,256]{2,1,0:T(1,128)}, u32[]{:S(2)}, u32[]{:S(2)}) async-start(f32[32,1,256]{2,1,0:T(1,128)} %get-tuple-element.16), calls=%async_computation | async-start | bytes 65536 | tf_op jit(solution)/shard_map/all_to_all | solution.py:339
  67.9 18.9 %collective-permute-start.21 = (bf16[4,64,768]{2,1,0:T(8,128)(2,1)S(1)}, bf16[4,64,768]{2,1,0:T(8,128)(2,1)S(1)}, u32[]{:S(2)}, u32[]{:S(2)}) collective-permute-start(bf16[4,64,768]{2,1,0:T(8,128)(2,1)S(1)} %bitcast.12), channel_id=1, source_target_pairs={{0,1},{1,0},{2,3},{3,2},{4,5},{5,4},{6,7},{7,6},{8,9},{9,8},{10,11... | collective-permute-start | bytes 1179656 | tf_op jit(solution)/shard_map/ppermute | solution.py:343
  74.8 12.0 %collective-permute-start.23 = (bf16[4,64,768]{2,1,0:T(8,128)(2,1)S(1)}, bf16[4,64,768]{2,1,0:T(8,128)(2,1)}, u32[]{:S(2)}, u32[]{:S(2)}) collective-permute-start(bf16[4,64,768]{2,1,0:T(8,128)(2,1)S(1)} %collective-permute-done.20.refs_2_), channel_id=1, source_target_pairs={{0,1},{1,0},{2,3},{3,2},{4,5},{5,4},{6,7},{7,6},{8,9},{9,8},{10,11... | collective-permute-start | bytes 1179656 | tf_op jit(solution)/shard_map/ppermute | solution.py:343
  79.2 7.7 %collective-permute-start.22 = (bf16[4,64,768]{2,1,0:T(8,128)(2,1)S(1)}, bf16[4,64,768]{2,1,0:T(8,128)(2,1)}, u32[]{:S(2)}, u32[]{:S(2)}) collective-permute-start(bf16[4,64,768]{2,1,0:T(8,128)(2,1)S(1)} %collective-permute-done.19.refs_1_), channel_id=1, source_target_pairs={{0,1},{1,0},{2,3},{3,2},{4,5},{5,4},{6,7},{7,6},{8,9},{9,8},{10,11... | collective-permute-start | bytes 1179656 | tf_op jit(solution)/shard_map/ppermute | solution.py:343
  83.4 3.5 %collective-permute-start.24 = (bf16[4,64,768]{2,1,0:T(8,128)(2,1)S(1)}, bf16[4,64,768]{2,1,0:T(8,128)(2,1)S(1)}, u32[]{:S(2)}, u32[]{:S(2)}) collective-permute-start(bf16[4,64,768]{2,1,0:T(8,128)(2,1)S(1)} %get-tuple-element.18.refs_3_), channel_id=1, source_target_pairs={{0,1},{1,0},{2,3},{3,2},{4,5},{5,4},{6,7},{7,6},{8,9},{9,8},{10,11... | collective-permute-start | bytes 1179656 | tf_op jit(solution)/shard_map/ppermute | solution.py:343
  85.4 1.4 %collective-permute-start.18 = (f32[8,256]{1,0:T(8,128)S(1)}, f32[8,256]{1,0:T(8,128)S(1)}, u32[]{:S(2)}, u32[]{:S(2)}) collective-permute-start(f32[8,256]{1,0:T(8,128)S(1)} %get-tuple-element.17.key_total), channel_id=1, source_target_pairs={{0,1},{1,0},{2,3},{3,2},{4,5},{5,4},{6,7},{7,6},{8,9},{9,8},{10,11... | collective-permute-start | bytes 24584 | tf_op jit(solution)/shard_map/ppermute | solution.py:345
  85.5 0.7 copy-start.3
